TPU v7x, 256 devices: a whole 4x4x8 slice. The times are simulated.
256 devices in a mesh: tm: 2 (over z_lo), row: 16 (over y, z_hi), col: 8 (over x, core).
Axes of the slice: x: 4, y: 4, z: 8 (z_hi: 4, z_lo: 2; z = z_hi * 2 + z_lo), core: 2. Of those that a mesh axis runs over, the one named last changes fastest.
Arguments:
- sweeps: bfloat16 [32, 16, 512, 1024], P(None, 'tm', 'row', 'col'), may hold values from -6 to 6
- temporal_kernel: bfloat16 [64, 32, 3, 3, 3], replicated, may hold values from -0.21875 to 0.21875
- temporal_bias: float32 [64], replicated, may hold values from -3 to 3
- frame_weights: float32 [16], replicated, may hold values from 0.02 to 0.3
- conv1_kernel: bfloat16 [128, 64, 3, 3], replicated, may hold values from -0.25 to 0.25
- conv1_bias: float32 [128], replicated, may hold values from -3 to 3
- conv2_kernel: bfloat16 [128, 128, 3, 3], replicated, may hold values from -0.1875 to 0.1875
- conv2_bias: float32 [128], replicated, may hold values from -3 to 3
Outputs:
- merged: bfloat16 [128, 512, 1024], P(None, ('row', 'tm'), 'col')
All inputs are finite; a program needn't handle non-finite values.
Results may differ from a plain program's by a relative error of at most 0.015.
Values may be sent and summed in bfloat16 or wider, within the bound.
No kernel may reach another device: no remote copies, remote signals or barrier semaphores. Data moves between devices by JAX's collectives and lax.ppermute only.
A program may use at most 128 MiB of HBM per device.

v0:
```python
import jax
import jax.numpy as jnp
from jax import lax
from jax.sharding import PartitionSpec as P


def padded(block, sides, width):
    for axis, dim in sides:
        count = lax.axis_size(axis)
        forward = [(i, i + 1) for i in range(count - 1)]
        backward = [(target, source) for source, target in forward]
        low = lax.ppermute(
            lax.slice_in_dim(block, block.shape[dim] - width, None, axis=dim), axis, forward
        )
        high = lax.ppermute(lax.slice_in_dim(block, 0, width, axis=dim), axis, backward)
        block = jnp.concatenate([low, block, high], axis=dim)
    return block


def swapped(block, axis, bit):
    count = lax.axis_size(axis)
    route = []
    for low in range(count):
        high = low | 1 << bit
        if high != low and high < count:
            route += [(low, high), (high, low)]
    return lax.ppermute(block, axis, route)


def fine_halo(field, width):
    lead = field.shape[:-2]
    rows = field.shape[-2]
    cols = field.shape[-1]
    flat = field.reshape((-1, rows, cols))
    wide = padded(flat, (("col", 2),), width)
    rims = jnp.stack([wide[:, :width, :], wide[:, rows - width :, :]])
    partner = swapped(rims, "tm", 0)
    joined = jnp.concatenate([partner[0], partner[1]], axis=1)
    across = padded(joined, (("row", 1),), width)
    first = lax.axis_index("tm") == 0
    upper = jnp.where(first, across[:, :width, :], partner[1])
    lower = jnp.where(first, partner[0], across[:, across.shape[1] - width :, :])
    whole = jnp.concatenate([upper, wide, lower], axis=1)
    return whole.reshape(lead + (rows + 2 * width, cols + 2 * width))


def temporal_conv(field, kernel, bias, frame_pad):
    out = lax.conv_general_dilated(
        field[None],
        kernel,
        (1, 1, 1),
        ((frame_pad, frame_pad), (0, 0), (0, 0)),
        dimension_numbers=("NCDHW", "OIDHW", "NCDHW"),
        preferred_element_type=jnp.float32,
    )[0]
    return jax.nn.relu(out + bias[:, None, None, None])


def spatial_conv(field, kernel, bias):
    out = lax.conv_general_dilated(
        field[None],
        kernel,
        (1, 1),
        "VALID",
        dimension_numbers=("NCHW", "OIHW", "NCHW"),
        preferred_element_type=jnp.float32,
    )[0]
    return jax.nn.relu(out + bias[:, None, None])


def shards(
    sweeps,
    temporal_kernel,
    temporal_bias,
    frame_weights,
    conv1_kernel,
    conv1_bias,
    conv2_kernel,
    conv2_bias,
):
    frames = sweeps.shape[1]
    margin = padded(sweeps, (("tm", 1), ("row", 2), ("col", 3)), 1)
    temporal = temporal_conv(margin, temporal_kernel, temporal_bias, 0)
    own_weights = lax.dynamic_slice_in_dim(frame_weights, lax.axis_index("tm") * frames, frames)
    partial_sum = jnp.sum(temporal * own_weights[None, :, None, None], axis=1)
    collapsed = lax.psum_scatter(
        partial_sum.astype(jnp.bfloat16), "tm", scatter_dimension=1, tiled=True
    )
    hidden = spatial_conv(fine_halo(collapsed, 1), conv1_kernel, conv1_bias).astype(jnp.bfloat16)
    merged = spatial_conv(fine_halo(hidden, 1), conv2_kernel, conv2_bias)
    return merged.astype(jnp.bfloat16)


def solution(mesh):
    placed = (P(None, "tm", "row", "col"), P(), P(), P(), P(), P(), P(), P())
    return jax.shard_map(
        shards, mesh=mesh, in_specs=placed, out_specs=P(None, ("row", "tm"), "col"), check_vma=False
    )
```

profile of v0, /device:TPU:30, one launch (start us, length us, event | category | flops | bytes accessed | tf_op | source)
XLA Modules:
  0.0 256.6 jit_solution(17486206173332223516)
XLA Ops:
  7.7 3.8 %collective-permute-start = (bf16[32,1,32,128]{3,2,1,0:T(8,128)(2,1)S(1)}, bf16[32,1,32,128]{3,2,1,0:T(8,128)(2,1)S(1)}, u32[]{:S(2)}, u32[]{:S(2)}) collective-permute-start(bf16[32,1,32,128]{3,2,1,0:T(8,128)(2,1)S(1)} %get-tuple-element.10), channel_id=1, source_target_pairs={{0,128},{1,129},{2,130},{3,131},{4,132},{5,133},{6,134},{7,135},{8... | collective-permute-start | bytes 786440 | tf_op jit(solution)/shard_map/ppermute | solution.py:12
  12.8 4.2 %collective-permute-done = bf16[32,1,32,128]{3,2,1,0:T(8,128)(2,1)S(1)} collective-permute-done((bf16[32,1,32,128]{3,2,1,0:T(8,128)(2,1)S(1)}, bf16[32,1,32,128]{3,2,1,0:T(8,128)(2,1)S(1)}, u32[]{:S(2)}, u32[]{:S(2)}) %collective-permute-start) | collective-permute-done | bytes 262176 | tf_op jit(solution)/shard_map/ppermute | solution.py:12
  21.5 5.2 %collective-permute-start.2 = (bf16[32,10,1,128]{3,0,2,1:T(8,128)(2,1)S(1)}, bf16[32,10,1,128]{3,0,2,1:T(8,128)(2,1)S(1)}, u32[]{:S(2)}, u32[]{:S(2)}) collective-permute-start(bf16[32,10,1,128]{3,0,2,1:T(8,128)(2,1)S(1)} %copy.239), channel_id=1, source_target_pairs={{0,8},{8,16},{16,24},{24,32},{32,40},{40,48},{48,56},{56,64},{64,7... | collective-permute-start | bytes 245768 | tf_op jit(solution)/shard_map/ppermute | solution.py:12
  26.7 4.2 %collective-permute-start.3 = (bf16[32,10,1,128]{3,0,2,1:T(8,128)(2,1)S(1)}, bf16[32,10,1,128]{3,0,2,1:T(8,128)(2,1)S(1)}, u32[]{:S(2)}, u32[]{:S(2)}) collective-permute-start(bf16[32,10,1,128]{3,0,2,1:T(8,128)(2,1)S(1)} %copy.240), channel_id=1, source_target_pairs={{8,0},{16,8},{24,16},{32,24},{40,32},{48,40},{56,48},{64,56},{72,6... | collective-permute-start | bytes 245768 | tf_op jit(solution)/shard_map/ppermute | solution.py:15
  30.9 14.3 %copy.209 = bf16[32,10,32,128]{2,0,3,1:T(8,128)(2,1)} copy(bf16[32,10,32,128]{3,2,1,0:T(8,128)(2,1)S(1)} %constant_dynamic-update-slice_fusion) | data formatting | bytes 5242880 | tf_op jit(solution)/shard_map/concatenate | solution.py:16
  45.3 7.8 %copy.208 = bf16[32,10,1,128]{2,0,3,1:T(8,128)(2,1)} copy(bf16[32,10,1,128]{3,0,2,1:T(8,128)(2,1)S(1)} %collective-permute-done.2) | data formatting | bytes 163840 | tf_op jit(solution)/shard_map/ppermute | solution.py:12
  53.1 7.8 %copy.210 = bf16[32,10,1,128]{2,0,3,1:T(8,128)(2,1)} copy(bf16[32,10,1,128]{3,0,2,1:T(8,128)(2,1)S(1)} %collective-permute-done.3) | data formatting | bytes 163840 | tf_op jit(solution)/shard_map/ppermute | solution.py:15
  64.1 3.6 %collective-permute-start.5 = (bf16[32,10,34,1]{2,0,3,1:T(8,128)(2,1)S(1)}, bf16[32,10,34,1]{2,0,3,1:T(8,128)(2,1)S(1)}, u32[]{:S(2)}, u32[]{:S(2)}) collective-permute-start(bf16[32,10,34,1]{2,0,3,1:T(8,128)(2,1)S(1)} %get-tuple-element.6), channel_id=1, source_target_pairs={{1,0},{2,1},{3,2},{4,3},{5,4},{6,5},{7,6},{9,8},{10,9},{11,10},{12... | collective-permute-start | bytes 65288 | tf_op jit(solution)/shard_map/ppermute | solution.py:15
  69.8 14.4 %maximum_bitcast_fusion = bf16[32,10,34,1,130]{2,0,4,1,3:T(8,128)(2,1)S(1)} fusion(bf16[32,10,34,1]{2,0,3,1:T(8,128)(2,1)S(1)} %collective-permute-done.5, bf16[32,10,1,128]{2,0,3,1:T(8,128)(2,1)} %copy.210, bf16[32,10,32,128]{2,0,3,1:T(8,128)(2,1)} %copy.209, bf16[32,10,1,128]{2,0,3,1:T(8,128)(2,1)} %copy.208, ...), kind=kLoop, calls=%fused_computation.13 | loop fusion | flops 14144000 | bytes 5657600 | tf_op jit(solution)/shard_map/broadcast_in_dim | solution.py:49
  84.2 5.4 %pad = bf16[32,10,34,1,136]{2,0,4,1,3:T(8,128)(2,1)} pad(bf16[32,10,34,1,130]{2,0,4,1,3:T(8,128)(2,1)S(1)} %maximum_bitcast_fusion, bf16[]{:T(256)} %constant.19), padding=0_0x0_0x0_0x0_0x0_6 | pad | bytes 5788162 | tf_op jit(solution)/shard_map/broadcast_in_dim | solution.py:49
  89.6 18.5 %copy.212 = bf16[32,10,34,1,8,17]{0,4,5,2,1,3:T(8,128)(2,1)} copy(bf16[32,10,34,1,8,17]{2,0,5,4,1,3:T(8,128)(2,1)} %bitcast.73) | data formatting | bytes 5918720 | tf_op jit(solution)/shard_map/conv_general_dilated | solution.py:48
  109.9 33.1 %fusion.12 = f32[8,32,8,17,64]{4,2,3,1,0:T(8,128)} fusion(bf16[64,32,3,3,3]{0,1,4,3,2:T(8,128)(2,1)S(1)} %copy-done.4, bf16[32,10,34,1,7,2]{0,4,5,2,1,3:T(8,128)(2,1)S(1)} %slice.84, bf16[32,10,34,1,8,17]{0,4,5,2,1,3:T(8,128)(2,1)} %copy.212, pred[8,17]{0,1:T(8,128)(4,1)S(1)} %copy-done.7), kind=kOutput, calls=%fused_computation.14 | convolution fusion | flops 3862521856 | bytes 12287624 | tf_op jit(solution)/shard_map/conv_general_dilated | solution.py:48
  143.0 14.8 %copy.213 = f32[8,32,8,17,64]{4,1,3,2,0:T(8,128)} copy(f32[8,32,8,17,64]{4,2,3,1,0:T(8,128)} %fusion.12) | data formatting | bytes 17825792 | tf_op jit(solution)/shard_map/conv_general_dilated | solution.py:48
  157.8 9.9 %fusion.4 = bf16[64,32,128]{0,1,2:T(8,128)(2,1)} fusion(f32[8,32,1,136,64]{4,1,3,0,2:T(8,128)} %bitcast.72, f32[8]{0:T(128)S(1)} %dynamic_slice.3, f32[64]{0:T(128)S(1)} %copy-done.1), kind=kLoop, calls=%fused_computation.6 | loop fusion | flops 8126464 | bytes 8913184 | tf_op jit(solution)/shard_map/reduce_sum | solution.py:85
  167.7 26.9 %reduce-scatter.2.cloned.1.call-done = bf16[64,16,128]{0,1,2:T(8,128)(2,1)} async-done(((bf16[64,32,128]{0,1,2:T(8,128)(2,1)}), bf16[64,16,128]{0,1,2:T(8,128)(2,1)}) %reduce-scatter.2.cloned.1.call-update) | async-done | bytes 262160 | tf_op jit(solution)/shard_map/reduce_scatter | solution.py:86
  197.2 3.6 %collective-permute-start.7 = (bf16[64,16,1]{0,1,2:T(8,128)(2,1)S(1)}, bf16[64,16,1]{0,1,2:T(8,128)(2,1)S(1)}, u32[]{:S(2)}, u32[]{:S(2)}) collective-permute-start(bf16[64,16,1]{0,1,2:T(8,128)(2,1)S(1)} %get-tuple-element.17), channel_id=1, source_target_pairs={{1,0},{2,1},{3,2},{4,3},{5,4},{6,5},{7,6},{9,8},{10,9},{11,10},{12... | collective-permute-start | bytes 6152 | tf_op jit(solution)/shard_map/ppermute | solution.py:15
  203.1 3.8 %collective-permute-done.8 = bf16[2,64,1,130]{3,1,2,0:T(8,128)(2,1)S(1)} collective-permute-done((bf16[2,64,1,130]{3,1,2,0:T(8,128)(2,1)S(1)}, bf16[2,64,1,130]{3,1,2,0:T(8,128)(2,1)S(1)}, u32[]{:S(2)}, u32[]{:S(2)}) %collective-permute-start.8) | collective-permute-done | bytes 33312 | tf_op jit(solution)/shard_map/ppermute | solution.py:27
  207.0 4.4 %collective-permute-start.9 = (bf16[64,1,130]{0,1,2:T(2,128)(2,1)S(1)}, bf16[64,1,130]{0,1,2:T(2,128)(2,1)S(1)}, u32[]{:S(2)}, u32[]{:S(2)}) collective-permute-start(bf16[64,1,130]{0,1,2:T(2,128)(2,1)S(1)} %copy.216), channel_id=1, source_target_pairs={{0,8},{8,16},{16,24},{24,32},{32,40},{40,48},{48,56},{56,64},{64,7... | collective-permute-start | bytes 49928 | tf_op jit(solution)/shard_map/ppermute | solution.py:12
  211.6 4.4 %collective-permute-start.10 = (bf16[64,1,130]{0,1,2:T(2,128)(2,1)S(1)}, bf16[64,1,130]{0,1,2:T(2,128)(2,1)S(1)}, u32[]{:S(2)}, u32[]{:S(2)}) collective-permute-start(bf16[64,1,130]{0,1,2:T(2,128)(2,1)S(1)} %copy.219), channel_id=1, source_target_pairs={{8,0},{16,8},{24,16},{32,24},{40,32},{48,40},{56,48},{64,56},{72,6... | collective-permute-start | bytes 49928 | tf_op jit(solution)/shard_map/ppermute | solution.py:15
  222.9 3.6 %collective-permute-start.12 = (bf16[128,16,1]{0,1,2:T(8,128)(2,1)S(1)}, bf16[128,16,1]{0,1,2:T(8,128)(2,1)S(1)}, u32[]{:S(2)}, u32[]{:S(2)}) collective-permute-start(bf16[128,16,1]{0,1,2:T(8,128)(2,1)S(1)} %get-tuple-element.16), channel_id=1, source_target_pairs={{1,0},{2,1},{3,2},{4,3},{5,4},{6,5},{7,6},{9,8},{10,9},{11,10},{12... | collective-permute-start | bytes 12296 | tf_op jit(solution)/shard_map/ppermute | solution.py:15
  229.3 3.1 %collective-permute-done.13 = bf16[2,128,1,130]{1,3,2,0:T(8,128)(2,1)S(1)} collective-permute-done((bf16[2,128,1,130]{1,3,2,0:T(8,128)(2,1)S(1)}, bf16[2,128,1,130]{1,3,2,0:T(8,128)(2,1)S(1)}, u32[]{:S(2)}, u32[]{:S(2)}) %collective-permute-start.13) | collective-permute-done | bytes 66592 | tf_op jit(solution)/shard_map/ppermute | solution.py:27
  232.5 5.9 %collective-permute-start.14 = (bf16[128,1,130]{0,1,2:T(2,128)(2,1)S(1)}, bf16[128,1,130]{0,1,2:T(2,128)(2,1)S(1)}, u32[]{:S(2)}, u32[]{:S(2)}) collective-permute-start(bf16[128,1,130]{0,1,2:T(2,128)(2,1)S(1)} %copy.224), channel_id=1, source_target_pairs={{0,8},{8,16},{16,24},{24,32},{32,40},{40,48},{48,56},{56,64},{64,7... | collective-permute-start | bytes 99848 | tf_op jit(solution)/shard_map/ppermute | solution.py:12
  238.5 3.4 %collective-permute-start.15 = (bf16[128,1,130]{0,1,2:T(2,128)(2,1)S(1)}, bf16[128,1,130]{0,1,2:T(2,128)(2,1)S(1)}, u32[]{:S(2)}, u32[]{:S(2)}) collective-permute-start(bf16[128,1,130]{0,1,2:T(2,128)(2,1)S(1)} %copy.227), channel_id=1, source_target_pairs={{8,0},{16,8},{24,16},{32,24},{40,32},{48,40},{56,48},{64,56},{72,6... | collective-permute-start | bytes 99848 | tf_op jit(solution)/shard_map/ppermute | solution.py:15
  242.1 3.5 %collective-permute-done.15 = bf16[128,1,130]{0,1,2:T(2,128)(2,1)S(1)} collective-permute-done((bf16[128,1,130]{0,1,2:T(2,128)(2,1)S(1)}, bf16[128,1,130]{0,1,2:T(2,128)(2,1)S(1)}, u32[]{:S(2)}, u32[]{:S(2)}) %collective-permute-start.15) | collective-permute-done | bytes 33312 | tf_op jit(solution)/shard_map/ppermute | solution.py:15
  (83 shorter events, 32.8 us)
Async XLA Ops:
  6.5 239.9 %copy-start = (bf16[128,128,3,3]{1,0,3,2:T(8,128)(2,1)S(1)}, bf16[128,128,3,3]{1,0,3,2:T(8,128)(2,1)}, u32[]{:S(2)}) copy-start(bf16[128,128,3,3]{1,0,3,2:T(8,128)(2,1)} %param.14) | copy-start | bytes 884740
  6.5 188.1 %reduce-scatter.2.cloned.1.call-start = ((), (), s32[]{:S(2)}) async-start(), calls=%async_computation.1 | async-start | bytes 1572864 | tf_op jit(solution)/shard_map/reduce_scatter | solution.py:86
  7.7 9.4 %collective-permute-start = (bf16[32,1,32,128]{3,2,1,0:T(8,128)(2,1)S(1)}, bf16[32,1,32,128]{3,2,1,0:T(8,128)(2,1)S(1)}, u32[]{:S(2)}, u32[]{:S(2)}) collective-permute-start(bf16[32,1,32,128]{3,2,1,0:T(8,128)(2,1)S(1)} %get-tuple-element.10), channel_id=1, source_target_pairs={{0,128},{1,129},{2,130},{3,131},{4,132},{5,133},{6,134},{7,135},{8... | collective-permute-start | bytes 786440 | tf_op jit(solution)/shard_map/ppermute | solution.py:12
  11.5 9.7 %collective-permute-start.1 = (bf16[32,1,32,128]{3,2,1,0:T(8,128)(2,1)S(1)}, bf16[32,1,32,128]{3,2,1,0:T(8,128)(2,1)S(1)}, u32[]{:S(2)}, u32[]{:S(2)}) collective-permute-start(bf16[32,1,32,128]{3,2,1,0:T(8,128)(2,1)S(1)} %get-tuple-element.9), channel_id=1, source_target_pairs={{128,0},{129,1},{130,2},{131,3},{132,4},{133,5},{134,6},{135,7},{1... | collective-permute-start | bytes 786440 | tf_op jit(solution)/shard_map/ppermute | solution.py:15
  21.5 23.8 %collective-permute-start.2 = (bf16[32,10,1,128]{3,0,2,1:T(8,128)(2,1)S(1)}, bf16[32,10,1,128]{3,0,2,1:T(8,128)(2,1)S(1)}, u32[]{:S(2)}, u32[]{:S(2)}) collective-permute-start(bf16[32,10,1,128]{3,0,2,1:T(8,128)(2,1)S(1)} %copy.239), channel_id=1, source_target_pairs={{0,8},{8,16},{16,24},{24,32},{32,40},{40,48},{48,56},{56,64},{64,7... | collective-permute-start | bytes 245768 | tf_op jit(solution)/shard_map/ppermute | solution.py:12
  26.7 26.4 %collective-permute-start.3 = (bf16[32,10,1,128]{3,0,2,1:T(8,128)(2,1)S(1)}, bf16[32,10,1,128]{3,0,2,1:T(8,128)(2,1)S(1)}, u32[]{:S(2)}, u32[]{:S(2)}) collective-permute-start(bf16[32,10,1,128]{3,0,2,1:T(8,128)(2,1)S(1)} %copy.240), channel_id=1, source_target_pairs={{8,0},{16,8},{24,16},{32,24},{40,32},{48,40},{56,48},{64,56},{72,6... | collective-permute-start | bytes 245768 | tf_op jit(solution)/shard_map/ppermute | solution.py:15
  62.2 5.8 %collective-permute-start.4 = (bf16[32,10,34,1]{2,0,3,1:T(8,128)(2,1)S(1)}, bf16[32,10,34,1]{2,0,3,1:T(8,128)(2,1)S(1)}, u32[]{:S(2)}, u32[]{:S(2)}) collective-permute-start(bf16[32,10,34,1]{2,0,3,1:T(8,128)(2,1)S(1)} %get-tuple-element.5), channel_id=1, source_target_pairs={{0,1},{1,2},{2,3},{3,4},{4,5},{5,6},{6,7},{8,9},{9,10},{10,11},{11... | collective-permute-start | bytes 65288 | tf_op jit(solution)/shard_map/ppermute | solution.py:12
  64.1 5.7 %collective-permute-start.5 = (bf16[32,10,34,1]{2,0,3,1:T(8,128)(2,1)S(1)}, bf16[32,10,34,1]{2,0,3,1:T(8,128)(2,1)S(1)}, u32[]{:S(2)}, u32[]{:S(2)}) collective-permute-start(bf16[32,10,34,1]{2,0,3,1:T(8,128)(2,1)S(1)} %get-tuple-element.6), channel_id=1, source_target_pairs={{1,0},{2,1},{3,2},{4,3},{5,4},{6,5},{7,6},{9,8},{10,9},{11,10},{12... | collective-permute-start | bytes 65288 | tf_op jit(solution)/shard_map/ppermute | solution.py:15
  89.6 20.2 %copy-start.4 = (bf16[64,32,3,3,3]{0,1,4,3,2:T(8,128)(2,1)S(1)}, bf16[64,32,3,3,3]{0,1,4,3,2:T(8,128)(2,1)}, u32[]{:S(2)}) copy-start(bf16[64,32,3,3,3]{0,1,4,3,2:T(8,128)(2,1)} %param.9) | copy-start | bytes 331780
  89.6 20.3 %copy-start.7 = (pred[8,17]{0,1:T(8,128)(4,1)S(1)}, pred[8,17]{0,1:T(8,128)(4,1)}, u32[]{:S(2)}) copy-start(pred[8,17]{0,1:T(8,128)(4,1)} %constant.31) | copy-start | bytes 412
  143.0 14.8 %copy-start.1 = (f32[64]{0:T(128)S(1)}, f32[64]{0:T(128)}, u32[]{:S(2)}) copy-start(f32[64]{0:T(128)} %param.10) | copy-start | bytes 772
  167.7 51.9 %copy-start.5 = (bf16[128,64,3,3]{0,1,3,2:T(8,128)(2,1)S(1)}, bf16[128,64,3,3]{0,1,3,2:T(8,128)(2,1)}, u32[]{:S(2)}) copy-start(bf16[128,64,3,3]{0,1,3,2:T(8,128)(2,1)} %param.12) | copy-start | bytes 442372
  195.3 5.6 %collective-permute-start.6 = (bf16[64,16,1]{0,1,2:T(8,128)(2,1)S(1)}, bf16[64,16,1]{0,1,2:T(8,128)(2,1)S(1)}, u32[]{:S(2)}, u32[]{:S(2)}) collective-permute-start(bf16[64,16,1]{0,1,2:T(8,128)(2,1)S(1)} %get-tuple-element.18), channel_id=1, source_target_pairs={{0,1},{1,2},{2,3},{3,4},{4,5},{5,6},{6,7},{8,9},{9,10},{10,11},{11... | collective-permute-start | bytes 6152 | tf_op jit(solution)/shard_map/ppermute | solution.py:12
  197.2 5.0 %collective-permute-start.7 = (bf16[64,16,1]{0,1,2:T(8,128)(2,1)S(1)}, bf16[64,16,1]{0,1,2:T(8,128)(2,1)S(1)}, u32[]{:S(2)}, u32[]{:S(2)}) collective-permute-start(bf16[64,16,1]{0,1,2:T(8,128)(2,1)S(1)} %get-tuple-element.17), channel_id=1, source_target_pairs={{1,0},{2,1},{3,2},{4,3},{5,4},{6,5},{7,6},{9,8},{10,9},{11,10},{12... | collective-permute-start | bytes 6152 | tf_op jit(solution)/shard_map/ppermute | solution.py:15
  202.0 18.8 %copy-start.2 = (f32[128]{0:T(128)S(1)}, f32[128]{0:T(128)}, u32[]{:S(2)}) copy-start(f32[128]{0:T(128)} %param.13) | copy-start | bytes 1540
  202.6 4.4 %collective-permute-start.8 = (bf16[2,64,1,130]{3,1,2,0:T(8,128)(2,1)S(1)}, bf16[2,64,1,130]{3,1,2,0:T(8,128)(2,1)S(1)}, u32[]{:S(2)}, u32[]{:S(2)}) collective-permute-start(bf16[2,64,1,130]{3,1,2,0:T(8,128)(2,1)S(1)} %pad_maximum_fusion.7), channel_id=1, source_target_pairs={{0,128},{128,0},{1,129},{129,1},{2,130},{130,2},{3,131},{131,3},{4... | collective-permute-start | bytes 99848 | tf_op jit(solution)/shard_map/ppermute | solution.py:27
  207.0 9.2 %collective-permute-start.9 = (bf16[64,1,130]{0,1,2:T(2,128)(2,1)S(1)}, bf16[64,1,130]{0,1,2:T(2,128)(2,1)S(1)}, u32[]{:S(2)}, u32[]{:S(2)}) collective-permute-start(bf16[64,1,130]{0,1,2:T(2,128)(2,1)S(1)} %copy.216), channel_id=1, source_target_pairs={{0,8},{8,16},{16,24},{24,32},{32,40},{40,48},{48,56},{56,64},{64,7... | collective-permute-start | bytes 49928 | tf_op jit(solution)/shard_map/ppermute | solution.py:12
  211.6 7.1 %collective-permute-start.10 = (bf16[64,1,130]{0,1,2:T(2,128)(2,1)S(1)}, bf16[64,1,130]{0,1,2:T(2,128)(2,1)S(1)}, u32[]{:S(2)}, u32[]{:S(2)}) collective-permute-start(bf16[64,1,130]{0,1,2:T(2,128)(2,1)S(1)} %copy.219), channel_id=1, source_target_pairs={{8,0},{16,8},{24,16},{32,24},{40,32},{48,40},{56,48},{64,56},{72,6... | collective-permute-start | bytes 49928 | tf_op jit(solution)/shard_map/ppermute | solution.py:15
  221.0 5.6 %collective-permute-start.11 = (bf16[128,16,1]{0,1,2:T(8,128)(2,1)S(1)}, bf16[128,16,1]{0,1,2:T(8,128)(2,1)S(1)}, u32[]{:S(2)}, u32[]{:S(2)}) collective-permute-start(bf16[128,16,1]{0,1,2:T(8,128)(2,1)S(1)} %get-tuple-element.15), channel_id=1, source_target_pairs={{0,1},{1,2},{2,3},{3,4},{4,5},{5,6},{6,7},{8,9},{9,10},{10,11},{11... | collective-permute-start | bytes 12296 | tf_op jit(solution)/shard_map/ppermute | solution.py:12
  222.9 25.2 %copy-start.3 = (f32[128]{0:T(128)S(1)}, f32[128]{0:T(128)}, u32[]{:S(2)}) copy-start(f32[128]{0:T(128)} %param.15) | copy-start | bytes 1540
  222.9 5.0 %collective-permute-start.12 = (bf16[128,16,1]{0,1,2:T(8,128)(2,1)S(1)}, bf16[128,16,1]{0,1,2:T(8,128)(2,1)S(1)}, u32[]{:S(2)}, u32[]{:S(2)}) collective-permute-start(bf16[128,16,1]{0,1,2:T(8,128)(2,1)S(1)} %get-tuple-element.16), channel_id=1, source_target_pairs={{1,0},{2,1},{3,2},{4,3},{5,4},{6,5},{7,6},{9,8},{10,9},{11,10},{12... | collective-permute-start | bytes 12296 | tf_op jit(solution)/shard_map/ppermute | solution.py:15
  228.0 4.4 %collective-permute-start.13 = (bf16[2,128,1,130]{1,3,2,0:T(8,128)(2,1)S(1)}, bf16[2,128,1,130]{1,3,2,0:T(8,128)(2,1)S(1)}, u32[]{:S(2)}, u32[]{:S(2)}) collective-permute-start(bf16[2,128,1,130]{1,3,2,0:T(8,128)(2,1)S(1)} %pad_maximum_fusion.3), channel_id=1, source_target_pairs={{0,128},{128,0},{1,129},{129,1},{2,130},{130,2},{3,131},{131,3},{4... | collective-permute-start | bytes 199688 | tf_op jit(solution)/shard_map/ppermute | solution.py:27
  232.5 9.5 %collective-permute-start.14 = (bf16[128,1,130]{0,1,2:T(2,128)(2,1)S(1)}, bf16[128,1,130]{0,1,2:T(2,128)(2,1)S(1)}, u32[]{:S(2)}, u32[]{:S(2)}) collective-permute-start(bf16[128,1,130]{0,1,2:T(2,128)(2,1)S(1)} %copy.224), channel_id=1, source_target_pairs={{0,8},{8,16},{16,24},{24,32},{32,40},{40,48},{48,56},{56,64},{64,7... | collective-permute-start | bytes 99848 | tf_op jit(solution)/shard_map/ppermute | solution.py:12
  238.5 7.1 %collective-permute-start.15 = (bf16[128,1,130]{0,1,2:T(2,128)(2,1)S(1)}, bf16[128,1,130]{0,1,2:T(2,128)(2,1)S(1)}, u32[]{:S(2)}, u32[]{:S(2)}) collective-permute-start(bf16[128,1,130]{0,1,2:T(2,128)(2,1)S(1)} %copy.227), channel_id=1, source_target_pairs={{8,0},{16,8},{24,16},{32,24},{40,32},{48,40},{56,48},{64,56},{72,6... | collective-permute-start | bytes 99848 | tf_op jit(solution)/shard_map/ppermute | solution.py:15
  (1 other events, 6.9 us)
Sparse Core Ops, SparseCore 0:
  167.8 26.7 reduce-scatter.1
where the time goes:
time: 262 us; the launch traced here: 257 us
  local copies, waits for them, and re-layouts  79.3 us (30%)
  starting transfers between devices  51.3 us (20%)
  waiting for transfers between devices  49.4 us (19%)
  matrix products  35.5 us (14%)
  other arithmetic  27.2 us (10%)
  between operations  13.9 us (5%)
    conv_general_dilated x3, local copies, waits for them, and re-layouts, temporal_conv(): lax.conv_general_dilated(field[None], kernel, (1, 1, 1), ((frame_pad, fra...  35.1 us
    conv_general_dilated x1, matrix products, temporal_conv(): lax.conv_general_dilated(field[None], kernel, (1, 1, 1), ((frame_pad, fra...  33.1 us
    reduce_scatter x1, waiting for transfers between devices, shards(): lax.psum_scatter(partial_sum.astype(jnp.bfloat16), 'tm', scatter_dimensio...  26.9 us
    ppermute x7, starting transfers between devices, padded(): lax.ppermute(lax.slice_in_dim(block, block.shape[dim] - width, None, axis...  25.1 us
    ppermute x7, starting transfers between devices, padded(): lax.ppermute(lax.slice_in_dim(block, 0, width, axis=dim), axis, backward)  24.3 us
    concatenate x3, local copies, waits for them, and re-layouts, padded(): block = jnp.concatenate([low, block, high], axis=dim)  14.4 us
    broadcast_in_dim x1, other arithmetic, temporal_conv(): field[None]  14.4 us
    ppermute x7, waiting for transfers between devices, padded(): lax.ppermute(lax.slice_in_dim(block, 0, width, axis=dim), axis, backward)  11 us
  transfers between devices with their start and end apart: 17, of which 13 were waited for; matrix products, arithmetic and copies ran while one was open for 10% of the time, Pallas kernels for 0%

commit v1 on v0

v1 whole, which is shorter than its diff:
```python
import functools

import jax
import jax.numpy as jnp
from jax import lax
from jax.experimental import pallas as pl
from jax.experimental.pallas import tpu as pltpu
from jax.sharding import PartitionSpec as P

BF = jnp.bfloat16
F32 = jnp.float32
ANY = pl.BlockSpec(memory_space=pl.ANY)
VMEM = pl.BlockSpec(memory_space=pltpu.VMEM)
SMEM = pl.BlockSpec(memory_space=pltpu.SMEM)


def params():
    return pltpu.CompilerParams(vmem_limit_bytes=40 * 1024 * 1024)


def cost(flops, nbytes):
    return pl.CostEstimate(flops=int(flops), bytes_accessed=int(nbytes), transcendentals=0)


def struct(shape, dtype=BF):
    return jax.ShapeDtypeStruct(shape, dtype)


def dot(a, b):
    return jnp.dot(a, b, preferred_element_type=F32)


def lanes_of(shape):
    return lax.broadcasted_iota(jnp.int32, shape, len(shape) - 1)


def swap16():
    row = lax.broadcasted_iota(jnp.int32, (256, 256), 0)
    col = lax.broadcasted_iota(jnp.int32, (256, 256), 1)
    return jnp.where(col == (row % 16) * 16 + row // 16, 1.0, 0.0).astype(BF)


def pack_kernel(x, xt, up, dn, slab, sup, sdn, perm):
    frame = pl.program_id(0)

    @pl.when(frame == 0)
    def _():
        perm[...] = swap16()

    for cb in range(2):
        chans = slice(cb * 16, cb * 16 + 16)
        halves = [x[chans, 0, rb * 16 : rb * 16 + 16, :].reshape(256, 128) for rb in range(2)]
        y = dot(perm[...], jnp.concatenate(halves, axis=1)).astype(BF)
        for rb in range(2):
            xt[rb * 16 : rb * 16 + 16, chans, :] = y[:, rb * 128 : rb * 128 + 128].reshape(16, 16, 128)
    up[...] = xt[0:3]
    dn[...] = xt[29:32]

    @pl.when(frame == 7 - 7 * lax.axis_index("tm"))
    def _():
        slab[...] = xt[...]
        sup[...] = xt[0:3]
        sdn[...] = xt[29:32]


def pack(sweeps):
    frame_block = lambda rows: pl.BlockSpec((rows, 32, 128), lambda f: (0, f, 0))
    fixed_block = lambda rows: pl.BlockSpec((rows, 32, 128), lambda f: (0, 0, 0))
    return pl.pallas_call(
        pack_kernel,
        grid=(8,),
        in_specs=[pl.BlockSpec((32, 1, 32, 128), lambda f: (0, f, 0, 0))],
        out_specs=[frame_block(32), frame_block(3), frame_block(3), fixed_block(32), fixed_block(3), fixed_block(3)],
        out_shape=[
            struct((32, 256, 128)),
            struct((3, 256, 128)),
            struct((3, 256, 128)),
            struct((32, 32, 128)),
            struct((3, 32, 128)),
            struct((3, 32, 128)),
        ],
        scratch_shapes=[pltpu.VMEM((256, 256), BF)],
        compiler_params=params(),
        cost_estimate=cost(6e8, 4.6e6),
        name="pack",
    )(sweeps)


def weights_kernel(kt, k1, k2, b0, b1, b2, w, ws, w1, w2, c0, c1, c2):
    base = {}
    for d in range(3):
        for b in range(3):
            rows = [kt[a, b, d].astype(F32) for a in range(3)] + [jnp.zeros((32, 64), F32)]
            base[d, b] = jnp.concatenate(rows, axis=0).T
    shifted = {}
    for key, value in base.items():
        shifted[key + (0,)] = value.astype(BF)
        shifted[key + (1,)] = pltpu.roll(value, 32, 1).astype(BF)
    for d in range(3):
        for fo in range(2):
            for b in range(3):
                ws[fo * 64 : fo * 64 + 64, (b * 3 + d) * 128 : (b * 3 + d) * 128 + 128] = shifted[d, b, fo]
            for ro in range(2):
                top = d * 256 + fo * 128 + ro * 64
                for ri in range(4):
                    b = ri - ro
                    block = shifted[d, b, fo] if 0 <= b <= 2 else jnp.zeros((64, 128), BF)
                    w[top : top + 64, ri * 128 : ri * 128 + 128] = block
    w1[...] = k1[...].reshape(576, 128).astype(F32).T.astype(BF)
    w2[...] = k2[...].reshape(1152, 128).astype(F32).T.astype(BF)
    wide = jnp.concatenate([b0[...], jnp.zeros((1, 64), F32)], axis=1)
    c0[...] = jnp.broadcast_to(wide, (128, 128)).T[0:64]
    c1[...] = jnp.broadcast_to(b1[...], (128, 128)).T
    c2[...] = jnp.broadcast_to(b2[...], (128, 128)).T


def weights(kt, b0, k1, b1, k2, b2):
    return pl.pallas_call(
        weights_kernel,
        in_specs=[VMEM] * 6,
        out_specs=[VMEM] * 7,
        out_shape=[
            struct((768, 512)),
            struct((128, 1152)),
            struct((128, 576)),
            struct((128, 1152)),
            struct((64, 128), F32),
            struct((128, 128), F32),
            struct((128, 128), F32),
        ],
        compiler_params=params(),
        cost_estimate=cost(1e6, 3e6),
        name="weights",
    )(
        jnp.transpose(kt, (2, 3, 4, 1, 0)),
        jnp.transpose(k1, (2, 3, 1, 0)),
        jnp.transpose(k2, (2, 3, 1, 0)),
        b0.reshape(1, 64),
        b1.reshape(1, 128),
        b2.reshape(1, 128),
    )


def strip_pack_kernel(xt, up, dn, slab, sup, sdn, left, right):
    lane = lanes_of((16, 128))

    def gather(read, at):
        acc_l = jnp.zeros((16, 128), BF)
        acc_r = jnp.zeros((16, 128), BF)
        for row in range(38):
            here = (lane >= 3 * row) & (lane < 3 * row + 3)
            tile = read(row)
            acc_l = jnp.where(here, pltpu.roll(tile, 3 * row, 1), acc_l)
            acc_r = jnp.where(here, pltpu.roll(tile, 3 * row + 3, 1), acc_r)
        left[at, :] = acc_l
        right[at, :] = acc_r

    def source(above, middle, below, at):
        def read(row):
            if row < 3:
                return above[row, at, :]
            if row < 35:
                return middle[row - 3, at, :]
            return below[row - 35, at, :]

        return read

    @pl.loop(0, 16)
    def _(s):
        at = pl.ds(pl.multiple_of(s * 16, 16), 16)
        gather(source(up, xt, dn, at), at)

    for s in range(2):
        at = pl.ds(s * 16, 16)
        gather(source(sup, slab, sdn, at), pl.ds(256 + s * 16, 16))


def strip_pack(*args):
    return pl.pallas_call(
        strip_pack_kernel,
        in_specs=[VMEM] * 6,
        out_specs=[VMEM] * 2,
        out_shape=[struct((288, 128))] * 2,
        compiler_params=params(),
        cost_estimate=cost(1e8, 3e6),
        name="strip_pack",
    )(*args)


def temporal_kernel(own, xt, up, dn, slab, sup, sdn, w, bias, fw, *rest):
    if own:
        out, xs, sems = rest
        quads = 4
    else:
        out, shared, xs, sems = rest
        quads = 5
    t = lax.axis_index("tm")
    lower = t == 1 if own else t == 0
    depth = 4 * quads + 2
    first = jnp.where(lower, 38 - depth, 0)
    inner = depth - 3
    start = jnp.where(lower, 32 - inner, 0)
    at_slab = 288 * (1 - t)
    at_zero = pl.ds(pl.multiple_of(288 * t, 32), 32)
    at_slab = pl.ds(pl.multiple_of(at_slab, 32), 32)
    frames = pl.ds(32, 256)
    place = jnp.where(lower, 0, 3)

    def moves(edge, edge_slab, edge_at):
        return [
            pltpu.make_async_copy(xt.at[pl.ds(start, inner)], xs.at[pl.ds(place, inner), frames], sems.at[0]),
            pltpu.make_async_copy(slab.at[pl.ds(start, inner)], xs.at[pl.ds(place, inner), at_slab], sems.at[1]),
            pltpu.make_async_copy(edge, xs.at[pl.ds(edge_at, 3), frames], sems.at[2]),
            pltpu.make_async_copy(edge_slab, xs.at[pl.ds(edge_at, 3), at_slab], sems.at[3]),
        ]

    @pl.when(lower)
    def _():
        for move in moves(dn, sdn, inner):
            move.start()

    @pl.when(jnp.logical_not(lower))
    def _():
        for move in moves(up, sup, 0):
            move.start()

    xs[:, at_zero, :] = jnp.zeros((depth, 32, 128), BF)
    for move in moves(up, sup, 0):
        move.wait()

    wide_bias = jnp.concatenate([bias[...], bias[...]], axis=0)

    @pl.loop(0, quads)
    def _(n):
        base = 4 * n
        acc = [jnp.zeros((128, 128), F32) for _ in range(2)]
        for g in range(4):
            sub = slice(64 * g, 64 * g + 128)
            rhs = jnp.concatenate(
                [jnp.concatenate([xs[base + ri, sub, :], xs[base + 2 + ri, sub, :]], axis=1) for ri in range(4)],
                axis=0,
            )
            y = dot(w[...], rhs)
            for fo in range(2):
                scale = fw[t * 8 + 2 * g + fo]
                for half in range(2):
                    cols = slice(128 * half, 128 * half + 128)
                    part = [y[d * 256 + fo * 128 : d * 256 + fo * 128 + 128, cols] for d in range(3)]
                    z = part[1] + pltpu.roll(part[0], 1, 1) + pltpu.roll(part[2], 127, 1) + wide_bias
                    acc[half] = acc[half] + jnp.maximum(z, 0.0) * scale
        for half in range(2):
            for ro in range(2):
                out[base + 2 * half + ro] = acc[half][ro * 64 : ro * 64 + 64].astype(out.dtype)
        if not own:

            @pl.when(n == 4 * t)
            def _():
                for half in range(2):
                    for ro in range(2):
                        shared[2 * half + ro] = acc[half][ro * 64 : ro * 64 + 64]


def temporal(own, xt, up, dn, slab, sup, sdn, w, bias, fw):
    quads = 4 if own else 5
    if own:
        out_shape = [struct((16, 64, 128), F32)]
    else:
        out_shape = [struct((20, 64, 128)), struct((4, 64, 128), F32)]
    return pl.pallas_call(
        functools.partial(temporal_kernel, own),
        in_specs=[ANY] * 6 + [VMEM, VMEM, SMEM],
        out_specs=[VMEM] * len(out_shape),
        out_shape=out_shape,
        scratch_shapes=[pltpu.VMEM((4 * quads + 2, 320, 128), BF), pltpu.SemaphoreType.DMA((4,))],
        compiler_params=params(),
        cost_estimate=cost(quads * 4 * 768 * 512 * 256 * 2, 3e6),
        name="temporal_own" if own else "temporal_partner",
    )(xt, up, dn, slab, sup, sdn, w, bias, fw)


def strip_temporal_kernel(own_l, own_r, nb_l, nb_r, ws, bias, fw, out, send, windows):
    t = lax.axis_index("tm")
    lane = lanes_of((16, 128))
    third = lane % 3

    windows[:, pl.ds(pl.multiple_of(288 * t, 32), 32), :] = jnp.zeros((9, 32, 256), BF)

    def fill(s, at):
        src = pl.ds(pl.multiple_of(s * 16, 16), 16)
        dst = pl.ds(pl.multiple_of(at, 16), 16)
        ol, nl, orr, nr = own_l[src, :], nb_l[src, :], own_r[src, :], nb_r[src, :]
        for b in range(3):
            for d in range(3):
                lo = pltpu.roll(nl, (128 - (3 * b + d)) % 128, 1)
                if d > 0:
                    lo = jnp.where(third < 3 - d, lo, pltpu.roll(ol, (128 - (3 * b + d - 3)) % 128, 1))
                hi = pltpu.roll(nr, (128 - (3 * b + d - 2)) % 128, 1)
                if d < 2:
                    hi = jnp.where(third < 2 - d, pltpu.roll(orr, 128 - (3 * b + d + 1), 1), hi)
                windows[b * 3 + d, dst, 0:128] = lo
                windows[b * 3 + d, dst, 128:256] = hi

    @pl.loop(0, 18)
    def _(s):
        fill(s, jnp.where(s < 16, 32 + 16 * s, 288 * (1 - t) + (s - 16) * 16))

    wide_bias = jnp.concatenate([bias[...], bias[...]], axis=1)
    acc = jnp.zeros((64, 256), F32)
    for g in range(4):
        rhs = jnp.concatenate([windows[k, 64 * g : 64 * g + 128, :] for k in range(9)], axis=0)
        y = dot(ws[...], rhs)
        for fo in range(2):
            acc = acc + jnp.maximum(y[fo * 64 : fo * 64 + 64] + wide_bias, 0.0) * fw[t * 8 + 2 * g + fo]
    for side in range(2):
        out[side] = acc[:, side * 128 : side * 128 + 128]
        send[side] = acc[:, side * 128 : side * 128 + 128].astype(BF)


def strip_temporal(own_l, own_r, nb_l, nb_r, ws, bias, fw):
    return pl.pallas_call(
        strip_temporal_kernel,
        in_specs=[VMEM] * 6 + [SMEM],
        out_specs=[VMEM] * 2,
        out_shape=[struct((2, 64, 128), F32), struct((2, 64, 128))],
        scratch_shapes=[pltpu.VMEM((9, 320, 256), BF)],
        compiler_params=params(),
        cost_estimate=cost(4 * 128 * 1152 * 256 * 2, 1e6),
        name="strip_temporal",
    )(own_l, own_r, nb_l, nb_r, ws, bias, fw)


def spatial_kernel(grid_rows, main, shared, partner, strips, partner_strips, w1, b1, w2, b2, out, c3, h3, ms):
    t = lax.axis_index("tm")
    row = lax.axis_index("row")
    col = lax.axis_index("col")
    first_col = col == 0
    last_col = col == lax.axis_size("col") - 1
    top = row * 32 + t * 16
    lane = lanes_of((64, 128))
    depth = lane // 3
    third = lane % 3

    def in_grid(g):
        return (g >= 0) & (g < grid_rows)

    edges = []
    for side in range(2):
        total = strips[side] + partner_strips[side].astype(F32)
        total = pltpu.roll(total, (128 - 48 * t) % 128, 1)
        off = (third < 2) & first_col if side == 0 else (third > 0) & last_col
        keep = in_grid(top + depth - 2) & jnp.logical_not(off)
        edges.append(jnp.where(keep, total, 0.0))
    edges_b = [edge.astype(BF) for edge in edges]

    def insert(index, value):
        value = value + partner[index].astype(F32)
        value = jnp.where(lane == 0, pltpu.roll(edges[0], lax.rem(254 - 3 * index, 128), 1), value)
        value = jnp.where(lane == 127, pltpu.roll(edges[1], 127 - 3 * index, 1), value)
        value = jnp.where(in_grid(top + index - 2), value, 0.0).astype(BF)
        c3[index, 0:64] = jnp.where(
            lane == 0, pltpu.roll(edges_b[0], 127 - 3 * index, 1), pltpu.roll(value, 1, 1)
        )
        c3[index, 64:128] = value
        c3[index, 128:192] = jnp.where(
            lane == 127, pltpu.roll(edges_b[1], 126 - 3 * index, 1), pltpu.roll(value, 127, 1)
        )

    @pl.loop(0, 16)
    def _(i):
        insert(i + 4 * t, main[i])

    @pl.loop(0, 4)
    def _(i):
        insert(i + 16 * (1 - t), shared[i])

    wide_b1 = jnp.concatenate([b1[...], b1[...]], axis=1)
    wide_b2 = jnp.concatenate([b2[...], b2[...]], axis=1)

    rhs = jnp.concatenate(
        [
            jnp.concatenate([pltpu.roll(edges_b[side], (128 - 3 * b - d) % 128, 1) for side in range(2)], axis=1)
            for b in range(3)
            for d in range(3)
        ],
        axis=0,
    )
    y = jnp.maximum(dot(w1[...], rhs) + wide_b1, 0.0)
    lane2 = lanes_of((128, 128))
    kept = in_grid(top + lane2 // 3 - 1)
    hs_l = jnp.where(kept & jnp.logical_not(first_col), y[:, :128], 0.0).astype(BF)
    hs_r = jnp.where(kept & jnp.logical_not(last_col), y[:, 128:], 0.0).astype(BF)

    @pl.loop(0, 9)
    def _(i):
        h = 2 * i
        rhs = jnp.concatenate(
            [jnp.concatenate([c3[h + b], c3[h + 1 + b]], axis=1) for b in range(3)], axis=0
        )
        y = jnp.maximum(dot(w1[...], rhs) + wide_b1, 0.0)
        for half in range(2):
            at = h + half
            value = jnp.where(in_grid(top + at - 1), y[:, half * 128 : half * 128 + 128], 0.0).astype(BF)
            h3[at, 0:128] = jnp.where(
                lane2 == 0, pltpu.roll(hs_l, lax.rem(128 - 3 * at, 128), 1), pltpu.roll(value, 1, 1)
            )
            h3[at, 128:256] = value
            h3[at, 256:384] = jnp.where(
                lane2 == 127, pltpu.roll(hs_r, 127 - 3 * at, 1), pltpu.roll(value, 127, 1)
            )

    @pl.loop(0, 8)
    def _(i):
        r = 2 * i
        rhs = jnp.concatenate(
            [jnp.concatenate([h3[r + b], h3[r + 1 + b]], axis=1) for b in range(3)], axis=0
        )
        y = jnp.maximum(dot(w2[...], rhs) + wide_b2, 0.0).astype(BF)
        ms[r] = y[:, :128]
        ms[r + 1] = y[:, 128:]

    perm = swap16()
    for pair in range(4):
        halves = [ms[:, (2 * pair + k) * 16 : (2 * pair + k) * 16 + 16, :].reshape(256, 128) for k in range(2)]
        y = dot(perm, jnp.concatenate(halves, axis=1)).astype(BF)
        for k in range(2):
            q = (2 * pair + k) * 16
            out[q : q + 16] = y[:, k * 128 : k * 128 + 128].reshape(16, 16, 128)


def spatial(grid_rows, *args):
    return pl.pallas_call(
        functools.partial(spatial_kernel, grid_rows),
        in_specs=[VMEM] * 9,
        out_specs=VMEM,
        out_shape=struct((128, 16, 128)),
        scratch_shapes=[
            pltpu.VMEM((20, 192, 128), BF),
            pltpu.VMEM((18, 384, 128), BF),
            pltpu.VMEM((16, 128, 128), BF),
        ],
        compiler_params=params(),
        cost_estimate=cost(1.2e9, 3e6),
        name="spatial",
    )(*args)


def shards(sweeps, kt, b0, fw, k1, b1, k2, b2):
    rows = lax.axis_size("row")
    cols = lax.axis_size("col")
    both = [(0, 1), (1, 0)]
    down = [(i, i + 1) for i in range(rows - 1)]
    up_route = [(i + 1, i) for i in range(rows - 1)]
    cross_down = [(t * rows + i, (1 - t) * rows + i + 1) for t in range(2) for i in range(rows - 1)]
    cross_up = [(t * rows + i + 1, (1 - t) * rows + i) for t in range(2) for i in range(rows - 1)]

    xt, first_rows, last_rows, slab, slab_first, slab_last = pack(sweeps)
    w, ws, w1, w2, c0, c1, c2 = weights(kt, b0, k1, b1, k2, b2)
    up = lax.ppermute(last_rows, "row", down)
    dn = lax.ppermute(first_rows, "row", up_route)
    halo = lax.ppermute(slab, "tm", both)
    sup = lax.ppermute(slab_last, ("tm", "row"), cross_down)
    sdn = lax.ppermute(slab_first, ("tm", "row"), cross_up)
    field = (xt, up, dn, halo, sup, sdn)

    own_l, own_r = strip_pack(*field)
    nb_l = lax.ppermute(own_r, "col", [(i, i + 1) for i in range(cols - 1)])
    nb_r = lax.ppermute(own_l, "col", [(i + 1, i) for i in range(cols - 1)])

    for_partner, shared = temporal(False, *field, w, c0, fw)
    partner = lax.ppermute(for_partner, "tm", both)
    strips, strips_send = strip_temporal(own_l, own_r, nb_l, nb_r, ws, c0, fw)
    partner_strips = lax.ppermute(strips_send, "tm", both)
    (main,) = temporal(True, *field, w, c0, fw)
    return spatial(rows * 32, main, shared, partner, strips, partner_strips, w1, c1, w2, c2)


def solution(mesh):
    placed = (P(None, "tm", "row", "col"), P(), P(), P(), P(), P(), P(), P())
    return jax.shard_map(
        shards, mesh=mesh, in_specs=placed, out_specs=P(None, ("row", "tm"), "col"), check_vma=False
    )
```

time: 262 us -> 65.9 us (0.25)
  the two profiles are of different devices: /device:TPU:30 before, /device:TPU:1 now
where the time goes in v1:
time: 65.9 us; the launch traced here: 65.7 us
  Pallas kernels  31.8 us (48%)
  starting transfers between devices  26.6 us (40%)
  waiting for transfers between devices  4.28 us (6%)
  local copies, waits for them, and re-layouts  2.85 us (4%)
    pallas_call x2, Pallas kernels, temporal(): pl.pallas_call(functools.partial(temporal_kernel, own), in_specs=[ANY] *...  12.3 us
    pallas_call x1, Pallas kernels, spatial(): pl.pallas_call(functools.partial(spatial_kernel, grid_rows), in_specs=[VM...  9.39 us
    ppermute x1, starting transfers between devices, shards(): sup = lax.ppermute(slab_last, ('tm', 'row'), cross_down)  6.28 us
    ppermute x1, starting transfers between devices, shards(): nb_r = lax.ppermute(own_l, 'col', [(i + 1, i) for i in range(cols - 1)])  5.63 us
    ppermute x1, starting transfers between devices, shards(): up = lax.ppermute(last_rows, 'row', down)  4.89 us
    pallas_call x1, Pallas kernels, pack(): pl.pallas_call(pack_kernel, grid=(8,), in_specs=[pl.BlockSpec((32, 1, 32,...  4.1 us
    ppermute x1, waiting for transfers between devices, shards(): sdn = lax.ppermute(slab_first, ('tm', 'row'), cross_up)  3.51 us
    ppermute x1, starting transfers between devices, shards(): nb_l = lax.ppermute(own_r, 'col', [(i, i + 1) for i in range(cols - 1)])  3.03 us
  transfers between devices with their start and end apart: 9, of which 3 were waited for; matrix products, arithmetic and copies ran while one was open for 2% of the time, Pallas kernels for 24%

profile of v1, /device:TPU:1, one launch (start us, length us, event | category | flops | bytes accessed | tf_op | source)
XLA Modules:
  0.0 65.7 jit_solution(12755873123229296737)
XLA Ops:
  0.0 1.6 %copy-done.5 = bf16[32,8,32,128]{3,2,1,0:T(8,128)(2,1)S(1)} copy-done((bf16[32,8,32,128]{3,2,1,0:T(8,128)(2,1)S(1)}, bf16[32,8,32,128]{3,2,1,0:T(8,128)(2,1)}, u32[]{:S(2)}) %copy-start.5) | copy-done | bytes 2097176
  1.7 4.1 %pack.1 = (bf16[32,256,128]{2,1,0:T(8,128)(2,1)S(1)}, bf16[3,256,128]{2,1,0:T(8,128)(2,1)}, bf16[3,256,128]{2,1,0:T(8,128)(2,1)}, bf16[32,32,128]{2,1,0:T(8,128)...) custom-call(bf16[32,8,32,128]{3,2,1,0:T(8,128)(2,1)S(1)} %copy-done.5), custom_call_target="tpu_custom_call" | custom-call | flops 600000000 | bytes 4600000 | tf_op jit(solution)/shard_map/pack/pallas_call | solution.py:69
  5.8 2.5 %collective-permute-start.2 = (bf16[32,32,128]{2,1,0:T(8,128)(2,1)}, bf16[32,32,128]{2,1,0:T(8,128)(2,1)S(1)}, u32[]{:S(2)}, u32[]{:S(2)}) collective-permute-start(bf16[32,32,128]{2,1,0:T(8,128)(2,1)} %get-tuple-element.27), channel_id=1, source_target_pairs={{0,128},{128,0},{1,129},{129,1},{2,130},{130,2},{3,131},{131,3},{4... | collective-permute-start | bytes 786440 | tf_op jit(solution)/shard_map/ppermute | solution.py:460
  8.3 4.9 %collective-permute-start = (bf16[3,256,128]{2,1,0:T(8,128)(2,1)}, bf16[3,256,128]{2,1,0:T(8,128)(2,1)S(1)}, u32[]{:S(2)}, u32[]{:S(2)}) collective-permute-start(bf16[3,256,128]{2,1,0:T(8,128)(2,1)} %get-tuple-element.25), channel_id=1, source_target_pairs={{0,8},{8,16},{16,24},{24,32},{32,40},{40,48},{48,56},{56,64},{64,7... | collective-permute-start | bytes 589832 | tf_op jit(solution)/shard_map/ppermute | solution.py:458
  13.2 1.3 %collective-permute-start.1 = (bf16[3,256,128]{2,1,0:T(8,128)(2,1)}, bf16[3,256,128]{2,1,0:T(8,128)(2,1)S(1)}, u32[]{:S(2)}, u32[]{:S(2)}) collective-permute-start(bf16[3,256,128]{2,1,0:T(8,128)(2,1)} %get-tuple-element.26), channel_id=1, source_target_pairs={{8,0},{16,8},{24,16},{32,24},{40,32},{48,40},{56,48},{64,56},{72,6... | collective-permute-start | bytes 589832 | tf_op jit(solution)/shard_map/ppermute | solution.py:459
  14.5 6.3 %collective-permute-start.3 = (bf16[3,32,128]{2,1,0:T(8,128)(2,1)S(1)}, bf16[3,32,128]{2,1,0:T(8,128)(2,1)S(1)}, u32[]{:S(2)}, u32[]{:S(2)}) collective-permute-start(bf16[3,32,128]{2,1,0:T(8,128)(2,1)S(1)} %get-tuple-element.28), channel_id=1, source_target_pairs={{0,136},{8,144},{16,152},{24,160},{32,168},{40,176},{48,184},{56,1... | collective-permute-start | bytes 73736 | tf_op jit(solution)/shard_map/ppermute | solution.py:461
  20.8 1.3 %collective-permute-start.4 = (bf16[3,32,128]{2,1,0:T(8,128)(2,1)S(1)}, bf16[3,32,128]{2,1,0:T(8,128)(2,1)S(1)}, u32[]{:S(2)}, u32[]{:S(2)}) collective-permute-start(bf16[3,32,128]{2,1,0:T(8,128)(2,1)S(1)} %get-tuple-element.29), channel_id=1, source_target_pairs={{8,128},{16,136},{24,144},{32,152},{40,160},{48,168},{56,176},{64,... | collective-permute-start | bytes 73736 | tf_op jit(solution)/shard_map/ppermute | solution.py:462
  22.1 1.2 %copy.9 = bf16[128,128,3,3]{0,1,3,2:T(8,128)(2,1)S(1)} copy(bf16[128,128,3,3]{1,0,3,2:T(8,128)(2,1)} %param.14) | data formatting | bytes 589824 | tf_op args[6]
  23.4 0.4 weights.1
  23.8 0.0 collective-permute-done.3.sup
  23.8 3.5 %collective-permute-done.4.sdn = bf16[3,32,128]{2,1,0:T(8,128)(2,1)S(1)} collective-permute-done((bf16[3,32,128]{2,1,0:T(8,128)(2,1)S(1)}, bf16[3,32,128]{2,1,0:T(8,128)(2,1)S(1)}, u32[]{:S(2)}, u32[]{:S(2)}) %collective-permute-start.4) | collective-permute-done | bytes 24608 | tf_op jit(solution)/shard_map/ppermute | solution.py:462
  27.3 0.0 collective-permute-done.up
  27.3 0.6 collective-permute-done.1.dn
  27.9 0.0 collective-permute-done.2.slab
  28.0 2.6 %strip_pack.1 = (bf16[288,128]{1,0:T(8,128)(2,1)S(1)}, bf16[288,128]{1,0:T(8,128)(2,1)S(1)}) custom-call(bf16[32,256,128]{2,1,0:T(8,128)(2,1)S(1)} %get-tuple-element.24.xt, bf16[3,256,128]{2,1,0:T(8,128)(2,1)S(1)} %collective-permute-done.up, bf16[3,256,128]{2,1,0:T(8,128)(2,1)S(1)} %collective-permute-done.1.dn, ...), custom_call_target="tpu_custom_call" | custom-call | flops 100000000 | bytes 3000000 | tf_op jit(solution)/shard_map/strip_pack/pallas_call | solution.py:179
  30.6 5.6 %collective-permute-start.7 = (bf16[288,128]{1,0:T(8,128)(2,1)S(1)}, bf16[288,128]{1,0:T(8,128)(2,1)S(1)}, u32[]{:S(2)}, u32[]{:S(2)}) collective-permute-start(bf16[288,128]{1,0:T(8,128)(2,1)S(1)} %get-tuple-element.34.own_l), channel_id=1, source_target_pairs={{1,0},{2,1},{3,2},{4,3},{5,4},{6,5},{7,6},{9,8},{10,9},{11,10},{12... | collective-permute-start | bytes 221192 | tf_op jit(solution)/shard_map/ppermute | solution.py:467
  36.2 3.0 %collective-permute-start.6 = (bf16[288,128]{1,0:T(8,128)(2,1)S(1)}, bf16[288,128]{1,0:T(8,128)(2,1)S(1)}, u32[]{:S(2)}, u32[]{:S(2)}) collective-permute-start(bf16[288,128]{1,0:T(8,128)(2,1)S(1)} %get-tuple-element.35.own_r), channel_id=1, source_target_pairs={{0,1},{1,2},{2,3},{3,4},{4,5},{5,6},{6,7},{8,9},{9,10},{10,11},{11... | collective-permute-start | bytes 221192 | tf_op jit(solution)/shard_map/ppermute | solution.py:466
  39.3 6.8 %temporal_partner.1 = (bf16[20,64,128]{2,1,0:T(8,128)(2,1)S(1)}, f32[4,64,128]{2,1,0:T(8,128)S(1)}) custom-call(bf16[32,256,128]{2,1,0:T(8,128)(2,1)S(1)} %get-tuple-element.24.xt, bf16[3,256,128]{2,1,0:T(8,128)(2,1)S(1)} %collective-permute-done.up, bf16[3,256,128]{2,1,0:T(8,128)(2,1)S(1)} %collective-permute-done.1.dn, ...), custom_call_target="tpu_custom_call" | custom-call | flops 4026531840 | bytes 3000000 | tf_op jit(solution)/shard_map/temporal_partner/pallas_call | solution.py:269
  46.0 0.1 collective-permute-start.5
  46.2 2.9 %strip_temporal.1 = (f32[2,64,128]{2,1,0:T(8,128)S(1)}, bf16[2,64,128]{2,1,0:T(8,128)(2,1)S(1)}) custom-call(bf16[288,128]{1,0:T(8,128)(2,1)S(1)} %get-tuple-element.34.own_l, bf16[288,128]{1,0:T(8,128)(2,1)S(1)} %get-tuple-element.35.own_r, bf16[288,128]{1,0:T(8,128)(2,1)S(1)} %collective-permute-done.6.nb_l, ...), custom_call_target="tpu_custom_call" | custom-call | flops 301989888 | bytes 1000000 | tf_op jit(solution)/shard_map/strip_temporal/pallas_call | solution.py:320
  49.1 1.5 %collective-permute-start.8 = (bf16[2,64,128]{2,1,0:T(8,128)(2,1)S(1)}, bf16[2,64,128]{2,1,0:T(8,128)(2,1)S(1)}, u32[]{:S(2)}, u32[]{:S(2)}) collective-permute-start(bf16[2,64,128]{2,1,0:T(8,128)(2,1)S(1)} %get-tuple-element.38), channel_id=1, source_target_pairs={{0,128},{128,0},{1,129},{129,1},{2,130},{130,2},{3,131},{131,3},{4... | collective-permute-start | bytes 98312 | tf_op jit(solution)/shard_map/ppermute | solution.py:472
  50.6 5.5 %temporal_own.1.main = f32[16,64,128]{2,1,0:T(8,128)S(1)} custom-call(bf16[32,256,128]{2,1,0:T(8,128)(2,1)S(1)} %get-tuple-element.24.xt, bf16[3,256,128]{2,1,0:T(8,128)(2,1)S(1)} %collective-permute-done.up, bf16[3,256,128]{2,1,0:T(8,128)(2,1)S(1)} %collective-permute-done.1.dn, bf16[32,32,128]{2,1,0:T(8,128)(2,1)S(1)} %collective-permute-done.2.slab, ...), custom_call_target="tpu_custom_call" | custom-call | flops 3221225472 | bytes 3000000 | tf_op jit(solution)/shard_map/temporal_own/pallas_call | solution.py:269
  56.1 0.1 collective-permute-done.8.partner_strips
  56.3 9.4 %spatial.1 = bf16[128,16,128]{2,1,0:T(8,128)(2,1)} custom-call(f32[16,64,128]{2,1,0:T(8,128)S(1)} %temporal_own.1.main, f32[4,64,128]{2,1,0:T(8,128)S(1)} %get-tuple-element.32.shared, bf16[20,64,128]{2,1,0:T(8,128)(2,1)S(1)} %collective-permute-done.5.partner, f32[2,64,128]{2,1,0:T(8,128)S(1)} %get-tuple-element.37.strips, ...), custom_call_target="tpu_custom_call" | custom-call | flops 1200000000 | bytes 3000000 | tf_op jit(solution)/shard_map/spatial/pallas_call | solution.py:431
  (16 shorter events, 0.0 us)
Async XLA Ops:
  0.0 23.3 %copy-start.4 = (f32[128]{0:T(128)S(1)}, f32[128]{0:T(128)}, u32[]{:S(2)}) copy-start(f32[128]{0:T(128)} %param.15) | copy-start | bytes 1540
  0.0 23.3 %copy-start.3 = (f32[128]{0:T(128)S(1)}, f32[128]{0:T(128)}, u32[]{:S(2)}) copy-start(f32[128]{0:T(128)} %param.13) | copy-start | bytes 1540
  0.0 23.3 %copy-start.1 = (bf16[128,64,3,3]{0,1,3,2:T(8,128)(2,1)S(1)}, bf16[128,64,3,3]{0,1,3,2:T(8,128)(2,1)}, u32[]{:S(2)}) copy-start(bf16[128,64,3,3]{0,1,3,2:T(8,128)(2,1)} %param.12) | copy-start | bytes 442372
  0.0 23.3 %copy-start.2 = (f32[64]{0:T(128)S(1)}, f32[64]{0:T(128)}, u32[]{:S(2)}) copy-start(f32[64]{0:T(128)} %param.10) | copy-start | bytes 772
  0.0 23.3 %copy-start = (bf16[64,32,3,3,3]{0,1,4,3,2:T(8,128)(2,1)S(1)}, bf16[64,32,3,3,3]{0,1,4,3,2:T(8,128)(2,1)}, u32[]{:S(2)}) copy-start(bf16[64,32,3,3,3]{0,1,4,3,2:T(8,128)(2,1)} %param.9) | copy-start | bytes 331780
  0.0 1.7 %copy-start.5 = (bf16[32,8,32,128]{3,2,1,0:T(8,128)(2,1)S(1)}, bf16[32,8,32,128]{3,2,1,0:T(8,128)(2,1)}, u32[]{:S(2)}) copy-start(bf16[32,8,32,128]{3,2,1,0:T(8,128)(2,1)} %x.1) | copy-start | bytes 6291460
  5.8 33.5 %copy-start.6 = (f32[16]{0:T(128)S(1)}, f32[16]{0:T(128)}, u32[]{:S(2)}) copy-start(f32[16]{0:T(128)} %fw.5) | copy-start | bytes 196
  5.8 22.2 %collective-permute-start.2 = (bf16[32,32,128]{2,1,0:T(8,128)(2,1)}, bf16[32,32,128]{2,1,0:T(8,128)(2,1)S(1)}, u32[]{:S(2)}, u32[]{:S(2)}) collective-permute-start(bf16[32,32,128]{2,1,0:T(8,128)(2,1)} %get-tuple-element.27), channel_id=1, source_target_pairs={{0,128},{128,0},{1,129},{129,1},{2,130},{130,2},{3,131},{131,3},{4... | collective-permute-start | bytes 786440 | tf_op jit(solution)/shard_map/ppermute | solution.py:460
  8.3 19.0 %collective-permute-start = (bf16[3,256,128]{2,1,0:T(8,128)(2,1)}, bf16[3,256,128]{2,1,0:T(8,128)(2,1)S(1)}, u32[]{:S(2)}, u32[]{:S(2)}) collective-permute-start(bf16[3,256,128]{2,1,0:T(8,128)(2,1)} %get-tuple-element.25), channel_id=1, source_target_pairs={{0,8},{8,16},{16,24},{24,32},{32,40},{40,48},{48,56},{56,64},{64,7... | collective-permute-start | bytes 589832 | tf_op jit(solution)/shard_map/ppermute | solution.py:458
  13.2 14.7 %collective-permute-start.1 = (bf16[3,256,128]{2,1,0:T(8,128)(2,1)}, bf16[3,256,128]{2,1,0:T(8,128)(2,1)S(1)}, u32[]{:S(2)}, u32[]{:S(2)}) collective-permute-start(bf16[3,256,128]{2,1,0:T(8,128)(2,1)} %get-tuple-element.26), channel_id=1, source_target_pairs={{8,0},{16,8},{24,16},{32,24},{40,32},{48,40},{56,48},{64,56},{72,6... | collective-permute-start | bytes 589832 | tf_op jit(solution)/shard_map/ppermute | solution.py:459
  14.5 9.2 %collective-permute-start.3 = (bf16[3,32,128]{2,1,0:T(8,128)(2,1)S(1)}, bf16[3,32,128]{2,1,0:T(8,128)(2,1)S(1)}, u32[]{:S(2)}, u32[]{:S(2)}) collective-permute-start(bf16[3,32,128]{2,1,0:T(8,128)(2,1)S(1)} %get-tuple-element.28), channel_id=1, source_target_pairs={{0,136},{8,144},{16,152},{24,160},{32,168},{40,176},{48,184},{56,1... | collective-permute-start | bytes 73736 | tf_op jit(solution)/shard_map/ppermute | solution.py:461
  20.8 6.5 %collective-permute-start.4 = (bf16[3,32,128]{2,1,0:T(8,128)(2,1)S(1)}, bf16[3,32,128]{2,1,0:T(8,128)(2,1)S(1)}, u32[]{:S(2)}, u32[]{:S(2)}) collective-permute-start(bf16[3,32,128]{2,1,0:T(8,128)(2,1)S(1)} %get-tuple-element.29), channel_id=1, source_target_pairs={{8,128},{16,136},{24,144},{32,152},{40,160},{48,168},{56,176},{64,... | collective-permute-start | bytes 73736 | tf_op jit(solution)/shard_map/ppermute | solution.py:462
  30.6 15.6 %collective-permute-start.7 = (bf16[288,128]{1,0:T(8,128)(2,1)S(1)}, bf16[288,128]{1,0:T(8,128)(2,1)S(1)}, u32[]{:S(2)}, u32[]{:S(2)}) collective-permute-start(bf16[288,128]{1,0:T(8,128)(2,1)S(1)} %get-tuple-element.34.own_l), channel_id=1, source_target_pairs={{1,0},{2,1},{3,2},{4,3},{5,4},{6,5},{7,6},{9,8},{10,9},{11,10},{12... | collective-permute-start | bytes 221192 | tf_op jit(solution)/shard_map/ppermute | solution.py:467
  36.2 9.9 %collective-permute-start.6 = (bf16[288,128]{1,0:T(8,128)(2,1)S(1)}, bf16[288,128]{1,0:T(8,128)(2,1)S(1)}, u32[]{:S(2)}, u32[]{:S(2)}) collective-permute-start(bf16[288,128]{1,0:T(8,128)(2,1)S(1)} %get-tuple-element.35.own_r), channel_id=1, source_target_pairs={{0,1},{1,2},{2,3},{3,4},{4,5},{5,6},{6,7},{8,9},{9,10},{10,11},{11... | collective-permute-start | bytes 221192 | tf_op jit(solution)/shard_map/ppermute | solution.py:466
  46.0 10.2 %collective-permute-start.5 = (bf16[20,64,128]{2,1,0:T(8,128)(2,1)S(1)}, bf16[20,64,128]{2,1,0:T(8,128)(2,1)S(1)}, u32[]{:S(2)}, u32[]{:S(2)}) collective-permute-start(bf16[20,64,128]{2,1,0:T(8,128)(2,1)S(1)} %get-tuple-element.33), channel_id=1, source_target_pairs={{0,128},{128,0},{1,129},{129,1},{2,130},{130,2},{3,131},{131,3},{4... | collective-permute-start | bytes 983048 | tf_op jit(solution)/shard_map/ppermute | solution.py:470
  49.1 7.2 %collective-permute-start.8 = (bf16[2,64,128]{2,1,0:T(8,128)(2,1)S(1)}, bf16[2,64,128]{2,1,0:T(8,128)(2,1)S(1)}, u32[]{:S(2)}, u32[]{:S(2)}) collective-permute-start(bf16[2,64,128]{2,1,0:T(8,128)(2,1)S(1)} %get-tuple-element.38), channel_id=1, source_target_pairs={{0,128},{128,0},{1,129},{129,1},{2,130},{130,2},{3,131},{131,3},{4... | collective-permute-start | bytes 98312 | tf_op jit(solution)/shard_map/ppermute | solution.py:472

commit v2 on v0

v2 whole, which is shorter than its diff:
```python
import functools

import jax
import jax.numpy as jnp
from jax import lax
from jax.experimental import pallas as pl
from jax.experimental.pallas import tpu as pltpu
from jax.sharding import PartitionSpec as P

BF = jnp.bfloat16
F32 = jnp.float32
VMEM = pl.BlockSpec(memory_space=pltpu.VMEM)


def params(mib=14):
    return pltpu.CompilerParams(vmem_limit_bytes=mib * 1024 * 1024)


def cost(flops, nbytes):
    return pl.CostEstimate(flops=int(flops), bytes_accessed=int(nbytes), transcendentals=0)


def struct(shape, dtype=BF):
    return jax.ShapeDtypeStruct(shape, dtype)


def dot(a, b):
    return jnp.dot(a, b, preferred_element_type=F32)


def lanes_of(shape):
    return lax.broadcasted_iota(jnp.int32, shape, len(shape) - 1)


def swap16():
    row = lax.broadcasted_iota(jnp.int32, (256, 256), 0)
    col = lax.broadcasted_iota(jnp.int32, (256, 256), 1)
    return jnp.where(col == (row % 16) * 16 + row // 16, 1.0, 0.0).astype(BF)


def pack_kernel(x, xt, e_rows, o_rows):
    even = lax.axis_index("row") % 2 == 0
    perm = swap16()
    xt[:, 0:32, :] = jnp.zeros((32, 32, 128), BF)
    xt[:, 288:320, :] = jnp.zeros((32, 32, 128), BF)
    for f in range(8):
        for cb in range(2):
            halves = [
                x[cb * 16 : cb * 16 + 16, f, rb * 16 : rb * 16 + 16, :].reshape(256, 128) for rb in range(2)
            ]
            y = dot(perm, jnp.concatenate(halves, axis=1)).astype(BF)
            at = 32 + 32 * f + 16 * cb
            for rb in range(2):
                xt[rb * 16 : rb * 16 + 16, at : at + 16, :] = y[:, rb * 128 : rb * 128 + 128].reshape(16, 16, 128)
    e_start = jnp.where(even, 29, 0)
    e_rows[...] = xt[pl.ds(e_start, 3), 32:288]
    o_rows[...] = xt[pl.ds(29 - e_start, 3), 32:288]


def pack(sweeps):
    return pl.pallas_call(
        pack_kernel,
        in_specs=[VMEM],
        out_specs=[VMEM] * 3,
        out_shape=[
            struct((32, 320, 128)),
            struct((3, 256, 128)),
            struct((3, 256, 128)),
        ],
        compiler_params=params(),
        cost_estimate=cost(6e9, 4.6e6),
        name="pack",
    )(sweeps)


def taps(kt):
    base = {}
    for d in range(3):
        for b in range(3):
            rows = [kt[a, b, d].astype(F32) for a in range(3)] + [jnp.zeros((32, 64), F32)]
            value = jnp.concatenate(rows, axis=0).T
            base[d, b, 0] = value
            base[d, b, 1] = pltpu.roll(value, 32, 1)
    return base


def fill_w(base, w):
    for d in range(3):
        for fo in range(2):
            for ro in range(2):
                top = d * 256 + fo * 128 + ro * 64
                for ri in range(4):
                    b = ri - ro
                    block = base[d, b, fo].astype(BF) if 0 <= b <= 2 else jnp.zeros((64, 128), BF)
                    w[top : top + 64, ri * 128 : ri * 128 + 128] = block


def column(ref):
    n = ref.shape[1]
    wide = ref[...]
    if n < 128:
        wide = jnp.concatenate([wide, jnp.zeros((1, 128 - n), F32)], axis=1)
    return jnp.broadcast_to(wide, (128, 128)).T[0:n]


def scales_of(fw):
    both = column(fw)
    return jnp.where(lax.axis_index("tm") == 0, both[0:8], both[8:16])


def put_strips(lane, row, tile, left, right):
    here = (lane >= 3 * row) & (lane < 3 * row + 3)
    left = jnp.where(here, pltpu.roll(tile, 3 * row, 1), left)
    right = jnp.where(here, pltpu.roll(tile, 3 * row + 3, 1), right)
    return left, right


def halo_kernel(e_rows, o_rows, out):
    at = pl.ds(pl.multiple_of(224 * (1 - lax.axis_index("tm")), 32), 32)
    out[0:3] = e_rows[:, at, :]
    out[3:6] = o_rows[:, at, :]


def halo(e_rows, o_rows):
    return pl.pallas_call(
        halo_kernel,
        in_specs=[VMEM] * 2,
        out_specs=VMEM,
        out_shape=struct((6, 32, 128)),
        compiler_params=params(),
        cost_estimate=cost(1e10, 1e5),
        name="halo",
    )(e_rows, o_rows)


def strip_pack_kernel(left0, right0, e_rows, o_rows, slab, corner, left, right, e_send, o_send, corner_out, edge):
    lane = lanes_of((16, 128))
    even = lax.axis_index("row") % 2 == 0
    even_col = lax.axis_index("col") % 2 == 0
    e_at = jnp.where(even, 3, 0)
    corner_out[...] = corner[...]
    for k, (source, at) in enumerate(((e_rows, e_at), (o_rows, 3 - e_at))):
        edge[pl.ds(at, 3), 0:256] = source[...]
        edge[pl.ds(at, 3), 256:288] = corner[3 * k : 3 * k + 3]

    def add_edges(at, pair):
        for k in range(6):
            pair = put_strips(lane, k if k < 3 else 32 + k, edge[k, at, :], *pair)
        first, last = pair
        left[at, :] = first
        right[at, :] = last
        e_send[at, :] = jnp.where(even_col, last, first)
        o_send[at, :] = jnp.where(even_col, first, last)

    for s in range(16):
        at = slice(s * 16, s * 16 + 16)
        add_edges(at, (left0[at, :], right0[at, :]))

    for s in range(2):
        at = slice(s * 16, s * 16 + 16)
        pair = jnp.zeros((16, 128), BF), jnp.zeros((16, 128), BF)
        for row in range(32):
            pair = put_strips(lane, row + 3, slab[row, at, :], *pair)
        add_edges(slice(256 + s * 16, 272 + s * 16), pair)


def strip_pack(*args):
    return pl.pallas_call(
        strip_pack_kernel,
        in_specs=[VMEM] * 6,
        out_specs=[VMEM] * 5,
        out_shape=[struct((288, 128))] * 4 + [struct((6, 32, 128))],
        scratch_shapes=[pltpu.VMEM((6, 288, 128), BF)],
        compiler_params=params(),
        cost_estimate=cost(1e8, 1e6),
        name="strip_pack",
    )(*args)


def unit(acc, w, wide_bias, read, scales):
    rows = [read(k) for k in range(6)]
    rhs = jnp.concatenate(
        [jnp.concatenate([rows[ri], rows[ri + 2]], axis=1) for ri in range(4)], axis=0
    )
    y = dot(w[...], rhs)
    acc = list(acc)
    for fo in range(2):
        for half in range(2):
            cols = slice(128 * half, 128 * half + 128)
            part = [y[d * 256 + fo * 128 : d * 256 + fo * 128 + 128, cols] for d in range(3)]
            z = part[1] + pltpu.roll(part[0], 1, 1) + pltpu.roll(part[2], 127, 1) + wide_bias
            acc[half] = acc[half] + jnp.maximum(z, 0.0) * scales[fo]
    return acc


def blank():
    return [jnp.zeros((128, 128), F32) for _ in range(2)]


def store_quad(ref, base, acc):
    for half in range(2):
        for ro in range(2):
            ref[base + 2 * half + ro] = acc[half][ro * 64 : ro * 64 + 64].astype(ref.dtype)


def load_quad(ref, base):
    return [
        jnp.concatenate([ref[base + 2 * half], ref[base + 2 * half + 1]], axis=0) for half in range(2)
    ]


def interior_kernel(quads, xt, kt, b0, fw, *refs):
    if quads[0] == 0:
        out, left, right, slab, w = refs
    else:
        previous, out, w = refs
        for k in range(4 * quads[0]):
            out[k] = previous[k]
    t = lax.axis_index("tm")
    bias = column(b0)
    wide_bias = jnp.concatenate([bias, bias], axis=0)
    scale = scales_of(fw)
    scale = jnp.where(t == 0, scale[0:6], scale[2:8])
    fill_w(taps(kt), w)

    @pl.loop(quads[0], quads[1])
    def _(n):
        base = 4 * n
        acc = blank()
        for k in range(3):
            at = pl.ds(pl.multiple_of(64 * (k + t), 64), 128)
            scales = [scale[2 * k + fo : 2 * k + fo + 1] for fo in range(2)]
            acc = unit(acc, w, wide_bias, lambda r: xt[base + 1 + r, at, :], scales)
        store_quad(out, base, acc)

    if quads[0] == 0:
        lane = lanes_of((16, 128))

        @pl.loop(0, 16)
        def _(s):
            at = pl.ds(pl.multiple_of(s * 16, 16), 16)
            source = pl.ds(pl.multiple_of(s * 16 + 32, 16), 16)
            pair = jnp.zeros((16, 128), BF), jnp.zeros((16, 128), BF)
            for row in range(32):
                pair = put_strips(lane, row + 3, xt[row, source, :], *pair)
            left[at, :], right[at, :] = pair

        slab[...] = xt[:, pl.ds(pl.multiple_of(256 - 224 * t, 32), 32), :]


def interior(quads, xt, kt, b0, fw, *previous):
    out_shape = [struct((4 * quads[1], 64, 128), F32)]
    if not previous:
        out_shape += [struct((256, 128)), struct((256, 128)), struct((32, 32, 128))]
    return pl.pallas_call(
        functools.partial(interior_kernel, quads),
        in_specs=[VMEM] * (4 + len(previous)),
        out_specs=[VMEM] * len(out_shape),
        out_shape=out_shape,
        scratch_shapes=[pltpu.VMEM((768, 512), BF)],
        compiler_params=params(),
        cost_estimate=cost(1e3, 1e3),
        name="interior_%d" % quads[0],
    )(xt, kt, b0, fw, *previous)


def slab_kernel(xt, inner, slab, kt, b0, fw, out, w):
    t = lax.axis_index("tm")
    bias = column(b0)
    wide_bias = jnp.concatenate([bias, bias], axis=0)
    base = {key: jnp.where(t == 1, pltpu.roll(value, 96, 1), value) for key, value in taps(kt).items()}
    fill_w(base, w)
    own_at = pl.ds(pl.multiple_of(192 - 160 * t, 32), 96)
    scale = scales_of(fw)
    scale = jnp.where(t == 0, scale[6:8], scale[0:2])
    scales = [scale[fo : fo + 1] for fo in range(2)]

    @pl.loop(0, 7)
    def _(n):
        base = 4 * n

        def read(r):
            return jnp.concatenate([xt[base + 1 + r, own_at, :], slab[base + 1 + r]], axis=0)

        store_quad(out, base, unit(load_quad(inner, base), w, wide_bias, read, scales))


def slab_pairs(xt, inner, slab, kt, b0, fw):
    return pl.pallas_call(
        slab_kernel,
        in_specs=[VMEM] * 6,
        out_specs=VMEM,
        out_shape=struct((28, 64, 128), F32),
        scratch_shapes=[pltpu.VMEM((768, 512), BF)],
        compiler_params=params(),
        cost_estimate=cost(7 * 768 * 512 * 256 * 2, 3e6),
        name="slab_pairs",
    )(xt, inner, slab, kt, b0, fw)


def edge_kernel(own, xt, inner, e_rows, o_rows, slab, corner, kt, b0, fw, out, edge, w):
    t = lax.axis_index("tm")
    low = t if own else 1 - t
    bias = column(b0)
    wide_bias = jnp.concatenate([bias, bias], axis=0)
    fill_w(taps(kt), w)

    at_slab = pl.ds(pl.multiple_of(288 * (1 - t), 32), 32)
    edge[:, pl.ds(pl.multiple_of(288 * t, 32), 32), :] = jnp.zeros((6, 32, 128), BF)
    edge[pl.ds(3 - 3 * low, 3), 32:288] = xt[pl.ds(29 * low, 3), 32:288]
    edge[pl.ds(3 - 3 * low, 3), at_slab] = slab[pl.ds(29 * low, 3)]
    from_e = (lax.axis_index("row") + low) % 2 == 1

    @pl.when(from_e)
    def _():
        edge[pl.ds(3 * low, 3), 32:288] = e_rows[...]
        edge[pl.ds(3 * low, 3), at_slab] = corner[0:3]

    @pl.when(jnp.logical_not(from_e))
    def _():
        edge[pl.ds(3 * low, 3), 32:288] = o_rows[...]
        edge[pl.ds(3 * low, 3), at_slab] = corner[3:6]

    acc = blank()
    scale = scales_of(fw)
    for g in range(4):
        scales = [scale[2 * g + fo : 2 * g + fo + 1] for fo in range(2)]
        acc = unit(acc, w, wide_bias, lambda r: edge[r, 64 * g : 64 * g + 128, :], scales)
    if own:
        store_quad(out, 0, acc)
    else:
        out[pl.ds(4 - 4 * low, 16)] = inner[pl.ds(12 * low, 16)].astype(BF)
        store_quad(out, 16 * low, acc)


def edge_quad(own, xt, inner, e_rows, o_rows, slab, corner, kt, b0, fw):
    return pl.pallas_call(
        functools.partial(edge_kernel, own),
        in_specs=[VMEM] * 9,
        out_specs=VMEM,
        out_shape=struct((4, 64, 128), F32) if own else struct((20, 64, 128)),
        scratch_shapes=[pltpu.VMEM((6, 320, 128), BF), pltpu.VMEM((768, 512), BF)],
        compiler_params=params(),
        cost_estimate=cost(1e10 if own else 1e6, 2e6),
        name="edge_own" if own else "edge_partner",
    )(xt, inner, e_rows, o_rows, slab, corner, kt, b0, fw)


def strip_temporal_kernel(own_l, own_r, e_col, o_col, kt, b0, fw, out, send, windows, ws):
    t = lax.axis_index("tm")
    even = lax.axis_index("col") % 2 == 0
    lane = lanes_of((16, 128))
    third = lane % 3
    bias = column(b0)
    for (d, b, fo), value in taps(kt).items():
        ws[fo * 64 : fo * 64 + 64, (b * 3 + d) * 128 : (b * 3 + d) * 128 + 128] = value.astype(BF)

    windows[:, pl.ds(pl.multiple_of(288 * t, 32), 32), :] = jnp.zeros((9, 32, 256), BF)

    def fill(s, at):
        src = slice(s * 16, s * 16 + 16)
        dst = pl.ds(at if isinstance(at, int) else pl.multiple_of(at, 16), 16)
        ol, orr, ne, no = own_l[src, :], own_r[src, :], e_col[src, :], o_col[src, :]
        nl, nr = jnp.where(even, no, ne), jnp.where(even, ne, no)
        for b in range(3):
            for d in range(3):
                lo = pltpu.roll(nl, (128 - (3 * b + d)) % 128, 1)
                if d > 0:
                    lo = jnp.where(third < 3 - d, lo, pltpu.roll(ol, (128 - (3 * b + d - 3)) % 128, 1))
                hi = pltpu.roll(nr, (128 - (3 * b + d - 2)) % 128, 1)
                if d < 2:
                    hi = jnp.where(third < 2 - d, pltpu.roll(orr, 128 - (3 * b + d + 1), 1), hi)
                windows[b * 3 + d, dst, 0:128] = lo
                windows[b * 3 + d, dst, 128:256] = hi

    for s in range(18):
        fill(s, 32 + 16 * s if s < 16 else 288 * (1 - t) + (s - 16) * 16)

    wide_bias = jnp.concatenate([bias, bias], axis=1)
    both = scales_of(fw)
    both = jnp.concatenate([both, both], axis=1)
    scale = [both[k : k + 1] for k in range(8)]
    acc = jnp.zeros((64, 256), F32)
    for g in range(4):
        rhs = jnp.concatenate([windows[k, 64 * g : 64 * g + 128, :] for k in range(9)], axis=0)
        y = dot(ws[...], rhs)
        for fo in range(2):
            acc = acc + jnp.maximum(y[fo * 64 : fo * 64 + 64] + wide_bias, 0.0) * scale[2 * g + fo]
    for side in range(2):
        out[side] = acc[:, side * 128 : side * 128 + 128]
        send[side] = acc[:, side * 128 : side * 128 + 128].astype(BF)


def strip_temporal(own_l, own_r, e_col, o_col, kt, b0, fw):
    return pl.pallas_call(
        strip_temporal_kernel,
        in_specs=[VMEM] * 7,
        out_specs=[VMEM] * 2,
        out_shape=[struct((2, 64, 128), F32), struct((2, 64, 128))],
        scratch_shapes=[pltpu.VMEM((9, 320, 256), BF), pltpu.VMEM((128, 1152), BF)],
        compiler_params=params(),
        cost_estimate=cost(1e10, 1e6),
        name="strip_temporal",
    )(own_l, own_r, e_col, o_col, kt, b0, fw)


def spatial_kernel(grid_rows, inner, near, partner, strips, partner_strips, k1, b1, k2, b2, out, own, c3, h3, ms, w2):
    t = lax.axis_index("tm")
    row = lax.axis_index("row")
    col = lax.axis_index("col")
    first_col = col == 0
    last_col = col == lax.axis_size("col") - 1
    top = row * 32 + t * 16
    lane = lanes_of((64, 128))
    depth = lane // 3
    third = lane % 3

    own[pl.ds(4 - 4 * t, 16)] = inner[pl.ds(12 * t, 16)]
    own[pl.ds(16 * t, 4)] = near[...]
    w1 = k1[...].reshape(576, 128).astype(F32).T.astype(BF)
    for k in range(9):
        w2[:, k * 128 : k * 128 + 128] = k2[k // 3, k % 3]

    def in_grid(g):
        return (g >= 0) & (g < grid_rows)

    edges = []
    for side in range(2):
        total = strips[side] + partner_strips[side].astype(F32)
        total = pltpu.roll(total, (128 - 48 * t) % 128, 1)
        off = (third < 2) & first_col if side == 0 else (third > 0) & last_col
        keep = in_grid(top + depth - 2) & jnp.logical_not(off)
        edges.append(jnp.where(keep, total, 0.0).astype(BF))

    for r in range(20):
        value = (own[r] + partner[r].astype(F32)).astype(BF)
        value = jnp.where(lane == 0, pltpu.roll(edges[0], (126 - 3 * r) % 128, 1), value)
        value = jnp.where(lane == 127, pltpu.roll(edges[1], 127 - 3 * r, 1), value)
        value = jnp.where(in_grid(top + r - 2), value, jnp.zeros_like(value))
        c3[r, 0:64] = jnp.where(lane == 0, pltpu.roll(edges[0], 127 - 3 * r, 1), pltpu.roll(value, 1, 1))
        c3[r, 64:128] = value
        c3[r, 128:192] = jnp.where(
            lane == 127, pltpu.roll(edges[1], 126 - 3 * r, 1), pltpu.roll(value, 127, 1)
        )

    bias1 = column(b1)
    bias2 = column(b2)
    wide_b1 = jnp.concatenate([bias1, bias1], axis=1)
    wide_b2 = jnp.concatenate([bias2, bias2], axis=1)

    rhs = jnp.concatenate(
        [
            jnp.concatenate([pltpu.roll(edges[side], (128 - 3 * b - d) % 128, 1) for side in range(2)], axis=1)
            for b in range(3)
            for d in range(3)
        ],
        axis=0,
    )
    y = jnp.maximum(dot(w1, rhs) + wide_b1, 0.0)
    lane2 = lanes_of((128, 128))
    kept = in_grid(top + lane2 // 3 - 1)
    hs_l = jnp.where(kept & jnp.logical_not(first_col), y[:, :128], 0.0).astype(BF)
    hs_r = jnp.where(kept & jnp.logical_not(last_col), y[:, 128:], 0.0).astype(BF)

    for h in range(0, 18, 2):
        rhs = jnp.concatenate(
            [jnp.concatenate([c3[h + b], c3[h + 1 + b]], axis=1) for b in range(3)], axis=0
        )
        y = jnp.maximum(dot(w1, rhs) + wide_b1, 0.0)
        for at in range(h, h + 2):
            value = y[:, (at - h) * 128 : (at - h) * 128 + 128].astype(BF)
            value = jnp.where(in_grid(top + at - 1), value, jnp.zeros_like(value))
            h3[at, 0:128] = jnp.where(
                lane2 == 0, pltpu.roll(hs_l, (128 - 3 * at) % 128, 1), pltpu.roll(value, 1, 1)
            )
            h3[at, 128:256] = value
            h3[at, 256:384] = jnp.where(
                lane2 == 127, pltpu.roll(hs_r, 127 - 3 * at, 1), pltpu.roll(value, 127, 1)
            )

    for r in range(0, 16, 2):
        rhs = jnp.concatenate(
            [jnp.concatenate([h3[r + b], h3[r + 1 + b]], axis=1) for b in range(3)], axis=0
        )
        y = jnp.maximum(dot(w2[...], rhs) + wide_b2, 0.0).astype(BF)
        ms[r] = y[:, :128]
        ms[r + 1] = y[:, 128:]

    perm = swap16()
    for pair in range(4):
        halves = [ms[:, (2 * pair + k) * 16 : (2 * pair + k) * 16 + 16, :].reshape(256, 128) for k in range(2)]
        y = dot(perm, jnp.concatenate(halves, axis=1)).astype(BF)
        for k in range(2):
            q = (2 * pair + k) * 16
            out[q : q + 16] = y[:, k * 128 : k * 128 + 128].reshape(16, 16, 128)


def spatial(grid_rows, *args):
    return pl.pallas_call(
        functools.partial(spatial_kernel, grid_rows),
        in_specs=[VMEM] * 9,
        out_specs=VMEM,
        out_shape=struct((128, 16, 128)),
        scratch_shapes=[
            pltpu.VMEM((20, 64, 128), F32),
            pltpu.VMEM((20, 192, 128), BF),
            pltpu.VMEM((18, 384, 128), BF),
            pltpu.VMEM((16, 128, 128), BF),
            pltpu.VMEM((128, 1152), BF),
        ],
        compiler_params=params(),
        cost_estimate=cost(1.2e9, 3e6),
        name="spatial",
    )(*args)


def swaps(count, odd):
    return [pair for i in range(odd, count - 1, 2) for pair in ((i, i + 1), (i + 1, i))]


def shards(sweeps, kt, b0, fw, k1, b1, k2, b2):
    rows = lax.axis_size("row")
    cols = lax.axis_size("col")
    both = [(0, 1), (1, 0)]
    kt = jnp.transpose(kt, (2, 3, 4, 1, 0))
    k1 = jnp.transpose(k1, (2, 3, 1, 0))
    k2 = jnp.transpose(k2, (2, 3, 0, 1))
    b0, fw, b1, b2 = (value.reshape(1, -1) for value in (b0, fw, b1, b2))

    xt, e_rows, o_rows = pack(sweeps)
    e_rows = lax.ppermute(e_rows, "row", swaps(rows, 0))
    o_rows = lax.ppermute(o_rows, "row", swaps(rows, 1))
    inner, left0, right0, slab = interior((0, 3), xt, kt, b0, fw)
    slab = lax.ppermute(slab, "tm", both)
    (inner,) = interior((3, 7), xt, kt, b0, fw, inner)

    corner = lax.ppermute(halo(e_rows, o_rows), "tm", both)
    inner = slab_pairs(xt, inner, slab, kt, b0, fw)
    left, right, e_col, o_col, corner = strip_pack(left0, right0, e_rows, o_rows, slab, corner)
    e_col = lax.ppermute(e_col, "col", swaps(cols, 0))
    o_col = lax.ppermute(o_col, "col", swaps(cols, 1))

    field = (xt, inner, e_rows, o_rows, slab, corner, kt, b0, fw)
    partner = lax.ppermute(edge_quad(False, *field), "tm", both)
    strips, strips_send = strip_temporal(left, right, e_col, o_col, kt, b0, fw)
    partner_strips = lax.ppermute(strips_send, "tm", both)
    near = edge_quad(True, *field)
    return spatial(rows * 32, inner, near, partner, strips, partner_strips, k1, b1, k2, b2)


def solution(mesh):
    placed = (P(None, "tm", "row", "col"), P(), P(), P(), P(), P(), P(), P())
    return jax.shard_map(
        shards, mesh=mesh, in_specs=placed, out_specs=P(None, ("row", "tm"), "col"), check_vma=False
    )
```

time: 262 us -> 49.6 us (0.19)
  the two profiles are of different devices: /device:TPU:30 before, /device:TPU:11 now
where the time goes in v2:
time: 49.6 us; the launch traced here: 49.5 us
  Pallas kernels  21.3 us (43%)
  starting transfers between devices  19 us (38%)
  waiting for transfers between devices  7.33 us (15%)
  local copies, waits for them, and re-layouts  1.66 us (3%)
    pallas_call x2, Pallas kernels, interior(): pl.pallas_call(functools.partial(interior_kernel, quads), in_specs=[VMEM]...  9.19 us
    ppermute x1, waiting for transfers between devices, shards(): partner_strips = lax.ppermute(strips_send, 'tm', both)  6.03 us
    ppermute x1, starting transfers between devices, shards(): o_rows = lax.ppermute(o_rows, 'row', swaps(rows, 1))  5.99 us
    pallas_call x1, Pallas kernels, slab_pairs(): pl.pallas_call(slab_kernel, in_specs=[VMEM] * 6, out_specs=VMEM, out_shap...  3.41 us
    ppermute x1, starting transfers between devices, shards(): corner = lax.ppermute(halo(e_rows, o_rows), 'tm', both)  3.38 us
    pallas_call x1, Pallas kernels, spatial(): pl.pallas_call(functools.partial(spatial_kernel, grid_rows), in_specs=[VM...  3.37 us
    ppermute x1, starting transfers between devices, shards(): e_rows = lax.ppermute(e_rows, 'row', swaps(rows, 0))  3.07 us
    ppermute x1, starting transfers between devices, shards(): o_col = lax.ppermute(o_col, 'col', swaps(cols, 1))  2.99 us
  transfers between devices with their start and end apart: 8, of which 2 were waited for; matrix products, arithmetic and copies ran while one was open for 0% of the time, Pallas kernels for 34%

profile of v2, /device:TPU:11, one launch (start us, length us, event | category | flops | bytes accessed | tf_op | source)
XLA Modules:
  0.0 49.5 jit_solution(4363347589372084191)
XLA Ops:
  0.0 1.6 %copy-done.3 = bf16[32,8,32,128]{3,2,1,0:T(8,128)(2,1)S(1)} copy-done((bf16[32,8,32,128]{3,2,1,0:T(8,128)(2,1)S(1)}, bf16[32,8,32,128]{3,2,1,0:T(8,128)(2,1)}, u32[]{:S(2)}) %copy-start.3) | copy-done | bytes 2097176
  1.6 0.8 %pack.1 = (bf16[32,320,128]{2,1,0:T(8,128)(2,1)S(1)}, bf16[3,256,128]{2,1,0:T(8,128)(2,1)S(1)}, bf16[3,256,128]{2,1,0:T(8,128)(2,1)S(1)}) custom-call(bf16[32,8,32,128]{3,2,1,0:T(8,128)(2,1)S(1)} %copy-done.3), custom_call_target="tpu_custom_call" | custom-call | flops 6000000000 | bytes 4600000 | tf_op jit(solution)/shard_map/pack/pallas_call | solution.py:61
  2.5 3.1 %collective-permute-start.1 = (bf16[3,256,128]{2,1,0:T(8,128)(2,1)S(1)}, bf16[3,256,128]{2,1,0:T(8,128)(2,1)S(1)}, u32[]{:S(2)}, u32[]{:S(2)}) collective-permute-start(bf16[3,256,128]{2,1,0:T(8,128)(2,1)S(1)} %get-tuple-element.22), channel_id=1, source_target_pairs={{0,8},{8,0},{16,24},{24,16},{32,40},{40,32},{48,56},{56,48},{64,72... | collective-permute-start | bytes 589832 | tf_op jit(solution)/shard_map/ppermute | solution.py:531
  5.5 6.0 %collective-permute-start.2 = (bf16[3,256,128]{2,1,0:T(8,128)(2,1)S(1)}, bf16[3,256,128]{2,1,0:T(8,128)(2,1)S(1)}, u32[]{:S(2)}, u32[]{:S(2)}) collective-permute-start(bf16[3,256,128]{2,1,0:T(8,128)(2,1)S(1)} %get-tuple-element.23), channel_id=1, source_target_pairs={{8,16},{16,8},{24,32},{32,24},{40,48},{48,40},{56,64},{64,56},{72,... | collective-permute-start | bytes 589832 | tf_op jit(solution)/shard_map/ppermute | solution.py:532
  11.6 5.2 %interior_0.1 = (f32[12,64,128]{2,1,0:T(8,128)S(1)}, bf16[256,128]{1,0:T(8,128)(2,1)S(1)}, bf16[256,128]{1,0:T(8,128)(2,1)S(1)}, bf16[32,32,128]{2,1,0:T(8,128)(2,1)S(1)}) custom-call(bf16[32,320,128]{2,1,0:T(8,128)(2,1)S(1)} %get-tuple-element.19.xt, bf16[3,3,3,32,64]{4,3,2,1,0:T(8,128)(2,1)S(1)} %bitcast.7, f32[1,64]{1,0:T(1,128)S(1)} %bitcast.13, ...), custom_call_target="tpu_custom_call" | custom-call | flops 1000 | bytes 1000 | tf_op jit(solution)/shard_map/interior_0/pallas_call | solution.py:255
  16.8 0.8 %collective-permute-start = (bf16[32,32,128]{2,1,0:T(8,128)(2,1)S(1)}, bf16[32,32,128]{2,1,0:T(8,128)(2,1)S(1)}, u32[]{:S(2)}, u32[]{:S(2)}) collective-permute-start(bf16[32,32,128]{2,1,0:T(8,128)(2,1)S(1)} %get-tuple-element.21), channel_id=1, source_target_pairs={{0,128},{128,0},{1,129},{129,1},{2,130},{130,2},{3,131},{131,3},{4... | collective-permute-start | bytes 786440 | tf_op jit(solution)/shard_map/ppermute | solution.py:534
  17.6 1.3 %collective-permute-done.2.o_rows = bf16[3,256,128]{2,1,0:T(8,128)(2,1)S(1)} collective-permute-done((bf16[3,256,128]{2,1,0:T(8,128)(2,1)S(1)}, bf16[3,256,128]{2,1,0:T(8,128)(2,1)S(1)}, u32[]{:S(2)}, u32[]{:S(2)}) %collective-permute-start.2) | collective-permute-done | bytes 196640 | tf_op jit(solution)/shard_map/ppermute | solution.py:532
  18.9 3.4 %collective-permute-start.3 = (bf16[6,32,128]{2,1,0:T(8,128)(2,1)S(1)}, bf16[6,32,128]{2,1,0:T(8,128)(2,1)S(1)}, u32[]{:S(2)}, u32[]{:S(2)}) collective-permute-start(bf16[6,32,128]{2,1,0:T(8,128)(2,1)S(1)} %halo.1), channel_id=1, source_target_pairs={{0,128},{128,0},{1,129},{129,1},{2,130},{130,2},{3,131},{131,3},{4... | collective-permute-start | bytes 147464 | tf_op jit(solution)/shard_map/ppermute | solution.py:537
  22.3 4.0 %interior_3.1.inner = f32[28,64,128]{2,1,0:T(8,128)S(1)} custom-call(bf16[32,320,128]{2,1,0:T(8,128)(2,1)S(1)} %get-tuple-element.19.xt, bf16[3,3,3,32,64]{4,3,2,1,0:T(8,128)(2,1)S(1)} %bitcast.8, f32[1,64]{1,0:T(1,128)S(1)} %bitcast.14, f32[1,16]{1,0:T(1,128)S(1)} %bitcast.20, f32[12,64,128]{2,1,0:T(8,128)S(1)} %get-tuple-element.20.refs_0_), custom_call_target="tpu_custom_call" | custom-call | flops 1000 | bytes 1000 | tf_op jit(solution)/shard_map/interior_3/pallas_call | solution.py:255
  26.3 0.5 strip_pack.1
  26.8 1.0 %collective-permute-start.5 = (bf16[288,128]{1,0:T(8,128)(2,1)S(1)}, bf16[288,128]{1,0:T(8,128)(2,1)S(1)}, u32[]{:S(2)}, u32[]{:S(2)}) collective-permute-start(bf16[288,128]{1,0:T(8,128)(2,1)S(1)} %get-tuple-element.29), channel_id=1, source_target_pairs={{0,1},{1,0},{2,3},{3,2},{4,5},{5,4},{6,7},{7,6},{8,9},{9,8},{10,11... | collective-permute-start | bytes 221192 | tf_op jit(solution)/shard_map/ppermute | solution.py:540
  27.7 3.0 %collective-permute-start.6 = (bf16[288,128]{1,0:T(8,128)(2,1)S(1)}, bf16[288,128]{1,0:T(8,128)(2,1)S(1)}, u32[]{:S(2)}, u32[]{:S(2)}) collective-permute-start(bf16[288,128]{1,0:T(8,128)(2,1)S(1)} %get-tuple-element.30), channel_id=1, source_target_pairs={{1,2},{2,1},{3,4},{4,3},{5,6},{6,5},{9,10},{10,9},{11,12},{12,11},... | collective-permute-start | bytes 221192 | tf_op jit(solution)/shard_map/ppermute | solution.py:541
  30.7 3.4 %slab_pairs.1.inner = f32[28,64,128]{2,1,0:T(8,128)S(1)} custom-call(bf16[32,320,128]{2,1,0:T(8,128)(2,1)S(1)} %get-tuple-element.19.xt, f32[28,64,128]{2,1,0:T(8,128)S(1)} %interior_3.1.inner, bf16[32,32,128]{2,1,0:T(8,128)(2,1)S(1)} %collective-permute-done.slab, bf16[3,3,3,32,64]{4,3,2,1,0:T(8,128)(2,1)S(1)} %bitcast.9, f32[1,64]{1,0:T(1,128)S(1)} %bitcast.15, ...), custom_call_target="tpu_custom_call" | custom-call | flops 1409286144 | bytes 3000000 | tf_op jit(solution)/shard_map/slab_pairs/pallas_call | solution.py:289
  34.2 1.4 %edge_partner.1 = bf16[20,64,128]{2,1,0:T(8,128)(2,1)S(1)} custom-call(bf16[32,320,128]{2,1,0:T(8,128)(2,1)S(1)} %get-tuple-element.19.xt, f32[28,64,128]{2,1,0:T(8,128)S(1)} %slab_pairs.1.inner, bf16[3,256,128]{2,1,0:T(8,128)(2,1)S(1)} %collective-permute-done.1.e_rows, bf16[3,256,128]{2,1,0:T(8,128)(2,1)S(1)} %collective-permute-done.2.o_rows, ...), custom_call_target="tpu_custom_call" | custom-call | flops 1000000 | bytes 2000000 | tf_op jit(solution)/shard_map/edge_partner/pallas_call | solution.py:337
  35.5 1.7 %collective-permute-start.4 = (bf16[20,64,128]{2,1,0:T(8,128)(2,1)S(1)}, bf16[20,64,128]{2,1,0:T(8,128)(2,1)S(1)}, u32[]{:S(2)}, u32[]{:S(2)}) collective-permute-start(bf16[20,64,128]{2,1,0:T(8,128)(2,1)S(1)} %edge_partner.1), channel_id=1, source_target_pairs={{0,128},{128,0},{1,129},{129,1},{2,130},{130,2},{3,131},{131,3},{4... | collective-permute-start | bytes 983048 | tf_op jit(solution)/shard_map/ppermute | solution.py:544
  37.2 1.1 %strip_temporal.1 = (f32[2,64,128]{2,1,0:T(8,128)S(1)}, bf16[2,64,128]{2,1,0:T(8,128)(2,1)S(1)}) custom-call(bf16[288,128]{1,0:T(8,128)(2,1)S(1)} %get-tuple-element.27.own_l, bf16[288,128]{1,0:T(8,128)(2,1)S(1)} %get-tuple-element.28.own_r, bf16[288,128]{1,0:T(8,128)(2,1)S(1)} %collective-permute-done.5.e_col, ...), custom_call_target="tpu_custom_call" | custom-call | flops 10000000000 | bytes 1000000 | tf_op jit(solution)/shard_map/strip_temporal/pallas_call | solution.py:395
  38.3 0.0 copy-start.4
  38.3 0.0 copy-start.5
  38.3 0.0 copy-start.6
  38.3 0.0 copy-start.7
  38.4 0.1 collective-permute-start.7
  38.5 1.5 %edge_own.1.near = f32[4,64,128]{2,1,0:T(8,128)S(1)} custom-call(bf16[32,320,128]{2,1,0:T(8,128)(2,1)S(1)} %get-tuple-element.19.xt, f32[28,64,128]{2,1,0:T(8,128)S(1)} %slab_pairs.1.inner, bf16[3,256,128]{2,1,0:T(8,128)(2,1)S(1)} %collective-permute-done.1.e_rows, bf16[3,256,128]{2,1,0:T(8,128)(2,1)S(1)} %collective-permute-done.2.o_rows, ...), custom_call_target="tpu_custom_call" | custom-call | flops 10000000000 | bytes 2000000 | tf_op jit(solution)/shard_map/edge_own/pallas_call | solution.py:337
  40.0 6.0 %collective-permute-done.7.partner_strips = bf16[2,64,128]{2,1,0:T(8,128)(2,1)S(1)} collective-permute-done((bf16[2,64,128]{2,1,0:T(8,128)(2,1)S(1)}, bf16[2,64,128]{2,1,0:T(8,128)(2,1)S(1)}, u32[]{:S(2)}, u32[]{:S(2)}) %collective-permute-start.7) | collective-permute-done | bytes 32800 | tf_op jit(solution)/shard_map/ppermute | solution.py:546
  46.1 3.4 %spatial.1 = bf16[128,16,128]{2,1,0:T(8,128)(2,1)} custom-call(f32[28,64,128]{2,1,0:T(8,128)S(1)} %slab_pairs.1.inner, f32[4,64,128]{2,1,0:T(8,128)S(1)} %edge_own.1.near, bf16[20,64,128]{2,1,0:T(8,128)(2,1)S(1)} %collective-permute-done.4.partner, f32[2,64,128]{2,1,0:T(8,128)S(1)} %get-tuple-element.31.strips, ...), custom_call_target="tpu_custom_call" | custom-call | flops 1200000000 | bytes 3000000 | tf_op jit(solution)/shard_map/spatial/pallas_call | solution.py:499
  (18 shorter events, 0.0 us)
Async XLA Ops:
  0.0 11.5 %copy-start = (bf16[64,32,3,3,3]{0,1,4,3,2:T(8,128)(2,1)S(1)}, bf16[64,32,3,3,3]{0,1,4,3,2:T(8,128)(2,1)}, u32[]{:S(2)}) copy-start(bf16[64,32,3,3,3]{0,1,4,3,2:T(8,128)(2,1)} %param.9) | copy-start | bytes 331780
  0.0 11.5 %copy-start.1 = (f32[64]{0:T(128)S(1)}, f32[64]{0:T(128)}, u32[]{:S(2)}) copy-start(f32[64]{0:T(128)} %param.10) | copy-start | bytes 772
  0.0 11.5 %copy-start.2 = (f32[16]{0:T(128)S(1)}, f32[16]{0:T(128)}, u32[]{:S(2)}) copy-start(f32[16]{0:T(128)} %param.11) | copy-start | bytes 196
  0.0 1.6 %copy-start.3 = (bf16[32,8,32,128]{3,2,1,0:T(8,128)(2,1)S(1)}, bf16[32,8,32,128]{3,2,1,0:T(8,128)(2,1)}, u32[]{:S(2)}) copy-start(bf16[32,8,32,128]{3,2,1,0:T(8,128)(2,1)} %x.1) | copy-start | bytes 6291460
  2.5 15.2 %collective-permute-start.1 = (bf16[3,256,128]{2,1,0:T(8,128)(2,1)S(1)}, bf16[3,256,128]{2,1,0:T(8,128)(2,1)S(1)}, u32[]{:S(2)}, u32[]{:S(2)}) collective-permute-start(bf16[3,256,128]{2,1,0:T(8,128)(2,1)S(1)} %get-tuple-element.22), channel_id=1, source_target_pairs={{0,8},{8,0},{16,24},{24,16},{32,40},{40,32},{48,56},{56,48},{64,72... | collective-permute-start | bytes 589832 | tf_op jit(solution)/shard_map/ppermute | solution.py:531
  5.5 13.4 %collective-permute-start.2 = (bf16[3,256,128]{2,1,0:T(8,128)(2,1)S(1)}, bf16[3,256,128]{2,1,0:T(8,128)(2,1)S(1)}, u32[]{:S(2)}, u32[]{:S(2)}) collective-permute-start(bf16[3,256,128]{2,1,0:T(8,128)(2,1)S(1)} %get-tuple-element.23), channel_id=1, source_target_pairs={{8,16},{16,8},{24,32},{32,24},{40,48},{48,40},{56,64},{64,56},{72,... | collective-permute-start | bytes 589832 | tf_op jit(solution)/shard_map/ppermute | solution.py:532
  16.8 9.5 %collective-permute-start = (bf16[32,32,128]{2,1,0:T(8,128)(2,1)S(1)}, bf16[32,32,128]{2,1,0:T(8,128)(2,1)S(1)}, u32[]{:S(2)}, u32[]{:S(2)}) collective-permute-start(bf16[32,32,128]{2,1,0:T(8,128)(2,1)S(1)} %get-tuple-element.21), channel_id=1, source_target_pairs={{0,128},{128,0},{1,129},{129,1},{2,130},{130,2},{3,131},{131,3},{4... | collective-permute-start | bytes 786440 | tf_op jit(solution)/shard_map/ppermute | solution.py:534
  18.9 7.3 %collective-permute-start.3 = (bf16[6,32,128]{2,1,0:T(8,128)(2,1)S(1)}, bf16[6,32,128]{2,1,0:T(8,128)(2,1)S(1)}, u32[]{:S(2)}, u32[]{:S(2)}) collective-permute-start(bf16[6,32,128]{2,1,0:T(8,128)(2,1)S(1)} %halo.1), channel_id=1, source_target_pairs={{0,128},{128,0},{1,129},{129,1},{2,130},{130,2},{3,131},{131,3},{4... | collective-permute-start | bytes 147464 | tf_op jit(solution)/shard_map/ppermute | solution.py:537
  26.8 10.4 %collective-permute-start.5 = (bf16[288,128]{1,0:T(8,128)(2,1)S(1)}, bf16[288,128]{1,0:T(8,128)(2,1)S(1)}, u32[]{:S(2)}, u32[]{:S(2)}) collective-permute-start(bf16[288,128]{1,0:T(8,128)(2,1)S(1)} %get-tuple-element.29), channel_id=1, source_target_pairs={{0,1},{1,0},{2,3},{3,2},{4,5},{5,4},{6,7},{7,6},{8,9},{9,8},{10,11... | collective-permute-start | bytes 221192 | tf_op jit(solution)/shard_map/ppermute | solution.py:540
  27.7 9.5 %collective-permute-start.6 = (bf16[288,128]{1,0:T(8,128)(2,1)S(1)}, bf16[288,128]{1,0:T(8,128)(2,1)S(1)}, u32[]{:S(2)}, u32[]{:S(2)}) collective-permute-start(bf16[288,128]{1,0:T(8,128)(2,1)S(1)} %get-tuple-element.30), channel_id=1, source_target_pairs={{1,2},{2,1},{3,4},{4,3},{5,6},{6,5},{9,10},{10,9},{11,12},{12,11},... | collective-permute-start | bytes 221192 | tf_op jit(solution)/shard_map/ppermute | solution.py:541
  35.5 10.5 %collective-permute-start.4 = (bf16[20,64,128]{2,1,0:T(8,128)(2,1)S(1)}, bf16[20,64,128]{2,1,0:T(8,128)(2,1)S(1)}, u32[]{:S(2)}, u32[]{:S(2)}) collective-permute-start(bf16[20,64,128]{2,1,0:T(8,128)(2,1)S(1)} %edge_partner.1), channel_id=1, source_target_pairs={{0,128},{128,0},{1,129},{129,1},{2,130},{130,2},{3,131},{131,3},{4... | collective-permute-start | bytes 983048 | tf_op jit(solution)/shard_map/ppermute | solution.py:544
  38.3 7.8 %copy-start.4 = (bf16[128,128,3,3]{1,0,3,2:T(8,128)(2,1)S(1)}, bf16[128,128,3,3]{1,0,3,2:T(8,128)(2,1)}, u32[]{:S(2)}) copy-start(bf16[128,128,3,3]{1,0,3,2:T(8,128)(2,1)} %param.14) | copy-start | bytes 884740
  38.3 7.7 %copy-start.5 = (bf16[128,64,3,3]{0,1,3,2:T(8,128)(2,1)S(1)}, bf16[128,64,3,3]{0,1,3,2:T(8,128)(2,1)}, u32[]{:S(2)}) copy-start(bf16[128,64,3,3]{0,1,3,2:T(8,128)(2,1)} %param.12) | copy-start | bytes 442372
  38.3 7.7 %copy-start.6 = (f32[128]{0:T(128)S(1)}, f32[128]{0:T(128)}, u32[]{:S(2)}) copy-start(f32[128]{0:T(128)} %param.13) | copy-start | bytes 1540
  38.3 7.7 %copy-start.7 = (f32[128]{0:T(128)S(1)}, f32[128]{0:T(128)}, u32[]{:S(2)}) copy-start(f32[128]{0:T(128)} %param.15) | copy-start | bytes 1540
  38.4 7.7 %collective-permute-start.7 = (bf16[2,64,128]{2,1,0:T(8,128)(2,1)S(1)}, bf16[2,64,128]{2,1,0:T(8,128)(2,1)S(1)}, u32[]{:S(2)}, u32[]{:S(2)}) collective-permute-start(bf16[2,64,128]{2,1,0:T(8,128)(2,1)S(1)} %get-tuple-element.32), channel_id=1, source_target_pairs={{0,128},{128,0},{1,129},{129,1},{2,130},{130,2},{3,131},{131,3},{4... | collective-permute-start | bytes 98312 | tf_op jit(solution)/shard_map/ppermute | solution.py:546

commit v3 on v2

--- a/solution.py
+++ b/solution.py
@@ -9,6 +9,7 @@
 
 BF = jnp.bfloat16
 F32 = jnp.float32
+ANY = pl.BlockSpec(memory_space=pl.ANY)
 VMEM = pl.BlockSpec(memory_space=pltpu.VMEM)
 
 
@@ -109,36 +110,51 @@
 
 
 def put_strips(lane, row, tile, left, right):
-    here = (lane >= 3 * row) & (lane < 3 * row + 3)
-    left = jnp.where(here, pltpu.roll(tile, 3 * row, 1), left)
-    right = jnp.where(here, pltpu.roll(tile, 3 * row + 3, 1), right)
+    turned = pltpu.roll(tile, 3 * row + 3, 1)
+    left = jnp.where((lane >= 3 * row + 3) & (lane < 3 * row + 6), turned, left)
+    right = jnp.where((lane >= 3 * row) & (lane < 3 * row + 3), turned, right)
     return left, right
 
 
-def halo_kernel(e_rows, o_rows, out):
+def slab_kernel(xt, slab):
+    slab[...] = xt[:, pl.ds(pl.multiple_of(256 - 224 * lax.axis_index("tm"), 32), 32), :]
+
+
+def slab_of(xt):
+    return pl.pallas_call(
+        slab_kernel,
+        in_specs=[VMEM],
+        out_specs=VMEM,
+        out_shape=struct((32, 32, 128)),
+        compiler_params=params(),
+        cost_estimate=cost(1e3, 1e3),
+        name="slab",
+    )(xt)
+
+
+def halo_kernel(e_rows, o_rows, after, out):
     at = pl.ds(pl.multiple_of(224 * (1 - lax.axis_index("tm")), 32), 32)
     out[0:3] = e_rows[:, at, :]
     out[3:6] = o_rows[:, at, :]
 
 
-def halo(e_rows, o_rows):
+def halo(e_rows, o_rows, after):
     return pl.pallas_call(
         halo_kernel,
-        in_specs=[VMEM] * 2,
+        in_specs=[VMEM, VMEM, ANY],
         out_specs=VMEM,
         out_shape=struct((6, 32, 128)),
         compiler_params=params(),
         cost_estimate=cost(1e10, 1e5),
         name="halo",
-    )(e_rows, o_rows)
-
-
-def strip_pack_kernel(left0, right0, e_rows, o_rows, slab, corner, left, right, e_send, o_send, corner_out, edge):
+    )(e_rows, o_rows, after)
+
+
+def strip_pack_kernel(left0, right0, e_rows, o_rows, slab, corner, after, left, right, e_send, o_send, edge):
     lane = lanes_of((16, 128))
     even = lax.axis_index("row") % 2 == 0
     even_col = lax.axis_index("col") % 2 == 0
     e_at = jnp.where(even, 3, 0)
-    corner_out[...] = corner[...]
     for k, (source, at) in enumerate(((e_rows, e_at), (o_rows, 3 - e_at))):
         edge[pl.ds(at, 3), 0:256] = source[...]
         edge[pl.ds(at, 3), 256:288] = corner[3 * k : 3 * k + 3]
@@ -146,7 +162,7 @@
     def add_edges(at, pair):
         for k in range(6):
             pair = put_strips(lane, k if k < 3 else 32 + k, edge[k, at, :], *pair)
-        first, last = pair
+        first, last = pltpu.roll(pair[0], 125, 1), pair[1]
         left[at, :] = first
         right[at, :] = last
         e_send[at, :] = jnp.where(even_col, last, first)
@@ -167,9 +183,9 @@
 def strip_pack(*args):
     return pl.pallas_call(
         strip_pack_kernel,
-        in_specs=[VMEM] * 6,
-        out_specs=[VMEM] * 5,
-        out_shape=[struct((288, 128))] * 4 + [struct((6, 32, 128))],
+        in_specs=[VMEM] * 6 + [ANY],
+        out_specs=[VMEM] * 4,
+        out_shape=[struct((288, 128))] * 4,
         scratch_shapes=[pltpu.VMEM((6, 288, 128), BF)],
         compiler_params=params(),
         cost_estimate=cost(1e8, 1e6),
@@ -209,13 +225,7 @@
     ]
 
 
-def interior_kernel(quads, xt, kt, b0, fw, *refs):
-    if quads[0] == 0:
-        out, left, right, slab, w = refs
-    else:
-        previous, out, w = refs
-        for k in range(4 * quads[0]):
-            out[k] = previous[k]
+def interior_kernel(xt, kt, b0, fw, out, left, right, w):
     t = lax.axis_index("tm")
     bias = column(b0)
     wide_bias = jnp.concatenate([bias, bias], axis=0)
@@ -223,8 +233,7 @@
     scale = jnp.where(t == 0, scale[0:6], scale[2:8])
     fill_w(taps(kt), w)
 
-    @pl.loop(quads[0], quads[1])
-    def _(n):
+    for n in range(7):
         base = 4 * n
         acc = blank()
         for k in range(3):
@@ -233,117 +242,132 @@
             acc = unit(acc, w, wide_bias, lambda r: xt[base + 1 + r, at, :], scales)
         store_quad(out, base, acc)
 
-    if quads[0] == 0:
-        lane = lanes_of((16, 128))
-
-        @pl.loop(0, 16)
-        def _(s):
-            at = pl.ds(pl.multiple_of(s * 16, 16), 16)
-            source = pl.ds(pl.multiple_of(s * 16 + 32, 16), 16)
-            pair = jnp.zeros((16, 128), BF), jnp.zeros((16, 128), BF)
-            for row in range(32):
-                pair = put_strips(lane, row + 3, xt[row, source, :], *pair)
-            left[at, :], right[at, :] = pair
-
-        slab[...] = xt[:, pl.ds(pl.multiple_of(256 - 224 * t, 32), 32), :]
-
-
-def interior(quads, xt, kt, b0, fw, *previous):
-    out_shape = [struct((4 * quads[1], 64, 128), F32)]
-    if not previous:
-        out_shape += [struct((256, 128)), struct((256, 128)), struct((32, 32, 128))]
-    return pl.pallas_call(
-        functools.partial(interior_kernel, quads),
-        in_specs=[VMEM] * (4 + len(previous)),
-        out_specs=[VMEM] * len(out_shape),
-        out_shape=out_shape,
+    lane = lanes_of((16, 128))
+
+    @pl.loop(0, 16)
+    def _(s):
+        at = pl.ds(pl.multiple_of(s * 16, 16), 16)
+        source = pl.ds(pl.multiple_of(s * 16 + 32, 16), 16)
+        pair = jnp.zeros((16, 128), BF), jnp.zeros((16, 128), BF)
+        for row in range(32):
+            pair = put_strips(lane, row + 3, xt[row, source, :], *pair)
+        left[at, :], right[at, :] = pair
+
+
+def interior(xt, kt, b0, fw):
+    return pl.pallas_call(
+        interior_kernel,
+        in_specs=[VMEM] * 4,
+        out_specs=[VMEM] * 3,
+        out_shape=[struct((28, 64, 128), F32), struct((256, 128)), struct((256, 128))],
         scratch_shapes=[pltpu.VMEM((768, 512), BF)],
         compiler_params=params(),
         cost_estimate=cost(1e3, 1e3),
-        name="interior_%d" % quads[0],
-    )(xt, kt, b0, fw, *previous)
-
-
-def slab_kernel(xt, inner, slab, kt, b0, fw, out, w):
+        name="interior",
+    )(xt, kt, b0, fw)
+
+
+def edges_kernel(xt, e_rows, o_rows, after, kt, b0, fw, out, edge, w):
     t = lax.axis_index("tm")
     bias = column(b0)
     wide_bias = jnp.concatenate([bias, bias], axis=0)
-    base = {key: jnp.where(t == 1, pltpu.roll(value, 96, 1), value) for key, value in taps(kt).items()}
-    fill_w(base, w)
+    scale = scales_of(fw)
+    scale = jnp.where(t == 0, scale[0:6], scale[2:8])
+    fill_w(taps(kt), w)
+    even = lax.axis_index("row") % 2 == 0
+    for low in range(2):
+        edge[low, :, 0:32] = jnp.zeros((6, 32, 128), BF)
+        edge[low, :, 288:320] = jnp.zeros((6, 32, 128), BF)
+        edge[low, 3 - 3 * low : 6 - 3 * low, 32:288] = xt[29 * low : 29 * low + 3, 32:288]
+        first, second = (o_rows, e_rows) if low == 0 else (e_rows, o_rows)
+        edge[low, 3 * low : 3 * low + 3, 32:288] = jnp.where(even, first[...], second[...])
+    for low in range(2):
+        acc = blank()
+        for k in range(3):
+            at = pl.ds(pl.multiple_of(64 * (k + t), 64), 128)
+            scales = [scale[2 * k + fo : 2 * k + fo + 1] for fo in range(2)]
+            acc = unit(acc, w, wide_bias, lambda r: edge[low, r, at, :], scales)
+        store_quad(out, 4 * low, acc)
+
+
+def edge_quads(xt, e_rows, o_rows, after, kt, b0, fw):
+    return pl.pallas_call(
+        edges_kernel,
+        in_specs=[VMEM] * 3 + [ANY] + [VMEM] * 3,
+        out_specs=VMEM,
+        out_shape=struct((8, 64, 128), F32),
+        scratch_shapes=[pltpu.VMEM((2, 6, 320, 128), BF), pltpu.VMEM((768, 512), BF)],
+        compiler_params=params(),
+        cost_estimate=cost(6 * 768 * 512 * 256 * 2, 2e6),
+        name="edge_quads",
+    )(xt, e_rows, o_rows, after, kt, b0, fw)
+
+
+def rest_kernel(own, xt, inner, slab, kt, b0, fw, *refs):
+    if own:
+        outer, e_rows, o_rows, corner, out, far, edge, w = refs
+        quads = 3
+    else:
+        out, mid, w = refs
+        quads = 4
+    t = lax.axis_index("tm")
+    start = 16 * t if own else 12 * (1 - t)
+    bias = column(b0)
+    wide_bias = jnp.concatenate([bias, bias], axis=0)
+    fill_w({key: jnp.where(t == 1, pltpu.roll(value, 96, 1), value) for key, value in taps(kt).items()}, w)
     own_at = pl.ds(pl.multiple_of(192 - 160 * t, 32), 96)
     scale = scales_of(fw)
     scale = jnp.where(t == 0, scale[6:8], scale[0:2])
     scales = [scale[fo : fo + 1] for fo in range(2)]
 
-    @pl.loop(0, 7)
-    def _(n):
-        base = 4 * n
+    for i in range(quads):
+        at = start + 4 * i
 
         def read(r):
-            return jnp.concatenate([xt[base + 1 + r, own_at, :], slab[base + 1 + r]], axis=0)
-
-        store_quad(out, base, unit(load_quad(inner, base), w, wide_bias, read, scales))
-
-
-def slab_pairs(xt, inner, slab, kt, b0, fw):
-    return pl.pallas_call(
-        slab_kernel,
-        in_specs=[VMEM] * 6,
-        out_specs=VMEM,
-        out_shape=struct((28, 64, 128), F32),
-        scratch_shapes=[pltpu.VMEM((768, 512), BF)],
-        compiler_params=params(),
-        cost_estimate=cost(7 * 768 * 512 * 256 * 2, 3e6),
-        name="slab_pairs",
-    )(xt, inner, slab, kt, b0, fw)
-
-
-def edge_kernel(own, xt, inner, e_rows, o_rows, slab, corner, kt, b0, fw, out, edge, w):
-    t = lax.axis_index("tm")
-    low = t if own else 1 - t
-    bias = column(b0)
-    wide_bias = jnp.concatenate([bias, bias], axis=0)
-    fill_w(taps(kt), w)
-
-    at_slab = pl.ds(pl.multiple_of(288 * (1 - t), 32), 32)
-    edge[:, pl.ds(pl.multiple_of(288 * t, 32), 32), :] = jnp.zeros((6, 32, 128), BF)
-    edge[pl.ds(3 - 3 * low, 3), 32:288] = xt[pl.ds(29 * low, 3), 32:288]
-    edge[pl.ds(3 - 3 * low, 3), at_slab] = slab[pl.ds(29 * low, 3)]
-    from_e = (lax.axis_index("row") + low) % 2 == 1
-
-    @pl.when(from_e)
-    def _():
-        edge[pl.ds(3 * low, 3), 32:288] = e_rows[...]
-        edge[pl.ds(3 * low, 3), at_slab] = corner[0:3]
-
-    @pl.when(jnp.logical_not(from_e))
-    def _():
-        edge[pl.ds(3 * low, 3), 32:288] = o_rows[...]
-        edge[pl.ds(3 * low, 3), at_slab] = corner[3:6]
-
-    acc = blank()
-    scale = scales_of(fw)
-    for g in range(4):
-        scales = [scale[2 * g + fo : 2 * g + fo + 1] for fo in range(2)]
-        acc = unit(acc, w, wide_bias, lambda r: edge[r, 64 * g : 64 * g + 128, :], scales)
+            return jnp.concatenate([xt[at + 1 + r, own_at, :], slab[at + 1 + r]], axis=0)
+
+        acc = unit(load_quad(inner, at), w, wide_bias, read, scales)
+        store_quad(out, 4 * i + 4 * (1 - t) if own else 4 * i, acc)
+        if not own and i in (0, 3):
+
+            @pl.when(t == i // 3)
+            def _():
+                store_quad(mid, 0, acc)
+
     if own:
-        store_quad(out, 0, acc)
+        halo_at = pl.ds(pl.multiple_of(160 - 160 * t, 32), 96)
+        for far_edge in range(2):
+            low = 1 - t if far_edge else t
+            from_e = (lax.axis_index("row") + low) % 2 == 1
+            rows = edge.at[far_edge]
+            rows[pl.ds(3 - 3 * low, 3), 0:96] = xt[pl.ds(29 * low, 3), own_at]
+            rows[pl.ds(3 - 3 * low, 3), 96:128] = slab[pl.ds(29 * low, 3)]
+            rows[pl.ds(3 * low, 3), 0:96] = jnp.where(from_e, e_rows[:, halo_at, :], o_rows[:, halo_at, :])
+            rows[pl.ds(3 * low, 3), 96:128] = jnp.where(from_e, corner[0:3], corner[3:6])
+            acc = unit(load_quad(outer, 4 * low), w, wide_bias, lambda r: rows[r], scales)
+            if far_edge:
+                store_quad(far, 0, acc)
+            else:
+                store_quad(out, 12 * t, acc)
+
+
+def rest(own, *args):
+    scratch = [pltpu.VMEM((768, 512), BF)]
+    if own:
+        out_shape = [struct((16, 64, 128), F32), struct((4, 64, 128))]
+        scratch = [pltpu.VMEM((2, 6, 128, 128), BF)] + scratch
     else:
-        out[pl.ds(4 - 4 * low, 16)] = inner[pl.ds(12 * low, 16)].astype(BF)
-        store_quad(out, 16 * low, acc)
-
-
-def edge_quad(own, xt, inner, e_rows, o_rows, slab, corner, kt, b0, fw):
-    return pl.pallas_call(
-        functools.partial(edge_kernel, own),
-        in_specs=[VMEM] * 9,
-        out_specs=VMEM,
-        out_shape=struct((4, 64, 128), F32) if own else struct((20, 64, 128)),
-        scratch_shapes=[pltpu.VMEM((6, 320, 128), BF), pltpu.VMEM((768, 512), BF)],
-        compiler_params=params(),
-        cost_estimate=cost(1e10 if own else 1e6, 2e6),
-        name="edge_own" if own else "edge_partner",
-    )(xt, inner, e_rows, o_rows, slab, corner, kt, b0, fw)
+        out_shape = [struct((16, 64, 128)), struct((4, 64, 128), F32)]
+    return pl.pallas_call(
+        functools.partial(rest_kernel, own),
+        in_specs=[VMEM] * len(args),
+        out_specs=[VMEM] * len(out_shape),
+        out_shape=out_shape,
+        scratch_shapes=scratch,
+        compiler_params=params(),
+        cost_estimate=cost(1e6, 1e6),
+        name="rest_own" if own else "rest_partner",
+    )(*args)
 
 
 def strip_temporal_kernel(own_l, own_r, e_col, o_col, kt, b0, fw, out, send, windows, ws):
@@ -391,7 +415,27 @@
         send[side] = acc[:, side * 128 : side * 128 + 128].astype(BF)
 
 
-def strip_temporal(own_l, own_r, e_col, o_col, kt, b0, fw):
+def spatial_weights_kernel(k1, b1, k2, b2, after, w1, w2, c1, c2):
+    w1[...] = k1[...].reshape(576, 128).astype(F32).T.astype(BF)
+    for k in range(9):
+        w2[:, k * 128 : k * 128 + 128] = k2[k // 3, k % 3]
+    c1[...] = column(b1)
+    c2[...] = column(b2)
+
+
+def spatial_weights(*args):
+    return pl.pallas_call(
+        spatial_weights_kernel,
+        in_specs=[VMEM] * 4 + [ANY],
+        out_specs=[VMEM] * 4,
+        out_shape=[struct((128, 576)), struct((128, 1152)), struct((128, 128), F32), struct((128, 128), F32)],
+        compiler_params=params(),
+        cost_estimate=cost(1e3, 1e3),
+        name="spatial_weights",
+    )(*args)
+
+
+def strip_temporal(*args):
     return pl.pallas_call(
         strip_temporal_kernel,
         in_specs=[VMEM] * 7,
@@ -399,12 +443,12 @@
         out_shape=[struct((2, 64, 128), F32), struct((2, 64, 128))],
         scratch_shapes=[pltpu.VMEM((9, 320, 256), BF), pltpu.VMEM((128, 1152), BF)],
         compiler_params=params(),
-        cost_estimate=cost(1e10, 1e6),
+        cost_estimate=cost(1e6, 1e6),
         name="strip_temporal",
-    )(own_l, own_r, e_col, o_col, kt, b0, fw)
-
-
-def spatial_kernel(grid_rows, inner, near, partner, strips, partner_strips, k1, b1, k2, b2, out, own, c3, h3, ms, w2):
+    )(*args)
+
+
+def spatial_kernel(grid_rows, main, mid, partner, strips, partner_far, partner_strips, w1_ref, w2, c1, c2, out, own, theirs, c3, h3, ms):
     t = lax.axis_index("tm")
     row = lax.axis_index("row")
     col = lax.axis_index("col")
@@ -415,11 +459,11 @@
     depth = lane // 3
     third = lane % 3
 
-    own[pl.ds(4 - 4 * t, 16)] = inner[pl.ds(12 * t, 16)]
-    own[pl.ds(16 * t, 4)] = near[...]
-    w1 = k1[...].reshape(576, 128).astype(F32).T.astype(BF)
-    for k in range(9):
-        w2[:, k * 128 : k * 128 + 128] = k2[k // 3, k % 3]
+    own[pl.ds(4 * t, 16)] = main[...]
+    own[pl.ds(16 - 16 * t, 4)] = mid[...]
+    theirs[pl.ds(4 - 4 * t, 16)] = partner[...]
+    theirs[pl.ds(16 * t, 4)] = partner_far[...]
+    w1 = w1_ref[...]
 
     def in_grid(g):
         return (g >= 0) & (g < grid_rows)
@@ -433,7 +477,7 @@
         edges.append(jnp.where(keep, total, 0.0).astype(BF))
 
     for r in range(20):
-        value = (own[r] + partner[r].astype(F32)).astype(BF)
+        value = (own[r] + theirs[r].astype(F32)).astype(BF)
         value = jnp.where(lane == 0, pltpu.roll(edges[0], (126 - 3 * r) % 128, 1), value)
         value = jnp.where(lane == 127, pltpu.roll(edges[1], 127 - 3 * r, 1), value)
         value = jnp.where(in_grid(top + r - 2), value, jnp.zeros_like(value))
@@ -443,8 +487,7 @@
             lane == 127, pltpu.roll(edges[1], 126 - 3 * r, 1), pltpu.roll(value, 127, 1)
         )
 
-    bias1 = column(b1)
-    bias2 = column(b2)
+    bias1, bias2 = c1[...], c2[...]
     wide_b1 = jnp.concatenate([bias1, bias1], axis=1)
     wide_b2 = jnp.concatenate([bias2, bias2], axis=1)
 
@@ -498,15 +541,15 @@
 def spatial(grid_rows, *args):
     return pl.pallas_call(
         functools.partial(spatial_kernel, grid_rows),
-        in_specs=[VMEM] * 9,
+        in_specs=[VMEM] * 10,
         out_specs=VMEM,
         out_shape=struct((128, 16, 128)),
         scratch_shapes=[
             pltpu.VMEM((20, 64, 128), F32),
+            pltpu.VMEM((20, 64, 128), BF),
             pltpu.VMEM((20, 192, 128), BF),
             pltpu.VMEM((18, 384, 128), BF),
             pltpu.VMEM((16, 128, 128), BF),
-            pltpu.VMEM((128, 1152), BF),
         ],
         compiler_params=params(),
         cost_estimate=cost(1.2e9, 3e6),
@@ -530,22 +573,24 @@
     xt, e_rows, o_rows = pack(sweeps)
     e_rows = lax.ppermute(e_rows, "row", swaps(rows, 0))
     o_rows = lax.ppermute(o_rows, "row", swaps(rows, 1))
-    inner, left0, right0, slab = interior((0, 3), xt, kt, b0, fw)
-    slab = lax.ppermute(slab, "tm", both)
-    (inner,) = interior((3, 7), xt, kt, b0, fw, inner)
-
-    corner = lax.ppermute(halo(e_rows, o_rows), "tm", both)
-    inner = slab_pairs(xt, inner, slab, kt, b0, fw)
-    left, right, e_col, o_col, corner = strip_pack(left0, right0, e_rows, o_rows, slab, corner)
+    slab = lax.ppermute(slab_of(xt), "tm", both)
+    inner, left0, right0 = interior(xt, kt, b0, fw)
+    field = (xt, inner, slab, kt, b0, fw)
+    for_partner, mid = rest(False, *field)
+    partner = lax.ppermute(for_partner, "tm", both)
+
+    corner = halo(e_rows, o_rows, mid)
+    outer = edge_quads(xt, e_rows, o_rows, corner, kt, b0, fw)
+    corner = lax.ppermute(corner, "tm", both)
+    left, right, e_col, o_col = strip_pack(left0, right0, e_rows, o_rows, slab, corner, outer)
+    o_col = lax.ppermute(o_col, "col", swaps(cols, 1))
     e_col = lax.ppermute(e_col, "col", swaps(cols, 0))
-    o_col = lax.ppermute(o_col, "col", swaps(cols, 1))
-
-    field = (xt, inner, e_rows, o_rows, slab, corner, kt, b0, fw)
-    partner = lax.ppermute(edge_quad(False, *field), "tm", both)
+    main, far = rest(True, *field, outer, e_rows, o_rows, corner)
+    far = lax.ppermute(far, "tm", both)
     strips, strips_send = strip_temporal(left, right, e_col, o_col, kt, b0, fw)
-    partner_strips = lax.ppermute(strips_send, "tm", both)
-    near = edge_quad(True, *field)
-    return spatial(rows * 32, inner, near, partner, strips, partner_strips, k1, b1, k2, b2)
+    w1, w2, c1, c2 = spatial_weights(k1, b1, k2, b2, strips)
+    strips_recv = lax.ppermute(strips_send, "tm", both)
+    return spatial(rows * 32, main, mid, partner, strips, far, strips_recv, w1, w2, c1, c2)
 
 
 def solution(mesh):

time: 49.6 us -> 46.1 us (0.929)
  the two profiles are of different devices: /device:TPU:11 before, /device:TPU:30 now
where the time goes in v3:
time: 46.1 us; the launch traced here: 46 us
  Pallas kernels  18.8 us (41%)
  starting transfers between devices  17.5 us (38%)
  waiting for transfers between devices  7.83 us (17%)
  local copies, waits for them, and re-layouts  1.63 us (4%)
    pallas_call x1, Pallas kernels, interior(): pl.pallas_call(interior_kernel, in_specs=[VMEM] * 4, out_specs=[VMEM] * 3...  6.72 us
    ppermute x1, starting transfers between devices, shards(): o_rows = lax.ppermute(o_rows, 'row', swaps(rows, 1))  5.67 us
    pallas_call x2, Pallas kernels, rest(): pl.pallas_call(functools.partial(rest_kernel, own), in_specs=[VMEM] * len...  4.25 us
    ppermute x1, waiting for transfers between devices, shards(): corner = lax.ppermute(corner, 'tm', both)  4.11 us
    ppermute x1, starting transfers between devices, shards(): e_rows = lax.ppermute(e_rows, 'row', swaps(rows, 0))  3.26 us
    pallas_call x1, Pallas kernels, spatial(): pl.pallas_call(functools.partial(spatial_kernel, grid_rows), in_specs=[VM...  3.2 us
    ppermute x1, starting transfers between devices, shards(): o_col = lax.ppermute(o_col, 'col', swaps(cols, 1))  2.93 us
    pallas_call x1, Pallas kernels, edge_quads(): pl.pallas_call(edges_kernel, in_specs=[VMEM] * 3 + [ANY] + [VMEM] * 3, ou...  2.01 us
  transfers between devices with their start and end apart: 9, of which 4 were waited for; matrix products, arithmetic and copies ran while one was open for 0% of the time, Pallas kernels for 32%

profile of v3, /device:TPU:30, one launch (start us, length us, event | category | flops | bytes accessed | tf_op | source)
XLA Modules:
  0.0 46.0 jit_solution(7068969185133029602)
XLA Ops:
  0.0 1.6 %copy-done.7 = bf16[32,8,32,128]{3,2,1,0:T(8,128)(2,1)S(1)} copy-done((bf16[32,8,32,128]{3,2,1,0:T(8,128)(2,1)S(1)}, bf16[32,8,32,128]{3,2,1,0:T(8,128)(2,1)}, u32[]{:S(2)}) %copy-start.7) | copy-done | bytes 2097176
  1.6 0.8 %pack.1 = (bf16[32,320,128]{2,1,0:T(8,128)(2,1)S(1)}, bf16[3,256,128]{2,1,0:T(8,128)(2,1)S(1)}, bf16[3,256,128]{2,1,0:T(8,128)(2,1)S(1)}) custom-call(bf16[32,8,32,128]{3,2,1,0:T(8,128)(2,1)S(1)} %copy-done.7), custom_call_target="tpu_custom_call" | custom-call | flops 6000000000 | bytes 4600000 | tf_op jit(solution)/shard_map/pack/pallas_call | solution.py:62
  2.4 0.0 copy-start
  2.5 2.0 %collective-permute-start = (bf16[32,32,128]{2,1,0:T(8,128)(2,1)S(1)}, bf16[32,32,128]{2,1,0:T(8,128)(2,1)S(1)}, u32[]{:S(2)}, u32[]{:S(2)}) collective-permute-start(bf16[32,32,128]{2,1,0:T(8,128)(2,1)S(1)} %slab.1), channel_id=1, source_target_pairs={{0,128},{128,0},{1,129},{129,1},{2,130},{130,2},{3,131},{131,3},{4... | collective-permute-start | bytes 786440 | tf_op jit(solution)/shard_map/ppermute | solution.py:576
  4.5 3.3 %collective-permute-start.1 = (bf16[3,256,128]{2,1,0:T(8,128)(2,1)S(1)}, bf16[3,256,128]{2,1,0:T(8,128)(2,1)S(1)}, u32[]{:S(2)}, u32[]{:S(2)}) collective-permute-start(bf16[3,256,128]{2,1,0:T(8,128)(2,1)S(1)} %get-tuple-element.27), channel_id=1, source_target_pairs={{0,8},{8,0},{16,24},{24,16},{32,40},{40,32},{48,56},{56,48},{64,72... | collective-permute-start | bytes 589832 | tf_op jit(solution)/shard_map/ppermute | solution.py:574
  7.7 5.7 %collective-permute-start.2 = (bf16[3,256,128]{2,1,0:T(8,128)(2,1)S(1)}, bf16[3,256,128]{2,1,0:T(8,128)(2,1)S(1)}, u32[]{:S(2)}, u32[]{:S(2)}) collective-permute-start(bf16[3,256,128]{2,1,0:T(8,128)(2,1)S(1)} %get-tuple-element.28), channel_id=1, source_target_pairs={{8,16},{16,8},{24,32},{32,24},{40,48},{48,40},{56,64},{64,56},{72,... | collective-permute-start | bytes 589832 | tf_op jit(solution)/shard_map/ppermute | solution.py:575
  13.4 6.7 %interior.1 = (f32[28,64,128]{2,1,0:T(8,128)S(1)}, bf16[256,128]{1,0:T(8,128)(2,1)S(1)}, bf16[256,128]{1,0:T(8,128)(2,1)S(1)}) custom-call(bf16[32,320,128]{2,1,0:T(8,128)(2,1)S(1)} %get-tuple-element.25.xt, bf16[3,3,3,32,64]{4,3,2,1,0:T(8,128)(2,1)S(1)} %bitcast.7, f32[1,64]{1,0:T(1,128)S(1)} %bitcast.14, f32[1,16]{1,0:T(1,128)S(1)} %bitcast.19), custom_call_target="tpu_custom_call" | custom-call | flops 1000 | bytes 1000 | tf_op jit(solution)/shard_map/interior/pallas_call | solution.py:258
  20.2 2.4 %rest_partner.1 = (bf16[16,64,128]{2,1,0:T(8,128)(2,1)S(1)}, f32[4,64,128]{2,1,0:T(8,128)S(1)}) custom-call(bf16[32,320,128]{2,1,0:T(8,128)(2,1)S(1)} %get-tuple-element.25.xt, f32[28,64,128]{2,1,0:T(8,128)S(1)} %get-tuple-element.26.inner, bf16[32,32,128]{2,1,0:T(8,128)(2,1)S(1)} %collective-permute-done.slab, bf16[3,3,3,32,64]{4,3,2,1,0:T(8,128)(2,1)S(1)} %bitcast.8, ...), custom_call_target="tpu_custom_call" | custom-call | flops 1000000 | bytes 1000000 | tf_op jit(solution)/shard_map/rest_partner/pallas_call | solution.py:361
  22.6 1.1 %collective-permute-start.4 = (bf16[16,64,128]{2,1,0:T(8,128)(2,1)S(1)}, bf16[16,64,128]{2,1,0:T(8,128)(2,1)S(1)}, u32[]{:S(2)}, u32[]{:S(2)}) collective-permute-start(bf16[16,64,128]{2,1,0:T(8,128)(2,1)S(1)} %get-tuple-element.31), channel_id=1, source_target_pairs={{0,128},{128,0},{1,129},{129,1},{2,130},{130,2},{3,131},{131,3},{4... | collective-permute-start | bytes 786440 | tf_op jit(solution)/shard_map/ppermute | solution.py:580
  23.6 1.0 %collective-permute-done.2.o_rows.refs_2_ = bf16[3,256,128]{2,1,0:T(8,128)(2,1)S(1)} collective-permute-done((bf16[3,256,128]{2,1,0:T(8,128)(2,1)S(1)}, bf16[3,256,128]{2,1,0:T(8,128)(2,1)S(1)}, u32[]{:S(2)}, u32[]{:S(2)}) %collective-permute-start.2) | collective-permute-done | bytes 196640 | tf_op jit(solution)/shard_map/ppermute | solution.py:575
  24.7 0.1 collective-permute-start.3
  24.8 2.0 %edge_quads.1.refs_0_.after = f32[8,64,128]{2,1,0:T(8,128)S(1)} custom-call(bf16[32,320,128]{2,1,0:T(8,128)(2,1)S(1)} %get-tuple-element.25.xt, bf16[3,256,128]{2,1,0:T(8,128)(2,1)S(1)} %collective-permute-done.1.e_rows.refs_1_, bf16[3,256,128]{2,1,0:T(8,128)(2,1)S(1)} %collective-permute-done.2.o_rows.refs_2_, bf16[6,32,128]{2,1,0:T(8,128)(2,1)S(1)} %halo.1.after, ...), custom_call_target="tpu_custom_call" | custom-call | flops 1207959552 | bytes 2000000 | tf_op jit(solution)/shard_map/edge_quads/pallas_call | solution.py:294
  26.8 4.1 %collective-permute-done.3.refs_3_.corner = bf16[6,32,128]{2,1,0:T(8,128)(2,1)S(1)} collective-permute-done((bf16[6,32,128]{2,1,0:T(8,128)(2,1)S(1)}, bf16[6,32,128]{2,1,0:T(8,128)(2,1)S(1)}, u32[]{:S(2)}, u32[]{:S(2)}) %collective-permute-start.3) | collective-permute-done | bytes 49184 | tf_op jit(solution)/shard_map/ppermute | solution.py:584
  30.9 0.6 %strip_pack.1 = (bf16[288,128]{1,0:T(8,128)(2,1)S(1)}, bf16[288,128]{1,0:T(8,128)(2,1)S(1)}, bf16[288,128]{1,0:T(8,128)(2,1)S(1)}, bf16[288,128]{1,0:T(8,128)(2,1)S(1)}) custom-call(bf16[256,128]{1,0:T(8,128)(2,1)S(1)} %get-tuple-element.32.left0, bf16[256,128]{1,0:T(8,128)(2,1)S(1)} %get-tuple-element.33.right0, ...), custom_call_target="tpu_custom_call" | custom-call | flops 100000000 | bytes 1000000 | tf_op jit(solution)/shard_map/strip_pack/pallas_call | solution.py:184
  31.5 0.2 collective-permute-start.5
  31.7 2.9 %collective-permute-start.6 = (bf16[288,128]{1,0:T(8,128)(2,1)S(1)}, bf16[288,128]{1,0:T(8,128)(2,1)S(1)}, u32[]{:S(2)}, u32[]{:S(2)}) collective-permute-start(bf16[288,128]{1,0:T(8,128)(2,1)S(1)} %get-tuple-element.37), channel_id=1, source_target_pairs={{1,2},{2,1},{3,4},{4,3},{5,6},{6,5},{9,10},{10,9},{11,12},{12,11},... | collective-permute-start | bytes 221192 | tf_op jit(solution)/shard_map/ppermute | solution.py:586
  34.7 1.9 %rest_own.1 = (f32[16,64,128]{2,1,0:T(8,128)S(1)}, bf16[4,64,128]{2,1,0:T(8,128)(2,1)S(1)}) custom-call(bf16[32,320,128]{2,1,0:T(8,128)(2,1)S(1)} %get-tuple-element.25.xt, f32[28,64,128]{2,1,0:T(8,128)S(1)} %get-tuple-element.26.inner, bf16[32,32,128]{2,1,0:T(8,128)(2,1)S(1)} %collective-permute-done.slab, bf16[3,3,3,32,64]{4,3,2,1,0:T(8,128)(2,1)S(1)} %bitcast.10, ...), custom_call_target="tpu_custom_call" | custom-call | flops 1000000 | bytes 1000000 | tf_op jit(solution)/shard_map/rest_own/pallas_call | solution.py:361
  36.6 1.1 %collective-permute-start.7 = (bf16[4,64,128]{2,1,0:T(8,128)(2,1)S(1)}, bf16[4,64,128]{2,1,0:T(8,128)(2,1)S(1)}, u32[]{:S(2)}, u32[]{:S(2)}) collective-permute-start(bf16[4,64,128]{2,1,0:T(8,128)(2,1)S(1)} %get-tuple-element.39), channel_id=1, source_target_pairs={{0,128},{128,0},{1,129},{129,1},{2,130},{130,2},{3,131},{131,3},{4... | collective-permute-start | bytes 196616 | tf_op jit(solution)/shard_map/ppermute | solution.py:589
  37.7 1.1 %strip_temporal.1 = (f32[2,64,128]{2,1,0:T(8,128)S(1)}, bf16[2,64,128]{2,1,0:T(8,128)(2,1)S(1)}) custom-call(bf16[288,128]{1,0:T(8,128)(2,1)S(1)} %get-tuple-element.34.own_l, bf16[288,128]{1,0:T(8,128)(2,1)S(1)} %get-tuple-element.35.own_r, bf16[288,128]{1,0:T(8,128)(2,1)S(1)} %collective-permute-done.5.e_col, ...), custom_call_target="tpu_custom_call" | custom-call | flops 1000000 | bytes 1000000 | tf_op jit(solution)/shard_map/strip_temporal/pallas_call | solution.py:439
  38.8 1.1 %collective-permute-start.8 = (bf16[2,64,128]{2,1,0:T(8,128)(2,1)S(1)}, bf16[2,64,128]{2,1,0:T(8,128)(2,1)S(1)}, u32[]{:S(2)}, u32[]{:S(2)}) collective-permute-start(bf16[2,64,128]{2,1,0:T(8,128)(2,1)S(1)} %get-tuple-element.40), channel_id=1, source_target_pairs={{0,128},{128,0},{1,129},{129,1},{2,130},{130,2},{3,131},{131,3},{4... | collective-permute-start | bytes 98312 | tf_op jit(solution)/shard_map/ppermute | solution.py:592
  39.9 0.2 spatial_weights.1
  40.1 0.9 %collective-permute-done.7.partner_far = bf16[4,64,128]{2,1,0:T(8,128)(2,1)S(1)} collective-permute-done((bf16[4,64,128]{2,1,0:T(8,128)(2,1)S(1)}, bf16[4,64,128]{2,1,0:T(8,128)(2,1)S(1)}, u32[]{:S(2)}, u32[]{:S(2)}) %collective-permute-start.7) | collective-permute-done | bytes 65568 | tf_op jit(solution)/shard_map/ppermute | solution.py:589
  40.9 1.8 %collective-permute-done.8.partner_strips = bf16[2,64,128]{2,1,0:T(8,128)(2,1)S(1)} collective-permute-done((bf16[2,64,128]{2,1,0:T(8,128)(2,1)S(1)}, bf16[2,64,128]{2,1,0:T(8,128)(2,1)S(1)}, u32[]{:S(2)}, u32[]{:S(2)}) %collective-permute-start.8) | collective-permute-done | bytes 32800 | tf_op jit(solution)/shard_map/ppermute | solution.py:592
  42.8 3.2 %spatial.1 = bf16[128,16,128]{2,1,0:T(8,128)(2,1)} custom-call(f32[16,64,128]{2,1,0:T(8,128)S(1)} %get-tuple-element.30.main, f32[4,64,128]{2,1,0:T(8,128)S(1)} %get-tuple-element.29.after.mid, bf16[16,64,128]{2,1,0:T(8,128)(2,1)S(1)} %collective-permute-done.4.partner, f32[2,64,128]{2,1,0:T(8,128)S(1)} %get-tuple-element.38.after.strips, ...), custom_call_target="tpu_custom_call" | custom-call | flops 1200000000 | bytes 3000000 | tf_op jit(solution)/shard_map/spatial/pallas_call | solution.py:542
  (21 shorter events, 0.1 us)
Async XLA Ops:
  0.0 1.6 %copy-start.7 = (bf16[32,8,32,128]{3,2,1,0:T(8,128)(2,1)S(1)}, bf16[32,8,32,128]{3,2,1,0:T(8,128)(2,1)}, u32[]{:S(2)}) copy-start(bf16[32,8,32,128]{3,2,1,0:T(8,128)(2,1)} %x.1) | copy-start | bytes 6291460
  2.4 11.0 %copy-start = (bf16[64,32,3,3,3]{0,1,4,3,2:T(8,128)(2,1)S(1)}, bf16[64,32,3,3,3]{0,1,4,3,2:T(8,128)(2,1)}, u32[]{:S(2)}) copy-start(bf16[64,32,3,3,3]{0,1,4,3,2:T(8,128)(2,1)} %param.9) | copy-start | bytes 331780
  2.4 11.0 %copy-start.3 = (f32[64]{0:T(128)S(1)}, f32[64]{0:T(128)}, u32[]{:S(2)}) copy-start(f32[64]{0:T(128)} %param.10) | copy-start | bytes 772
  2.4 11.0 %copy-start.4 = (f32[16]{0:T(128)S(1)}, f32[16]{0:T(128)}, u32[]{:S(2)}) copy-start(f32[16]{0:T(128)} %param.11) | copy-start | bytes 196
  2.5 17.7 %collective-permute-start = (bf16[32,32,128]{2,1,0:T(8,128)(2,1)S(1)}, bf16[32,32,128]{2,1,0:T(8,128)(2,1)S(1)}, u32[]{:S(2)}, u32[]{:S(2)}) collective-permute-start(bf16[32,32,128]{2,1,0:T(8,128)(2,1)S(1)} %slab.1), channel_id=1, source_target_pairs={{0,128},{128,0},{1,129},{129,1},{2,130},{130,2},{3,131},{131,3},{4... | collective-permute-start | bytes 786440 | tf_op jit(solution)/shard_map/ppermute | solution.py:576
  4.5 19.2 %collective-permute-start.1 = (bf16[3,256,128]{2,1,0:T(8,128)(2,1)S(1)}, bf16[3,256,128]{2,1,0:T(8,128)(2,1)S(1)}, u32[]{:S(2)}, u32[]{:S(2)}) collective-permute-start(bf16[3,256,128]{2,1,0:T(8,128)(2,1)S(1)} %get-tuple-element.27), channel_id=1, source_target_pairs={{0,8},{8,0},{16,24},{24,16},{32,40},{40,32},{48,56},{56,48},{64,72... | collective-permute-start | bytes 589832 | tf_op jit(solution)/shard_map/ppermute | solution.py:574
  7.7 16.9 %collective-permute-start.2 = (bf16[3,256,128]{2,1,0:T(8,128)(2,1)S(1)}, bf16[3,256,128]{2,1,0:T(8,128)(2,1)S(1)}, u32[]{:S(2)}, u32[]{:S(2)}) collective-permute-start(bf16[3,256,128]{2,1,0:T(8,128)(2,1)S(1)} %get-tuple-element.28), channel_id=1, source_target_pairs={{8,16},{16,8},{24,32},{32,24},{40,48},{48,40},{56,64},{64,56},{72,... | collective-permute-start | bytes 589832 | tf_op jit(solution)/shard_map/ppermute | solution.py:575
  22.6 20.2 %collective-permute-start.4 = (bf16[16,64,128]{2,1,0:T(8,128)(2,1)S(1)}, bf16[16,64,128]{2,1,0:T(8,128)(2,1)S(1)}, u32[]{:S(2)}, u32[]{:S(2)}) collective-permute-start(bf16[16,64,128]{2,1,0:T(8,128)(2,1)S(1)} %get-tuple-element.31), channel_id=1, source_target_pairs={{0,128},{128,0},{1,129},{129,1},{2,130},{130,2},{3,131},{131,3},{4... | collective-permute-start | bytes 786440 | tf_op jit(solution)/shard_map/ppermute | solution.py:580
  24.7 6.2 %collective-permute-start.3 = (bf16[6,32,128]{2,1,0:T(8,128)(2,1)S(1)}, bf16[6,32,128]{2,1,0:T(8,128)(2,1)S(1)}, u32[]{:S(2)}, u32[]{:S(2)}) collective-permute-start(bf16[6,32,128]{2,1,0:T(8,128)(2,1)S(1)} %halo.1.after), channel_id=1, source_target_pairs={{0,128},{128,0},{1,129},{129,1},{2,130},{130,2},{3,131},{131,3},{4... | collective-permute-start | bytes 147464 | tf_op jit(solution)/shard_map/ppermute | solution.py:584
  31.5 6.2 %collective-permute-start.5 = (bf16[288,128]{1,0:T(8,128)(2,1)S(1)}, bf16[288,128]{1,0:T(8,128)(2,1)S(1)}, u32[]{:S(2)}, u32[]{:S(2)}) collective-permute-start(bf16[288,128]{1,0:T(8,128)(2,1)S(1)} %get-tuple-element.36), channel_id=1, source_target_pairs={{0,1},{1,0},{2,3},{3,2},{4,5},{5,4},{6,7},{7,6},{8,9},{9,8},{10,11... | collective-permute-start | bytes 221192 | tf_op jit(solution)/shard_map/ppermute | solution.py:587
  31.7 8.2 %copy-start.1 = (bf16[128,128,3,3]{1,0,3,2:T(8,128)(2,1)S(1)}, bf16[128,128,3,3]{1,0,3,2:T(8,128)(2,1)}, u32[]{:S(2)}) copy-start(bf16[128,128,3,3]{1,0,3,2:T(8,128)(2,1)} %param.14) | copy-start | bytes 884740
  31.7 8.2 %copy-start.2 = (bf16[128,64,3,3]{0,1,3,2:T(8,128)(2,1)S(1)}, bf16[128,64,3,3]{0,1,3,2:T(8,128)(2,1)}, u32[]{:S(2)}) copy-start(bf16[128,64,3,3]{0,1,3,2:T(8,128)(2,1)} %param.12) | copy-start | bytes 442372
  31.7 8.2 %copy-start.5 = (f32[128]{0:T(128)S(1)}, f32[128]{0:T(128)}, u32[]{:S(2)}) copy-start(f32[128]{0:T(128)} %param.13) | copy-start | bytes 1540
  31.7 8.2 %copy-start.6 = (f32[128]{0:T(128)S(1)}, f32[128]{0:T(128)}, u32[]{:S(2)}) copy-start(f32[128]{0:T(128)} %param.15) | copy-start | bytes 1540
  31.7 5.9 %collective-permute-start.6 = (bf16[288,128]{1,0:T(8,128)(2,1)S(1)}, bf16[288,128]{1,0:T(8,128)(2,1)S(1)}, u32[]{:S(2)}, u32[]{:S(2)}) collective-permute-start(bf16[288,128]{1,0:T(8,128)(2,1)S(1)} %get-tuple-element.37), channel_id=1, source_target_pairs={{1,2},{2,1},{3,4},{4,3},{5,6},{6,5},{9,10},{10,9},{11,12},{12,11},... | collective-permute-start | bytes 221192 | tf_op jit(solution)/shard_map/ppermute | solution.py:586
  36.6 4.4 %collective-permute-start.7 = (bf16[4,64,128]{2,1,0:T(8,128)(2,1)S(1)}, bf16[4,64,128]{2,1,0:T(8,128)(2,1)S(1)}, u32[]{:S(2)}, u32[]{:S(2)}) collective-permute-start(bf16[4,64,128]{2,1,0:T(8,128)(2,1)S(1)} %get-tuple-element.39), channel_id=1, source_target_pairs={{0,128},{128,0},{1,129},{129,1},{2,130},{130,2},{3,131},{131,3},{4... | collective-permute-start | bytes 196616 | tf_op jit(solution)/shard_map/ppermute | solution.py:589
  38.8 4.0 %collective-permute-start.8 = (bf16[2,64,128]{2,1,0:T(8,128)(2,1)S(1)}, bf16[2,64,128]{2,1,0:T(8,128)(2,1)S(1)}, u32[]{:S(2)}, u32[]{:S(2)}) collective-permute-start(bf16[2,64,128]{2,1,0:T(8,128)(2,1)S(1)} %get-tuple-element.40), channel_id=1, source_target_pairs={{0,128},{128,0},{1,129},{129,1},{2,130},{130,2},{3,131},{131,3},{4... | collective-permute-start | bytes 98312 | tf_op jit(solution)/shard_map/ppermute | solution.py:592

commit v4 on v3

--- a/solution.py
+++ b/solution.py
@@ -150,7 +150,8 @@
     )(e_rows, o_rows, after)
 
 
-def strip_pack_kernel(left0, right0, e_rows, o_rows, slab, corner, after, left, right, e_send, o_send, edge):
+def strip_pack_kernel(left0, right0, e_rows, o_rows, slab, corner, after, for_partner, left, right, e_send, o_send, send, edge):
+    send[...] = for_partner[...]
     lane = lanes_of((16, 128))
     even = lax.axis_index("row") % 2 == 0
     even_col = lax.axis_index("col") % 2 == 0
@@ -183,9 +184,9 @@
 def strip_pack(*args):
     return pl.pallas_call(
         strip_pack_kernel,
-        in_specs=[VMEM] * 6 + [ANY],
-        out_specs=[VMEM] * 4,
-        out_shape=[struct((288, 128))] * 4,
+        in_specs=[VMEM] * 6 + [ANY, VMEM],
+        out_specs=[VMEM] * 5,
+        out_shape=[struct((288, 128))] * 4 + [struct((16, 64, 128))],
         scratch_shapes=[pltpu.VMEM((6, 288, 128), BF)],
         compiler_params=params(),
         cost_estimate=cost(1e8, 1e6),
@@ -577,12 +578,12 @@
     inner, left0, right0 = interior(xt, kt, b0, fw)
     field = (xt, inner, slab, kt, b0, fw)
     for_partner, mid = rest(False, *field)
-    partner = lax.ppermute(for_partner, "tm", both)
-
     corner = halo(e_rows, o_rows, mid)
     outer = edge_quads(xt, e_rows, o_rows, corner, kt, b0, fw)
     corner = lax.ppermute(corner, "tm", both)
-    left, right, e_col, o_col = strip_pack(left0, right0, e_rows, o_rows, slab, corner, outer)
+    packed = strip_pack(left0, right0, e_rows, o_rows, slab, corner, outer, for_partner)
+    left, right, e_col, o_col, for_partner = packed
+    partner = lax.ppermute(for_partner, "tm", both)
     o_col = lax.ppermute(o_col, "col", swaps(cols, 1))
     e_col = lax.ppermute(e_col, "col", swaps(cols, 0))
     main, far = rest(True, *field, outer, e_rows, o_rows, corner)

time: 46.1 us -> 44.7 us (0.970)
  waiting for transfers between devices: 7.83 us -> 6.89 us
  starting transfers between devices: 17.5 us -> 16.9 us
    ppermute x1, waiting for transfers between devices: 4.11 us -> 2.06 us  [shards(): corner = lax.ppermute(corner, 'tm', both)]
    ppermute x1, starting transfers between devices: 1.09 us -> 0.04 us  [shards(): partner = lax.ppermute(for_partner, 'tm', both)]
    ppermute x1, waiting for transfers between devices: 1.01 us -> 1.94 us  [shards(): o_rows = lax.ppermute(o_rows, 'row', swaps(rows, 1))]
    ppermute x1, starting transfers between devices: 1.1 us -> 1.83 us  [shards(): far = lax.ppermute(far, 'tm', both)]
where the time goes in v4:
time: 44.7 us; the launch traced here: 44.5 us
  Pallas kernels  18.8 us (42%)
  starting transfers between devices  16.9 us (38%)
  waiting for transfers between devices  6.89 us (15%)
  local copies, waits for them, and re-layouts  1.63 us (4%)
    pallas_call x1, Pallas kernels, interior(): pl.pallas_call(interior_kernel, in_specs=[VMEM] * 4, out_specs=[VMEM] * 3...  6.72 us
    ppermute x1, starting transfers between devices, shards(): o_rows = lax.ppermute(o_rows, 'row', swaps(rows, 1))  5.67 us
    pallas_call x2, Pallas kernels, rest(): pl.pallas_call(functools.partial(rest_kernel, own), in_specs=[VMEM] * len...  4.25 us
    ppermute x1, starting transfers between devices, shards(): e_rows = lax.ppermute(e_rows, 'row', swaps(rows, 0))  3.26 us
    pallas_call x1, Pallas kernels, spatial(): pl.pallas_call(functools.partial(spatial_kernel, grid_rows), in_specs=[VM...  3.2 us
    ppermute x1, starting transfers between devices, shards(): o_col = lax.ppermute(o_col, 'col', swaps(cols, 1))  2.93 us
    ppermute x1, waiting for transfers between devices, shards(): strips_recv = lax.ppermute(strips_send, 'tm', both)  2.22 us
    ppermute x1, waiting for transfers between devices, shards(): corner = lax.ppermute(corner, 'tm', both)  2.06 us
  transfers between devices with their start and end apart: 9, of which 4 were waited for; matrix products, arithmetic and copies ran while one was open for 0% of the time, Pallas kernels for 32%

profile of v4, /device:TPU:30, one launch (start us, length us, event | category | flops | bytes accessed | tf_op | source)
XLA Modules:
  0.0 44.5 jit_solution(2493745055182114784)
XLA Ops:
  0.0 1.6 %copy-done.7 = bf16[32,8,32,128]{3,2,1,0:T(8,128)(2,1)S(1)} copy-done((bf16[32,8,32,128]{3,2,1,0:T(8,128)(2,1)S(1)}, bf16[32,8,32,128]{3,2,1,0:T(8,128)(2,1)}, u32[]{:S(2)}) %copy-start.7) | copy-done | bytes 2097176
  1.6 0.8 %pack.1 = (bf16[32,320,128]{2,1,0:T(8,128)(2,1)S(1)}, bf16[3,256,128]{2,1,0:T(8,128)(2,1)S(1)}, bf16[3,256,128]{2,1,0:T(8,128)(2,1)S(1)}) custom-call(bf16[32,8,32,128]{3,2,1,0:T(8,128)(2,1)S(1)} %copy-done.7), custom_call_target="tpu_custom_call" | custom-call | flops 6000000000 | bytes 4600000 | tf_op jit(solution)/shard_map/pack/pallas_call | solution.py:62
  2.4 0.0 copy-start.3
  2.4 0.0 copy-start.4
  2.5 2.0 %collective-permute-start = (bf16[32,32,128]{2,1,0:T(8,128)(2,1)S(1)}, bf16[32,32,128]{2,1,0:T(8,128)(2,1)S(1)}, u32[]{:S(2)}, u32[]{:S(2)}) collective-permute-start(bf16[32,32,128]{2,1,0:T(8,128)(2,1)S(1)} %slab.1), channel_id=1, source_target_pairs={{0,128},{128,0},{1,129},{129,1},{2,130},{130,2},{3,131},{131,3},{4... | collective-permute-start | bytes 786440 | tf_op jit(solution)/shard_map/ppermute | solution.py:577
  4.5 3.3 %collective-permute-start.1 = (bf16[3,256,128]{2,1,0:T(8,128)(2,1)S(1)}, bf16[3,256,128]{2,1,0:T(8,128)(2,1)S(1)}, u32[]{:S(2)}, u32[]{:S(2)}) collective-permute-start(bf16[3,256,128]{2,1,0:T(8,128)(2,1)S(1)} %get-tuple-element.28), channel_id=1, source_target_pairs={{0,8},{8,0},{16,24},{24,16},{32,40},{40,32},{48,56},{56,48},{64,72... | collective-permute-start | bytes 589832 | tf_op jit(solution)/shard_map/ppermute | solution.py:575
  7.7 5.7 %collective-permute-start.2 = (bf16[3,256,128]{2,1,0:T(8,128)(2,1)S(1)}, bf16[3,256,128]{2,1,0:T(8,128)(2,1)S(1)}, u32[]{:S(2)}, u32[]{:S(2)}) collective-permute-start(bf16[3,256,128]{2,1,0:T(8,128)(2,1)S(1)} %get-tuple-element.29), channel_id=1, source_target_pairs={{8,16},{16,8},{24,32},{32,24},{40,48},{48,40},{56,64},{64,56},{72,... | collective-permute-start | bytes 589832 | tf_op jit(solution)/shard_map/ppermute | solution.py:576
  13.4 6.7 %interior.1 = (f32[28,64,128]{2,1,0:T(8,128)S(1)}, bf16[256,128]{1,0:T(8,128)(2,1)S(1)}, bf16[256,128]{1,0:T(8,128)(2,1)S(1)}) custom-call(bf16[32,320,128]{2,1,0:T(8,128)(2,1)S(1)} %get-tuple-element.26.xt, bf16[3,3,3,32,64]{4,3,2,1,0:T(8,128)(2,1)S(1)} %bitcast.7, f32[1,64]{1,0:T(1,128)S(1)} %bitcast.14, f32[1,16]{1,0:T(1,128)S(1)} %bitcast.19), custom_call_target="tpu_custom_call" | custom-call | flops 1000 | bytes 1000 | tf_op jit(solution)/shard_map/interior/pallas_call | solution.py:259
  20.2 2.4 %rest_partner.1 = (bf16[16,64,128]{2,1,0:T(8,128)(2,1)S(1)}, f32[4,64,128]{2,1,0:T(8,128)S(1)}) custom-call(bf16[32,320,128]{2,1,0:T(8,128)(2,1)S(1)} %get-tuple-element.26.xt, f32[28,64,128]{2,1,0:T(8,128)S(1)} %get-tuple-element.27.inner, bf16[32,32,128]{2,1,0:T(8,128)(2,1)S(1)} %collective-permute-done.slab, bf16[3,3,3,32,64]{4,3,2,1,0:T(8,128)(2,1)S(1)} %bitcast.8, ...), custom_call_target="tpu_custom_call" | custom-call | flops 1000000 | bytes 1000000 | tf_op jit(solution)/shard_map/rest_partner/pallas_call | solution.py:362
  22.6 1.9 %collective-permute-done.2.o_rows.refs_2_ = bf16[3,256,128]{2,1,0:T(8,128)(2,1)S(1)} collective-permute-done((bf16[3,256,128]{2,1,0:T(8,128)(2,1)S(1)}, bf16[3,256,128]{2,1,0:T(8,128)(2,1)S(1)}, u32[]{:S(2)}, u32[]{:S(2)}) %collective-permute-start.2) | collective-permute-done | bytes 196640 | tf_op jit(solution)/shard_map/ppermute | solution.py:576
  24.5 2.0 %edge_quads.1.refs_0_.after = f32[8,64,128]{2,1,0:T(8,128)S(1)} custom-call(bf16[32,320,128]{2,1,0:T(8,128)(2,1)S(1)} %get-tuple-element.26.xt, bf16[3,256,128]{2,1,0:T(8,128)(2,1)S(1)} %collective-permute-done.1.e_rows.refs_1_, bf16[3,256,128]{2,1,0:T(8,128)(2,1)S(1)} %collective-permute-done.2.o_rows.refs_2_, bf16[6,32,128]{2,1,0:T(8,128)(2,1)S(1)} %halo.1.after, ...), custom_call_target="tpu_custom_call" | custom-call | flops 1207959552 | bytes 2000000 | tf_op jit(solution)/shard_map/edge_quads/pallas_call | solution.py:295
  26.5 2.1 %collective-permute-done.3.refs_3_.corner = bf16[6,32,128]{2,1,0:T(8,128)(2,1)S(1)} collective-permute-done((bf16[6,32,128]{2,1,0:T(8,128)(2,1)S(1)}, bf16[6,32,128]{2,1,0:T(8,128)(2,1)S(1)}, u32[]{:S(2)}, u32[]{:S(2)}) %collective-permute-start.3) | collective-permute-done | bytes 49184 | tf_op jit(solution)/shard_map/ppermute | solution.py:583
  28.6 0.6 %strip_pack.1 = (bf16[288,128]{1,0:T(8,128)(2,1)S(1)}, bf16[288,128]{1,0:T(8,128)(2,1)S(1)}, bf16[288,128]{1,0:T(8,128)(2,1)S(1)}, bf16[288,128]{1,0:T(8,128)(2,1)S(1)}, bf16[16,64,128]{2,1,0:T(8,128)(2,1)S(1)}) custom-call(bf16[256,128]{1,0:T(8,128)(2,1)S(1)} %get-tuple-element.32.left0, bf16[256,128]{1,0:T(8,128)(2,1)S(1)} %get-tuple-element.33.right0, ...), custom_call_target="tpu_custom_call" | custom-call | flops 100000000 | bytes 1000000 | tf_op jit(solution)/shard_map/strip_pack/pallas_call | solution.py:185
  29.2 0.0 collective-permute-start.4
  29.2 0.3 collective-permute-start.5
  29.5 2.9 %collective-permute-start.6 = (bf16[288,128]{1,0:T(8,128)(2,1)S(1)}, bf16[288,128]{1,0:T(8,128)(2,1)S(1)}, u32[]{:S(2)}, u32[]{:S(2)}) collective-permute-start(bf16[288,128]{1,0:T(8,128)(2,1)S(1)} %get-tuple-element.39), channel_id=1, source_target_pairs={{1,2},{2,1},{3,4},{4,3},{5,6},{6,5},{9,10},{10,9},{11,12},{12,11},... | collective-permute-start | bytes 221192 | tf_op jit(solution)/shard_map/ppermute | solution.py:587
  32.5 1.9 %rest_own.1 = (f32[16,64,128]{2,1,0:T(8,128)S(1)}, bf16[4,64,128]{2,1,0:T(8,128)(2,1)S(1)}) custom-call(bf16[32,320,128]{2,1,0:T(8,128)(2,1)S(1)} %get-tuple-element.26.xt, f32[28,64,128]{2,1,0:T(8,128)S(1)} %get-tuple-element.27.inner, bf16[32,32,128]{2,1,0:T(8,128)(2,1)S(1)} %collective-permute-done.slab, bf16[3,3,3,32,64]{4,3,2,1,0:T(8,128)(2,1)S(1)} %bitcast.10, ...), custom_call_target="tpu_custom_call" | custom-call | flops 1000000 | bytes 1000000 | tf_op jit(solution)/shard_map/rest_own/pallas_call | solution.py:362
  34.4 1.8 %collective-permute-start.7 = (bf16[4,64,128]{2,1,0:T(8,128)(2,1)S(1)}, bf16[4,64,128]{2,1,0:T(8,128)(2,1)S(1)}, u32[]{:S(2)}, u32[]{:S(2)}) collective-permute-start(bf16[4,64,128]{2,1,0:T(8,128)(2,1)S(1)} %get-tuple-element.41), channel_id=1, source_target_pairs={{0,128},{128,0},{1,129},{129,1},{2,130},{130,2},{3,131},{131,3},{4... | collective-permute-start | bytes 196616 | tf_op jit(solution)/shard_map/ppermute | solution.py:590
  36.2 1.1 %strip_temporal.1 = (f32[2,64,128]{2,1,0:T(8,128)S(1)}, bf16[2,64,128]{2,1,0:T(8,128)(2,1)S(1)}) custom-call(bf16[288,128]{1,0:T(8,128)(2,1)S(1)} %get-tuple-element.36.own_l, bf16[288,128]{1,0:T(8,128)(2,1)S(1)} %get-tuple-element.37.own_r, bf16[288,128]{1,0:T(8,128)(2,1)S(1)} %collective-permute-done.5.e_col, ...), custom_call_target="tpu_custom_call" | custom-call | flops 1000000 | bytes 1000000 | tf_op jit(solution)/shard_map/strip_temporal/pallas_call | solution.py:440
  37.3 0.9 %collective-permute-start.8 = (bf16[2,64,128]{2,1,0:T(8,128)(2,1)S(1)}, bf16[2,64,128]{2,1,0:T(8,128)(2,1)S(1)}, u32[]{:S(2)}, u32[]{:S(2)}) collective-permute-start(bf16[2,64,128]{2,1,0:T(8,128)(2,1)S(1)} %get-tuple-element.42), channel_id=1, source_target_pairs={{0,128},{128,0},{1,129},{129,1},{2,130},{130,2},{3,131},{131,3},{4... | collective-permute-start | bytes 98312 | tf_op jit(solution)/shard_map/ppermute | solution.py:593
  38.3 0.2 spatial_weights.1
  38.4 0.7 %collective-permute-done.7.partner_far = bf16[4,64,128]{2,1,0:T(8,128)(2,1)S(1)} collective-permute-done((bf16[4,64,128]{2,1,0:T(8,128)(2,1)S(1)}, bf16[4,64,128]{2,1,0:T(8,128)(2,1)S(1)}, u32[]{:S(2)}, u32[]{:S(2)}) %collective-permute-start.7) | collective-permute-done | bytes 65568 | tf_op jit(solution)/shard_map/ppermute | solution.py:590
  39.1 2.2 %collective-permute-done.8.partner_strips = bf16[2,64,128]{2,1,0:T(8,128)(2,1)S(1)} collective-permute-done((bf16[2,64,128]{2,1,0:T(8,128)(2,1)S(1)}, bf16[2,64,128]{2,1,0:T(8,128)(2,1)S(1)}, u32[]{:S(2)}, u32[]{:S(2)}) %collective-permute-start.8) | collective-permute-done | bytes 32800 | tf_op jit(solution)/shard_map/ppermute | solution.py:593
  41.3 3.2 %spatial.1 = bf16[128,16,128]{2,1,0:T(8,128)(2,1)} custom-call(f32[16,64,128]{2,1,0:T(8,128)S(1)} %get-tuple-element.31.main, f32[4,64,128]{2,1,0:T(8,128)S(1)} %get-tuple-element.30.after.mid, bf16[16,64,128]{2,1,0:T(8,128)(2,1)S(1)} %collective-permute-done.4.partner, f32[2,64,128]{2,1,0:T(8,128)S(1)} %get-tuple-element.40.after.strips, ...), custom_call_target="tpu_custom_call" | custom-call | flops 1200000000 | bytes 3000000 | tf_op jit(solution)/shard_map/spatial/pallas_call | solution.py:543
  (21 shorter events, 0.1 us)
Async XLA Ops:
  0.0 1.6 %copy-start.7 = (bf16[32,8,32,128]{3,2,1,0:T(8,128)(2,1)S(1)}, bf16[32,8,32,128]{3,2,1,0:T(8,128)(2,1)}, u32[]{:S(2)}) copy-start(bf16[32,8,32,128]{3,2,1,0:T(8,128)(2,1)} %x.1) | copy-start | bytes 6291460
  2.4 11.0 %copy-start = (bf16[64,32,3,3,3]{0,1,4,3,2:T(8,128)(2,1)S(1)}, bf16[64,32,3,3,3]{0,1,4,3,2:T(8,128)(2,1)}, u32[]{:S(2)}) copy-start(bf16[64,32,3,3,3]{0,1,4,3,2:T(8,128)(2,1)} %param.9) | copy-start | bytes 331780
  2.4 11.0 %copy-start.3 = (f32[64]{0:T(128)S(1)}, f32[64]{0:T(128)}, u32[]{:S(2)}) copy-start(f32[64]{0:T(128)} %param.10) | copy-start | bytes 772
  2.4 11.0 %copy-start.4 = (f32[16]{0:T(128)S(1)}, f32[16]{0:T(128)}, u32[]{:S(2)}) copy-start(f32[16]{0:T(128)} %param.11) | copy-start | bytes 196
  2.5 17.7 %collective-permute-start = (bf16[32,32,128]{2,1,0:T(8,128)(2,1)S(1)}, bf16[32,32,128]{2,1,0:T(8,128)(2,1)S(1)}, u32[]{:S(2)}, u32[]{:S(2)}) collective-permute-start(bf16[32,32,128]{2,1,0:T(8,128)(2,1)S(1)} %slab.1), channel_id=1, source_target_pairs={{0,128},{128,0},{1,129},{129,1},{2,130},{130,2},{3,131},{131,3},{4... | collective-permute-start | bytes 786440 | tf_op jit(solution)/shard_map/ppermute | solution.py:577
  4.5 18.1 %collective-permute-start.1 = (bf16[3,256,128]{2,1,0:T(8,128)(2,1)S(1)}, bf16[3,256,128]{2,1,0:T(8,128)(2,1)S(1)}, u32[]{:S(2)}, u32[]{:S(2)}) collective-permute-start(bf16[3,256,128]{2,1,0:T(8,128)(2,1)S(1)} %get-tuple-element.28), channel_id=1, source_target_pairs={{0,8},{8,0},{16,24},{24,16},{32,40},{40,32},{48,56},{56,48},{64,72... | collective-permute-start | bytes 589832 | tf_op jit(solution)/shard_map/ppermute | solution.py:575
  7.7 16.8 %collective-permute-start.2 = (bf16[3,256,128]{2,1,0:T(8,128)(2,1)S(1)}, bf16[3,256,128]{2,1,0:T(8,128)(2,1)S(1)}, u32[]{:S(2)}, u32[]{:S(2)}) collective-permute-start(bf16[3,256,128]{2,1,0:T(8,128)(2,1)S(1)} %get-tuple-element.29), channel_id=1, source_target_pairs={{8,16},{16,8},{24,32},{32,24},{40,48},{48,40},{56,64},{64,56},{72,... | collective-permute-start | bytes 589832 | tf_op jit(solution)/shard_map/ppermute | solution.py:576
  24.5 4.1 %collective-permute-start.3 = (bf16[6,32,128]{2,1,0:T(8,128)(2,1)S(1)}, bf16[6,32,128]{2,1,0:T(8,128)(2,1)S(1)}, u32[]{:S(2)}, u32[]{:S(2)}) collective-permute-start(bf16[6,32,128]{2,1,0:T(8,128)(2,1)S(1)} %halo.1.after), channel_id=1, source_target_pairs={{0,128},{128,0},{1,129},{129,1},{2,130},{130,2},{3,131},{131,3},{4... | collective-permute-start | bytes 147464 | tf_op jit(solution)/shard_map/ppermute | solution.py:583
  29.2 12.1 %collective-permute-start.4 = (bf16[16,64,128]{2,1,0:T(8,128)(2,1)S(1)}, bf16[16,64,128]{2,1,0:T(8,128)(2,1)S(1)}, u32[]{:S(2)}, u32[]{:S(2)}) collective-permute-start(bf16[16,64,128]{2,1,0:T(8,128)(2,1)S(1)} %get-tuple-element.35), channel_id=1, source_target_pairs={{0,128},{128,0},{1,129},{129,1},{2,130},{130,2},{3,131},{131,3},{4... | collective-permute-start | bytes 786440 | tf_op jit(solution)/shard_map/ppermute | solution.py:586
  29.2 7.0 %collective-permute-start.5 = (bf16[288,128]{1,0:T(8,128)(2,1)S(1)}, bf16[288,128]{1,0:T(8,128)(2,1)S(1)}, u32[]{:S(2)}, u32[]{:S(2)}) collective-permute-start(bf16[288,128]{1,0:T(8,128)(2,1)S(1)} %get-tuple-element.38), channel_id=1, source_target_pairs={{0,1},{1,0},{2,3},{3,2},{4,5},{5,4},{6,7},{7,6},{8,9},{9,8},{10,11... | collective-permute-start | bytes 221192 | tf_op jit(solution)/shard_map/ppermute | solution.py:588
  29.5 8.7 %copy-start.1 = (bf16[128,128,3,3]{1,0,3,2:T(8,128)(2,1)S(1)}, bf16[128,128,3,3]{1,0,3,2:T(8,128)(2,1)}, u32[]{:S(2)}) copy-start(bf16[128,128,3,3]{1,0,3,2:T(8,128)(2,1)} %param.14) | copy-start | bytes 884740
  29.5 8.7 %copy-start.2 = (bf16[128,64,3,3]{0,1,3,2:T(8,128)(2,1)S(1)}, bf16[128,64,3,3]{0,1,3,2:T(8,128)(2,1)}, u32[]{:S(2)}) copy-start(bf16[128,64,3,3]{0,1,3,2:T(8,128)(2,1)} %param.12) | copy-start | bytes 442372
  29.5 8.7 %copy-start.5 = (f32[128]{0:T(128)S(1)}, f32[128]{0:T(128)}, u32[]{:S(2)}) copy-start(f32[128]{0:T(128)} %param.13) | copy-start | bytes 1540
  29.5 8.7 %copy-start.6 = (f32[128]{0:T(128)S(1)}, f32[128]{0:T(128)}, u32[]{:S(2)}) copy-start(f32[128]{0:T(128)} %param.15) | copy-start | bytes 1540
  29.5 6.7 %collective-permute-start.6 = (bf16[288,128]{1,0:T(8,128)(2,1)S(1)}, bf16[288,128]{1,0:T(8,128)(2,1)S(1)}, u32[]{:S(2)}, u32[]{:S(2)}) collective-permute-start(bf16[288,128]{1,0:T(8,128)(2,1)S(1)} %get-tuple-element.39), channel_id=1, source_target_pairs={{1,2},{2,1},{3,4},{4,3},{5,6},{6,5},{9,10},{10,9},{11,12},{12,11},... | collective-permute-start | bytes 221192 | tf_op jit(solution)/shard_map/ppermute | solution.py:587
  34.4 4.7 %collective-permute-start.7 = (bf16[4,64,128]{2,1,0:T(8,128)(2,1)S(1)}, bf16[4,64,128]{2,1,0:T(8,128)(2,1)S(1)}, u32[]{:S(2)}, u32[]{:S(2)}) collective-permute-start(bf16[4,64,128]{2,1,0:T(8,128)(2,1)S(1)} %get-tuple-element.41), channel_id=1, source_target_pairs={{0,128},{128,0},{1,129},{129,1},{2,130},{130,2},{3,131},{131,3},{4... | collective-permute-start | bytes 196616 | tf_op jit(solution)/shard_map/ppermute | solution.py:590
  37.3 4.0 %collective-permute-start.8 = (bf16[2,64,128]{2,1,0:T(8,128)(2,1)S(1)}, bf16[2,64,128]{2,1,0:T(8,128)(2,1)S(1)}, u32[]{:S(2)}, u32[]{:S(2)}) collective-permute-start(bf16[2,64,128]{2,1,0:T(8,128)(2,1)S(1)} %get-tuple-element.42), channel_id=1, source_target_pairs={{0,128},{128,0},{1,129},{129,1},{2,130},{130,2},{3,131},{131,3},{4... | collective-permute-start | bytes 98312 | tf_op jit(solution)/shard_map/ppermute | solution.py:593

commit v5 on v4

--- a/solution.py
+++ b/solution.py
@@ -309,15 +309,21 @@
         outer, e_rows, o_rows, corner, out, far, edge, w = refs
         quads = 3
     else:
-        out, mid, w = refs
+        out, mid, ws, c0, fws, w = refs
         quads = 4
     t = lax.axis_index("tm")
     start = 16 * t if own else 12 * (1 - t)
     bias = column(b0)
     wide_bias = jnp.concatenate([bias, bias], axis=0)
-    fill_w({key: jnp.where(t == 1, pltpu.roll(value, 96, 1), value) for key, value in taps(kt).items()}, w)
+    base = taps(kt)
+    fill_w({key: jnp.where(t == 1, pltpu.roll(value, 96, 1), value) for key, value in base.items()}, w)
     own_at = pl.ds(pl.multiple_of(192 - 160 * t, 32), 96)
     scale = scales_of(fw)
+    if not own:
+        c0[...] = bias
+        fws[...] = scale
+        for (d, b, fo), value in base.items():
+            ws[fo * 64 : fo * 64 + 64, (b * 3 + d) * 128 : (b * 3 + d) * 128 + 128] = value.astype(BF)
     scale = jnp.where(t == 0, scale[6:8], scale[0:2])
     scales = [scale[fo : fo + 1] for fo in range(2)]
 
@@ -359,6 +365,7 @@
         scratch = [pltpu.VMEM((2, 6, 128, 128), BF)] + scratch
     else:
         out_shape = [struct((16, 64, 128)), struct((4, 64, 128), F32)]
+        out_shape += [struct((128, 1152)), struct((64, 128), F32), struct((8, 128), F32)]
     return pl.pallas_call(
         functools.partial(rest_kernel, own),
         in_specs=[VMEM] * len(args),
@@ -371,14 +378,12 @@
     )(*args)
 
 
-def strip_temporal_kernel(own_l, own_r, e_col, o_col, kt, b0, fw, out, send, windows, ws):
+def strip_temporal_kernel(own_l, own_r, e_col, o_col, ws, c0, fws, out, send, windows):
     t = lax.axis_index("tm")
     even = lax.axis_index("col") % 2 == 0
     lane = lanes_of((16, 128))
     third = lane % 3
-    bias = column(b0)
-    for (d, b, fo), value in taps(kt).items():
-        ws[fo * 64 : fo * 64 + 64, (b * 3 + d) * 128 : (b * 3 + d) * 128 + 128] = value.astype(BF)
+    bias = c0[...]
 
     windows[:, pl.ds(pl.multiple_of(288 * t, 32), 32), :] = jnp.zeros((9, 32, 256), BF)
 
@@ -387,23 +392,20 @@
         dst = pl.ds(at if isinstance(at, int) else pl.multiple_of(at, 16), 16)
         ol, orr, ne, no = own_l[src, :], own_r[src, :], e_col[src, :], o_col[src, :]
         nl, nr = jnp.where(even, no, ne), jnp.where(even, ne, no)
-        for b in range(3):
-            for d in range(3):
-                lo = pltpu.roll(nl, (128 - (3 * b + d)) % 128, 1)
-                if d > 0:
-                    lo = jnp.where(third < 3 - d, lo, pltpu.roll(ol, (128 - (3 * b + d - 3)) % 128, 1))
-                hi = pltpu.roll(nr, (128 - (3 * b + d - 2)) % 128, 1)
-                if d < 2:
-                    hi = jnp.where(third < 2 - d, pltpu.roll(orr, 128 - (3 * b + d + 1), 1), hi)
-                windows[b * 3 + d, dst, 0:128] = lo
-                windows[b * 3 + d, dst, 128:256] = hi
+        ol, nr = pltpu.roll(ol, 3, 1), pltpu.roll(nr, 3, 1)
+        for d in range(3):
+            lo = nl if d == 0 else jnp.where(third >= d, nl, ol)
+            hi = nr if d == 2 else jnp.where(third >= d + 1, orr, nr)
+            for b in range(3):
+                turn = 3 * b + d
+                windows[b * 3 + d, dst, 0:128] = pltpu.roll(lo, (128 - turn) % 128, 1)
+                windows[b * 3 + d, dst, 128:256] = pltpu.roll(hi, 127 - turn, 1)
 
     for s in range(18):
         fill(s, 32 + 16 * s if s < 16 else 288 * (1 - t) + (s - 16) * 16)
 
     wide_bias = jnp.concatenate([bias, bias], axis=1)
-    both = scales_of(fw)
-    both = jnp.concatenate([both, both], axis=1)
+    both = jnp.concatenate([fws[...], fws[...]], axis=1)
     scale = [both[k : k + 1] for k in range(8)]
     acc = jnp.zeros((64, 256), F32)
     for g in range(4):
@@ -416,7 +418,8 @@
         send[side] = acc[:, side * 128 : side * 128 + 128].astype(BF)
 
 
-def spatial_weights_kernel(k1, b1, k2, b2, after, w1, w2, c1, c2):
+def spatial_weights_kernel(k1, b1, k2, b2, after, w1, w2, c1, c2, perm):
+    perm[...] = swap16()
     w1[...] = k1[...].reshape(576, 128).astype(F32).T.astype(BF)
     for k in range(9):
         w2[:, k * 128 : k * 128 + 128] = k2[k // 3, k % 3]
@@ -428,8 +431,14 @@
     return pl.pallas_call(
         spatial_weights_kernel,
         in_specs=[VMEM] * 4 + [ANY],
-        out_specs=[VMEM] * 4,
-        out_shape=[struct((128, 576)), struct((128, 1152)), struct((128, 128), F32), struct((128, 128), F32)],
+        out_specs=[VMEM] * 5,
+        out_shape=[
+            struct((128, 576)),
+            struct((128, 1152)),
+            struct((128, 128), F32),
+            struct((128, 128), F32),
+            struct((256, 256)),
+        ],
         compiler_params=params(),
         cost_estimate=cost(1e3, 1e3),
         name="spatial_weights",
@@ -442,14 +451,14 @@
         in_specs=[VMEM] * 7,
         out_specs=[VMEM] * 2,
         out_shape=[struct((2, 64, 128), F32), struct((2, 64, 128))],
-        scratch_shapes=[pltpu.VMEM((9, 320, 256), BF), pltpu.VMEM((128, 1152), BF)],
+        scratch_shapes=[pltpu.VMEM((9, 320, 256), BF)],
         compiler_params=params(),
         cost_estimate=cost(1e6, 1e6),
         name="strip_temporal",
     )(*args)
 
 
-def spatial_kernel(grid_rows, main, mid, partner, strips, partner_far, partner_strips, w1_ref, w2, c1, c2, out, own, theirs, c3, h3, ms):
+def spatial_kernel(grid_rows, main, mid, partner, strips, partner_far, partner_strips, w1_ref, w2, c1, c2, perm_ref, out, own, theirs, c3, h3, ms):
     t = lax.axis_index("tm")
     row = lax.axis_index("row")
     col = lax.axis_index("col")
@@ -477,16 +486,17 @@
         keep = in_grid(top + depth - 2) & jnp.logical_not(off)
         edges.append(jnp.where(keep, total, 0.0).astype(BF))
 
+    inner = jnp.where(third == 0, pltpu.roll(edges[0], 126, 1), pltpu.roll(edges[1], 127, 1))
+    outer = jnp.where(third == 0, pltpu.roll(edges[0], 127, 1), pltpu.roll(edges[1], 126, 1))
     for r in range(20):
+        turn = (128 - 3 * r) % 128
         value = (own[r] + theirs[r].astype(F32)).astype(BF)
-        value = jnp.where(lane == 0, pltpu.roll(edges[0], (126 - 3 * r) % 128, 1), value)
-        value = jnp.where(lane == 127, pltpu.roll(edges[1], 127 - 3 * r, 1), value)
+        value = jnp.where((lane == 0) | (lane == 127), pltpu.roll(inner, turn, 1), value)
         value = jnp.where(in_grid(top + r - 2), value, jnp.zeros_like(value))
-        c3[r, 0:64] = jnp.where(lane == 0, pltpu.roll(edges[0], 127 - 3 * r, 1), pltpu.roll(value, 1, 1))
+        beyond = pltpu.roll(outer, turn, 1)
+        c3[r, 0:64] = jnp.where(lane == 0, beyond, pltpu.roll(value, 1, 1))
         c3[r, 64:128] = value
-        c3[r, 128:192] = jnp.where(
-            lane == 127, pltpu.roll(edges[1], 126 - 3 * r, 1), pltpu.roll(value, 127, 1)
-        )
+        c3[r, 128:192] = jnp.where(lane == 127, beyond, pltpu.roll(value, 127, 1))
 
     bias1, bias2 = c1[...], c2[...]
     wide_b1 = jnp.concatenate([bias1, bias1], axis=1)
@@ -505,6 +515,7 @@
     kept = in_grid(top + lane2 // 3 - 1)
     hs_l = jnp.where(kept & jnp.logical_not(first_col), y[:, :128], 0.0).astype(BF)
     hs_r = jnp.where(kept & jnp.logical_not(last_col), y[:, 128:], 0.0).astype(BF)
+    sides = jnp.where(lane2 % 3 == 0, hs_l, pltpu.roll(hs_r, 127, 1))
 
     for h in range(0, 18, 2):
         rhs = jnp.concatenate(
@@ -514,13 +525,10 @@
         for at in range(h, h + 2):
             value = y[:, (at - h) * 128 : (at - h) * 128 + 128].astype(BF)
             value = jnp.where(in_grid(top + at - 1), value, jnp.zeros_like(value))
-            h3[at, 0:128] = jnp.where(
-                lane2 == 0, pltpu.roll(hs_l, (128 - 3 * at) % 128, 1), pltpu.roll(value, 1, 1)
-            )
+            beyond = pltpu.roll(sides, (128 - 3 * at) % 128, 1)
+            h3[at, 0:128] = jnp.where(lane2 == 0, beyond, pltpu.roll(value, 1, 1))
             h3[at, 128:256] = value
-            h3[at, 256:384] = jnp.where(
-                lane2 == 127, pltpu.roll(hs_r, 127 - 3 * at, 1), pltpu.roll(value, 127, 1)
-            )
+            h3[at, 256:384] = jnp.where(lane2 == 127, beyond, pltpu.roll(value, 127, 1))
 
     for r in range(0, 16, 2):
         rhs = jnp.concatenate(
@@ -530,7 +538,7 @@
         ms[r] = y[:, :128]
         ms[r + 1] = y[:, 128:]
 
-    perm = swap16()
+    perm = perm_ref[...]
     for pair in range(4):
         halves = [ms[:, (2 * pair + k) * 16 : (2 * pair + k) * 16 + 16, :].reshape(256, 128) for k in range(2)]
         y = dot(perm, jnp.concatenate(halves, axis=1)).astype(BF)
@@ -542,7 +550,7 @@
 def spatial(grid_rows, *args):
     return pl.pallas_call(
         functools.partial(spatial_kernel, grid_rows),
-        in_specs=[VMEM] * 10,
+        in_specs=[VMEM] * 11,
         out_specs=VMEM,
         out_shape=struct((128, 16, 128)),
         scratch_shapes=[
@@ -577,7 +585,7 @@
     slab = lax.ppermute(slab_of(xt), "tm", both)
     inner, left0, right0 = interior(xt, kt, b0, fw)
     field = (xt, inner, slab, kt, b0, fw)
-    for_partner, mid = rest(False, *field)
+    for_partner, mid, ws, c0, fws = rest(False, *field)
     corner = halo(e_rows, o_rows, mid)
     outer = edge_quads(xt, e_rows, o_rows, corner, kt, b0, fw)
     corner = lax.ppermute(corner, "tm", both)
@@ -588,10 +596,10 @@
     e_col = lax.ppermute(e_col, "col", swaps(cols, 0))
     main, far = rest(True, *field, outer, e_rows, o_rows, corner)
     far = lax.ppermute(far, "tm", both)
-    strips, strips_send = strip_temporal(left, right, e_col, o_col, kt, b0, fw)
-    w1, w2, c1, c2 = spatial_weights(k1, b1, k2, b2, strips)
+    strips, strips_send = strip_temporal(left, right, e_col, o_col, ws, c0, fws)
+    laid_out = spatial_weights(k1, b1, k2, b2, strips)
     strips_recv = lax.ppermute(strips_send, "tm", both)
-    return spatial(rows * 32, main, mid, partner, strips, far, strips_recv, w1, w2, c1, c2)
+    return spatial(rows * 32, main, mid, partner, strips, far, strips_recv, *laid_out)
 
 
 def solution(mesh):

time: 44.7 us -> 44.5 us (level)
  no operation moved by 1% of the time
where the time goes in v5:
time: 44.5 us; the launch traced here: 44.3 us
  Pallas kernels  18.7 us (42%)
  starting transfers between devices  17 us (38%)
  waiting for transfers between devices  6.85 us (15%)
  local copies, waits for them, and re-layouts  1.63 us (4%)
    pallas_call x1, Pallas kernels, interior(): pl.pallas_call(interior_kernel, in_specs=[VMEM] * 4, out_specs=[VMEM] * 3...  6.72 us
    ppermute x1, starting transfers between devices, shards(): o_rows = lax.ppermute(o_rows, 'row', swaps(rows, 1))  5.67 us
    pallas_call x2, Pallas kernels, rest(): pl.pallas_call(functools.partial(rest_kernel, own), in_specs=[VMEM] * len...  4.25 us
    ppermute x1, starting transfers between devices, shards(): e_rows = lax.ppermute(e_rows, 'row', swaps(rows, 0))  3.26 us
    pallas_call x1, Pallas kernels, spatial(): pl.pallas_call(functools.partial(spatial_kernel, grid_rows), in_specs=[VM...  3.22 us
    ppermute x1, starting transfers between devices, shards(): o_col = lax.ppermute(o_col, 'col', swaps(cols, 1))  2.93 us
    ppermute x1, waiting for transfers between devices, shards(): strips_recv = lax.ppermute(strips_send, 'tm', both)  2.21 us
    ppermute x1, waiting for transfers between devices, shards(): corner = lax.ppermute(corner, 'tm', both)  2.06 us
  transfers between devices with their start and end apart: 9, of which 4 were waited for; matrix products, arithmetic and copies ran while one was open for 0% of the time, Pallas kernels for 32%

profile of v5, /device:TPU:30, one launch (start us, length us, event | category | flops | bytes accessed | tf_op | source)
XLA Modules:
  0.0 44.3 jit_solution(6492023596347654415)
XLA Ops:
  0.0 1.6 %copy-done.7 = bf16[32,8,32,128]{3,2,1,0:T(8,128)(2,1)S(1)} copy-done((bf16[32,8,32,128]{3,2,1,0:T(8,128)(2,1)S(1)}, bf16[32,8,32,128]{3,2,1,0:T(8,128)(2,1)}, u32[]{:S(2)}) %copy-start.7) | copy-done | bytes 2097176
  1.6 0.8 %pack.1 = (bf16[32,320,128]{2,1,0:T(8,128)(2,1)S(1)}, bf16[3,256,128]{2,1,0:T(8,128)(2,1)S(1)}, bf16[3,256,128]{2,1,0:T(8,128)(2,1)S(1)}) custom-call(bf16[32,8,32,128]{3,2,1,0:T(8,128)(2,1)S(1)} %copy-done.7), custom_call_target="tpu_custom_call" | custom-call | flops 6000000000 | bytes 4600000 | tf_op jit(solution)/shard_map/pack/pallas_call | solution.py:62
  2.4 0.0 copy-start.3
  2.4 0.0 copy-start.4
  2.5 2.0 %collective-permute-start = (bf16[32,32,128]{2,1,0:T(8,128)(2,1)S(1)}, bf16[32,32,128]{2,1,0:T(8,128)(2,1)S(1)}, u32[]{:S(2)}, u32[]{:S(2)}) collective-permute-start(bf16[32,32,128]{2,1,0:T(8,128)(2,1)S(1)} %slab.1), channel_id=1, source_target_pairs={{0,128},{128,0},{1,129},{129,1},{2,130},{130,2},{3,131},{131,3},{4... | collective-permute-start | bytes 786440 | tf_op jit(solution)/shard_map/ppermute | solution.py:585
  4.5 3.3 %collective-permute-start.1 = (bf16[3,256,128]{2,1,0:T(8,128)(2,1)S(1)}, bf16[3,256,128]{2,1,0:T(8,128)(2,1)S(1)}, u32[]{:S(2)}, u32[]{:S(2)}) collective-permute-start(bf16[3,256,128]{2,1,0:T(8,128)(2,1)S(1)} %get-tuple-element.32), channel_id=1, source_target_pairs={{0,8},{8,0},{16,24},{24,16},{32,40},{40,32},{48,56},{56,48},{64,72... | collective-permute-start | bytes 589832 | tf_op jit(solution)/shard_map/ppermute | solution.py:583
  7.7 5.7 %collective-permute-start.2 = (bf16[3,256,128]{2,1,0:T(8,128)(2,1)S(1)}, bf16[3,256,128]{2,1,0:T(8,128)(2,1)S(1)}, u32[]{:S(2)}, u32[]{:S(2)}) collective-permute-start(bf16[3,256,128]{2,1,0:T(8,128)(2,1)S(1)} %get-tuple-element.33), channel_id=1, source_target_pairs={{8,16},{16,8},{24,32},{32,24},{40,48},{48,40},{56,64},{64,56},{72,... | collective-permute-start | bytes 589832 | tf_op jit(solution)/shard_map/ppermute | solution.py:584
  13.4 6.7 %interior.1 = (f32[28,64,128]{2,1,0:T(8,128)S(1)}, bf16[256,128]{1,0:T(8,128)(2,1)S(1)}, bf16[256,128]{1,0:T(8,128)(2,1)S(1)}) custom-call(bf16[32,320,128]{2,1,0:T(8,128)(2,1)S(1)} %get-tuple-element.30.xt, bf16[3,3,3,32,64]{4,3,2,1,0:T(8,128)(2,1)S(1)} %bitcast.7, f32[1,64]{1,0:T(1,128)S(1)} %bitcast.13, f32[1,16]{1,0:T(1,128)S(1)} %bitcast.17), custom_call_target="tpu_custom_call" | custom-call | flops 1000 | bytes 1000 | tf_op jit(solution)/shard_map/interior/pallas_call | solution.py:259
  20.2 2.4 %rest_partner.1 = (bf16[16,64,128]{2,1,0:T(8,128)(2,1)S(1)}, f32[4,64,128]{2,1,0:T(8,128)S(1)}, bf16[128,1152]{1,0:T(8,128)(2,1)S(1)}, f32[64,128]{1,0:T(8,128)S(1)}, f32[8,128]{1,0:T(8,128)S(1)}) custom-call(bf16[32,320,128]{2,1,0:T(8,128)(2,1)S(1)} %get-tuple-element.30.xt, f32[28,64,128]{2,1,0:T(8,128)S(1)} %get-tuple-element.31.inner, ...), custom_call_target="tpu_custom_call" | custom-call | flops 1000000 | bytes 1000000 | tf_op jit(solution)/shard_map/rest_partner/pallas_call | solution.py:369
  22.6 1.9 %collective-permute-done.2.o_rows.refs_2_ = bf16[3,256,128]{2,1,0:T(8,128)(2,1)S(1)} collective-permute-done((bf16[3,256,128]{2,1,0:T(8,128)(2,1)S(1)}, bf16[3,256,128]{2,1,0:T(8,128)(2,1)S(1)}, u32[]{:S(2)}, u32[]{:S(2)}) %collective-permute-start.2) | collective-permute-done | bytes 196640 | tf_op jit(solution)/shard_map/ppermute | solution.py:584
  24.5 2.0 %edge_quads.1.refs_0_.after = f32[8,64,128]{2,1,0:T(8,128)S(1)} custom-call(bf16[32,320,128]{2,1,0:T(8,128)(2,1)S(1)} %get-tuple-element.30.xt, bf16[3,256,128]{2,1,0:T(8,128)(2,1)S(1)} %collective-permute-done.1.e_rows.refs_1_, bf16[3,256,128]{2,1,0:T(8,128)(2,1)S(1)} %collective-permute-done.2.o_rows.refs_2_, bf16[6,32,128]{2,1,0:T(8,128)(2,1)S(1)} %halo.1.after, ...), custom_call_target="tpu_custom_call" | custom-call | flops 1207959552 | bytes 2000000 | tf_op jit(solution)/shard_map/edge_quads/pallas_call | solution.py:295
  26.5 2.1 %collective-permute-done.3.refs_3_.corner = bf16[6,32,128]{2,1,0:T(8,128)(2,1)S(1)} collective-permute-done((bf16[6,32,128]{2,1,0:T(8,128)(2,1)S(1)}, bf16[6,32,128]{2,1,0:T(8,128)(2,1)S(1)}, u32[]{:S(2)}, u32[]{:S(2)}) %collective-permute-start.3) | collective-permute-done | bytes 49184 | tf_op jit(solution)/shard_map/ppermute | solution.py:591
  28.6 0.6 %strip_pack.1 = (bf16[288,128]{1,0:T(8,128)(2,1)S(1)}, bf16[288,128]{1,0:T(8,128)(2,1)S(1)}, bf16[288,128]{1,0:T(8,128)(2,1)S(1)}, bf16[288,128]{1,0:T(8,128)(2,1)S(1)}, bf16[16,64,128]{2,1,0:T(8,128)(2,1)S(1)}) custom-call(bf16[256,128]{1,0:T(8,128)(2,1)S(1)} %get-tuple-element.36.left0, bf16[256,128]{1,0:T(8,128)(2,1)S(1)} %get-tuple-element.37.right0, ...), custom_call_target="tpu_custom_call" | custom-call | flops 100000000 | bytes 1000000 | tf_op jit(solution)/shard_map/strip_pack/pallas_call | solution.py:185
  29.2 0.0 collective-permute-start.4
  29.2 0.3 collective-permute-start.5
  29.5 2.9 %collective-permute-start.6 = (bf16[288,128]{1,0:T(8,128)(2,1)S(1)}, bf16[288,128]{1,0:T(8,128)(2,1)S(1)}, u32[]{:S(2)}, u32[]{:S(2)}) collective-permute-start(bf16[288,128]{1,0:T(8,128)(2,1)S(1)} %get-tuple-element.43), channel_id=1, source_target_pairs={{1,2},{2,1},{3,4},{4,3},{5,6},{6,5},{9,10},{10,9},{11,12},{12,11},... | collective-permute-start | bytes 221192 | tf_op jit(solution)/shard_map/ppermute | solution.py:595
  32.5 1.9 %rest_own.1 = (f32[16,64,128]{2,1,0:T(8,128)S(1)}, bf16[4,64,128]{2,1,0:T(8,128)(2,1)S(1)}) custom-call(bf16[32,320,128]{2,1,0:T(8,128)(2,1)S(1)} %get-tuple-element.30.xt, f32[28,64,128]{2,1,0:T(8,128)S(1)} %get-tuple-element.31.inner, bf16[32,32,128]{2,1,0:T(8,128)(2,1)S(1)} %collective-permute-done.slab, bf16[3,3,3,32,64]{4,3,2,1,0:T(8,128)(2,1)S(1)} %bitcast.10, ...), custom_call_target="tpu_custom_call" | custom-call | flops 1000000 | bytes 1000000 | tf_op jit(solution)/shard_map/rest_own/pallas_call | solution.py:369
  34.4 1.8 %collective-permute-start.7 = (bf16[4,64,128]{2,1,0:T(8,128)(2,1)S(1)}, bf16[4,64,128]{2,1,0:T(8,128)(2,1)S(1)}, u32[]{:S(2)}, u32[]{:S(2)}) collective-permute-start(bf16[4,64,128]{2,1,0:T(8,128)(2,1)S(1)} %get-tuple-element.48), channel_id=1, source_target_pairs={{0,128},{128,0},{1,129},{129,1},{2,130},{130,2},{3,131},{131,3},{4... | collective-permute-start | bytes 196616 | tf_op jit(solution)/shard_map/ppermute | solution.py:598
  36.2 0.9 %strip_temporal.1 = (f32[2,64,128]{2,1,0:T(8,128)S(1)}, bf16[2,64,128]{2,1,0:T(8,128)(2,1)S(1)}) custom-call(bf16[288,128]{1,0:T(8,128)(2,1)S(1)} %get-tuple-element.40.own_l, bf16[288,128]{1,0:T(8,128)(2,1)S(1)} %get-tuple-element.41.own_r, bf16[288,128]{1,0:T(8,128)(2,1)S(1)} %collective-permute-done.5.e_col, ...), custom_call_target="tpu_custom_call" | custom-call | flops 1000000 | bytes 1000000 | tf_op jit(solution)/shard_map/strip_temporal/pallas_call | solution.py:449
  37.1 0.9 %collective-permute-start.8 = (bf16[2,64,128]{2,1,0:T(8,128)(2,1)S(1)}, bf16[2,64,128]{2,1,0:T(8,128)(2,1)S(1)}, u32[]{:S(2)}, u32[]{:S(2)}) collective-permute-start(bf16[2,64,128]{2,1,0:T(8,128)(2,1)S(1)} %get-tuple-element.49), channel_id=1, source_target_pairs={{0,128},{128,0},{1,129},{129,1},{2,130},{130,2},{3,131},{131,3},{4... | collective-permute-start | bytes 98312 | tf_op jit(solution)/shard_map/ppermute | solution.py:601
  38.1 0.2 spatial_weights.1
  38.3 0.6 %collective-permute-done.7.partner_far = bf16[4,64,128]{2,1,0:T(8,128)(2,1)S(1)} collective-permute-done((bf16[4,64,128]{2,1,0:T(8,128)(2,1)S(1)}, bf16[4,64,128]{2,1,0:T(8,128)(2,1)S(1)}, u32[]{:S(2)}, u32[]{:S(2)}) %collective-permute-start.7) | collective-permute-done | bytes 65568 | tf_op jit(solution)/shard_map/ppermute | solution.py:598
  38.9 2.2 %collective-permute-done.8.partner_strips = bf16[2,64,128]{2,1,0:T(8,128)(2,1)S(1)} collective-permute-done((bf16[2,64,128]{2,1,0:T(8,128)(2,1)S(1)}, bf16[2,64,128]{2,1,0:T(8,128)(2,1)S(1)}, u32[]{:S(2)}, u32[]{:S(2)}) %collective-permute-start.8) | collective-permute-done | bytes 32800 | tf_op jit(solution)/shard_map/ppermute | solution.py:601
  41.1 3.2 %spatial.1 = bf16[128,16,128]{2,1,0:T(8,128)(2,1)} custom-call(f32[16,64,128]{2,1,0:T(8,128)S(1)} %get-tuple-element.35.main, f32[4,64,128]{2,1,0:T(8,128)S(1)} %get-tuple-element.34.after.mid, bf16[16,64,128]{2,1,0:T(8,128)(2,1)S(1)} %collective-permute-done.4.partner, f32[2,64,128]{2,1,0:T(8,128)S(1)} %get-tuple-element.47.after.strips, ...), custom_call_target="tpu_custom_call" | custom-call | flops 1200000000 | bytes 3000000 | tf_op jit(solution)/shard_map/spatial/pallas_call | solution.py:551
  (21 shorter events, 0.1 us)
Async XLA Ops:
  0.0 1.6 %copy-start.7 = (bf16[32,8,32,128]{3,2,1,0:T(8,128)(2,1)S(1)}, bf16[32,8,32,128]{3,2,1,0:T(8,128)(2,1)}, u32[]{:S(2)}) copy-start(bf16[32,8,32,128]{3,2,1,0:T(8,128)(2,1)} %x.1) | copy-start | bytes 6291460
  2.4 11.0 %copy-start = (bf16[64,32,3,3,3]{0,1,4,3,2:T(8,128)(2,1)S(1)}, bf16[64,32,3,3,3]{0,1,4,3,2:T(8,128)(2,1)}, u32[]{:S(2)}) copy-start(bf16[64,32,3,3,3]{0,1,4,3,2:T(8,128)(2,1)} %param.9) | copy-start | bytes 331780
  2.4 11.0 %copy-start.3 = (f32[64]{0:T(128)S(1)}, f32[64]{0:T(128)}, u32[]{:S(2)}) copy-start(f32[64]{0:T(128)} %param.10) | copy-start | bytes 772
  2.4 11.0 %copy-start.4 = (f32[16]{0:T(128)S(1)}, f32[16]{0:T(128)}, u32[]{:S(2)}) copy-start(f32[16]{0:T(128)} %param.11) | copy-start | bytes 196
  2.5 17.7 %collective-permute-start = (bf16[32,32,128]{2,1,0:T(8,128)(2,1)S(1)}, bf16[32,32,128]{2,1,0:T(8,128)(2,1)S(1)}, u32[]{:S(2)}, u32[]{:S(2)}) collective-permute-start(bf16[32,32,128]{2,1,0:T(8,128)(2,1)S(1)} %slab.1), channel_id=1, source_target_pairs={{0,128},{128,0},{1,129},{129,1},{2,130},{130,2},{3,131},{131,3},{4... | collective-permute-start | bytes 786440 | tf_op jit(solution)/shard_map/ppermute | solution.py:585
  4.5 18.1 %collective-permute-start.1 = (bf16[3,256,128]{2,1,0:T(8,128)(2,1)S(1)}, bf16[3,256,128]{2,1,0:T(8,128)(2,1)S(1)}, u32[]{:S(2)}, u32[]{:S(2)}) collective-permute-start(bf16[3,256,128]{2,1,0:T(8,128)(2,1)S(1)} %get-tuple-element.32), channel_id=1, source_target_pairs={{0,8},{8,0},{16,24},{24,16},{32,40},{40,32},{48,56},{56,48},{64,72... | collective-permute-start | bytes 589832 | tf_op jit(solution)/shard_map/ppermute | solution.py:583
  7.7 16.8 %collective-permute-start.2 = (bf16[3,256,128]{2,1,0:T(8,128)(2,1)S(1)}, bf16[3,256,128]{2,1,0:T(8,128)(2,1)S(1)}, u32[]{:S(2)}, u32[]{:S(2)}) collective-permute-start(bf16[3,256,128]{2,1,0:T(8,128)(2,1)S(1)} %get-tuple-element.33), channel_id=1, source_target_pairs={{8,16},{16,8},{24,32},{32,24},{40,48},{48,40},{56,64},{64,56},{72,... | collective-permute-start | bytes 589832 | tf_op jit(solution)/shard_map/ppermute | solution.py:584
  24.5 4.1 %collective-permute-start.3 = (bf16[6,32,128]{2,1,0:T(8,128)(2,1)S(1)}, bf16[6,32,128]{2,1,0:T(8,128)(2,1)S(1)}, u32[]{:S(2)}, u32[]{:S(2)}) collective-permute-start(bf16[6,32,128]{2,1,0:T(8,128)(2,1)S(1)} %halo.1.after), channel_id=1, source_target_pairs={{0,128},{128,0},{1,129},{129,1},{2,130},{130,2},{3,131},{131,3},{4... | collective-permute-start | bytes 147464 | tf_op jit(solution)/shard_map/ppermute | solution.py:591
  29.2 11.9 %collective-permute-start.4 = (bf16[16,64,128]{2,1,0:T(8,128)(2,1)S(1)}, bf16[16,64,128]{2,1,0:T(8,128)(2,1)S(1)}, u32[]{:S(2)}, u32[]{:S(2)}) collective-permute-start(bf16[16,64,128]{2,1,0:T(8,128)(2,1)S(1)} %get-tuple-element.39), channel_id=1, source_target_pairs={{0,128},{128,0},{1,129},{129,1},{2,130},{130,2},{3,131},{131,3},{4... | collective-permute-start | bytes 786440 | tf_op jit(solution)/shard_map/ppermute | solution.py:594
  29.2 7.0 %collective-permute-start.5 = (bf16[288,128]{1,0:T(8,128)(2,1)S(1)}, bf16[288,128]{1,0:T(8,128)(2,1)S(1)}, u32[]{:S(2)}, u32[]{:S(2)}) collective-permute-start(bf16[288,128]{1,0:T(8,128)(2,1)S(1)} %get-tuple-element.42), channel_id=1, source_target_pairs={{0,1},{1,0},{2,3},{3,2},{4,5},{5,4},{6,7},{7,6},{8,9},{9,8},{10,11... | collective-permute-start | bytes 221192 | tf_op jit(solution)/shard_map/ppermute | solution.py:596
  29.5 8.6 %copy-start.1 = (bf16[128,128,3,3]{1,0,3,2:T(8,128)(2,1)S(1)}, bf16[128,128,3,3]{1,0,3,2:T(8,128)(2,1)}, u32[]{:S(2)}) copy-start(bf16[128,128,3,3]{1,0,3,2:T(8,128)(2,1)} %param.14) | copy-start | bytes 884740
  29.5 8.6 %copy-start.2 = (bf16[128,64,3,3]{0,1,3,2:T(8,128)(2,1)S(1)}, bf16[128,64,3,3]{0,1,3,2:T(8,128)(2,1)}, u32[]{:S(2)}) copy-start(bf16[128,64,3,3]{0,1,3,2:T(8,128)(2,1)} %param.12) | copy-start | bytes 442372
  29.5 8.5 %copy-start.5 = (f32[128]{0:T(128)S(1)}, f32[128]{0:T(128)}, u32[]{:S(2)}) copy-start(f32[128]{0:T(128)} %param.13) | copy-start | bytes 1540
  29.5 8.5 %copy-start.6 = (f32[128]{0:T(128)S(1)}, f32[128]{0:T(128)}, u32[]{:S(2)}) copy-start(f32[128]{0:T(128)} %param.15) | copy-start | bytes 1540
  29.5 6.7 %collective-permute-start.6 = (bf16[288,128]{1,0:T(8,128)(2,1)S(1)}, bf16[288,128]{1,0:T(8,128)(2,1)S(1)}, u32[]{:S(2)}, u32[]{:S(2)}) collective-permute-start(bf16[288,128]{1,0:T(8,128)(2,1)S(1)} %get-tuple-element.43), channel_id=1, source_target_pairs={{1,2},{2,1},{3,4},{4,3},{5,6},{6,5},{9,10},{10,9},{11,12},{12,11},... | collective-permute-start | bytes 221192 | tf_op jit(solution)/shard_map/ppermute | solution.py:595
  34.4 4.5 %collective-permute-start.7 = (bf16[4,64,128]{2,1,0:T(8,128)(2,1)S(1)}, bf16[4,64,128]{2,1,0:T(8,128)(2,1)S(1)}, u32[]{:S(2)}, u32[]{:S(2)}) collective-permute-start(bf16[4,64,128]{2,1,0:T(8,128)(2,1)S(1)} %get-tuple-element.48), channel_id=1, source_target_pairs={{0,128},{128,0},{1,129},{129,1},{2,130},{130,2},{3,131},{131,3},{4... | collective-permute-start | bytes 196616 | tf_op jit(solution)/shard_map/ppermute | solution.py:598
  37.1 4.0 %collective-permute-start.8 = (bf16[2,64,128]{2,1,0:T(8,128)(2,1)S(1)}, bf16[2,64,128]{2,1,0:T(8,128)(2,1)S(1)}, u32[]{:S(2)}, u32[]{:S(2)}) collective-permute-start(bf16[2,64,128]{2,1,0:T(8,128)(2,1)S(1)} %get-tuple-element.49), channel_id=1, source_target_pairs={{0,128},{128,0},{1,129},{129,1},{2,130},{130,2},{3,131},{131,3},{4... | collective-permute-start | bytes 98312 | tf_op jit(solution)/shard_map/ppermute | solution.py:601
